TPU v7x, 256 devices: a whole 4x4x8 slice. The times are simulated.
256 devices in a mesh: seg: 8 (over y, core), coil: 16 (over x, z_lo), tile: 2 (over z_hi).
Axes of the slice: x: 4, y: 4, z: 8 (z_hi: 2, z_lo: 4; z = z_hi * 4 + z_lo), core: 2. Of those that a mesh axis runs over, the one named last changes fastest.
Arguments:
- right_side: float32 [1024, 128], P(('seg', 'coil', 'tile')), may hold values from -6 to 6
- sensitivity: float32 [32, 1024, 128], P('coil'), may hold values from -0.75 to 0.75
- field_map: float32 [1024, 64], replicated, may hold values from -12 to 12
- seg_map: int32 [1024, 4], replicated, may hold values from 0 to 23, all different within a row; in each aligned block of 1024 rows (0 to 1023, 1024 to 2047, ...) at most 256 rows name the same one
- sample_rows: int32 [24, 2048], P('seg', 'tile'), may hold values from 0 to 1023
- density: float32 [24, 2048, 64], P('seg', 'tile'), may hold values from 0.25 to 4
- step_alpha: float32 [2], replicated, may hold values from 0.15 to 0.35
- step_beta: float32 [2], replicated, may hold values from 0.1 to 0.5
Outputs:
- solution_field: float32 [1024, 128], P(('seg', 'coil', 'tile'))
- residual: float32 [1024, 128], P(('seg', 'coil', 'tile'))
Inputs may be any that keep to these rules, and one draw needn't show every extreme that they name: `seg_map`: each row names 4 different segments; each segment is named by at most 256 tiles, a bound that some block reaches.
All inputs are finite; a program needn't handle non-finite values.
Results may differ from a plain program's by a relative error of at most 0.0001.
Values sent between devices are 32-bit elements; how exact they have to be, the bound alone decides.
No kernel may reach another device: no remote copies, remote signals or barrier semaphores. Data moves between devices by JAX's collectives and lax.ppermute only.
A program may use at most 128 MiB of HBM per device.

v0:
```python
import math

import jax
import jax.numpy as jnp
from jax import lax
from jax.sharding import PartitionSpec as P

SEGS = 24
TV = 64
ITERS = 2
CAP = 256


ridge_weight = 0.25
highest = lax.Precision.HIGHEST


def tile_list(seg_map, segment, slots):
    tile_count = seg_map.shape[0]
    is_member = jnp.any(seg_map == segment, axis=1).astype(jnp.int32)
    live_count = jnp.sum(is_member)
    sort_keys = (1 - is_member) * tile_count + jnp.arange(tile_count, dtype=jnp.int32)
    sorted_tiles = jnp.argsort(sort_keys)
    listed = sorted_tiles[:slots]
    valid_slots = (jnp.arange(slots, dtype=jnp.int32) < live_count).astype(jnp.float32)
    return (listed, valid_slots)


def row_tables(rows_here, listed, valid_slots, tile_count):
    product = rows_here[:, None] * listed[None, :] % tile_count
    angles = product.astype(jnp.float32) * jnp.float32(2.0 * math.pi / tile_count)
    slot_scale = valid_slots[None, :] / jnp.float32(math.sqrt(tile_count))
    return (jnp.cos(angles) * slot_scale, -jnp.sin(angles) * slot_scale)


def column_tables(voxels):
    steps_here = jnp.arange(voxels, dtype=jnp.int32)
    product = steps_here[:, None] * steps_here[None, :] % voxels
    angles = product.astype(jnp.float32) * jnp.float32(2.0 * math.pi / voxels)
    norm_factor = jnp.float32(1.0 / math.sqrt(voxels))
    return (jnp.cos(angles) * norm_factor, -jnp.sin(angles) * norm_factor)


def segment_normal(
    dir_rows, sens_rows, field_rows, seg_time, row_cos, row_sin, col_cos, col_sin, weights
):
    voxels = field_rows.shape[1]
    phase_angle = field_rows * seg_time
    phase_real = jnp.cos(phase_angle)
    phase_imag = -jnp.sin(phase_angle)
    dir_real = dir_rows[:, :voxels]
    dir_imag = dir_rows[:, voxels:]
    image_real = phase_real * dir_real - phase_imag * dir_imag
    image_imag = phase_real * dir_imag + phase_imag * dir_real
    sens_real = sens_rows[..., :voxels]
    sens_imag = sens_rows[..., voxels:]
    coil_real = sens_real * image_real - sens_imag * image_imag
    coil_imag = sens_real * image_imag + sens_imag * image_real
    grid_real = jnp.einsum("mn,cnv->cmv", row_cos, coil_real, precision=highest) - jnp.einsum(
        "mn,cnv->cmv", row_sin, coil_imag, precision=highest
    )
    grid_imag = jnp.einsum("mn,cnv->cmv", row_cos, coil_imag, precision=highest) + jnp.einsum(
        "mn,cnv->cmv", row_sin, coil_real, precision=highest
    )
    kspace_real = jnp.einsum("cmv,vj->cmj", grid_real, col_cos, precision=highest) - jnp.einsum(
        "cmv,vj->cmj", grid_imag, col_sin, precision=highest
    )
    kspace_imag = jnp.einsum("cmv,vj->cmj", grid_real, col_sin, precision=highest) + jnp.einsum(
        "cmv,vj->cmj", grid_imag, col_cos, precision=highest
    )
    kspace_real = kspace_real * weights[None]
    kspace_imag = kspace_imag * weights[None]
    back_real = jnp.einsum("cmj,jv->cmv", kspace_real, col_cos, precision=highest) + jnp.einsum(
        "cmj,jv->cmv", kspace_imag, col_sin, precision=highest
    )
    back_imag = jnp.einsum("cmj,jv->cmv", kspace_imag, col_cos, precision=highest) - jnp.einsum(
        "cmj,jv->cmv", kspace_real, col_sin, precision=highest
    )
    rows_real = jnp.einsum("mn,cmv->cnv", row_cos, back_real, precision=highest) + jnp.einsum(
        "mn,cmv->cnv", row_sin, back_imag, precision=highest
    )
    rows_imag = jnp.einsum("mn,cmv->cnv", row_cos, back_imag, precision=highest) - jnp.einsum(
        "mn,cmv->cnv", row_sin, back_real, precision=highest
    )
    summed_real = jnp.sum(sens_real * rows_real + sens_imag * rows_imag, axis=0)
    summed_imag = jnp.sum(sens_real * rows_imag - sens_imag * rows_real, axis=0)
    result_real = phase_real * summed_real + phase_imag * summed_imag
    result_imag = phase_real * summed_imag - phase_imag * summed_real
    return jnp.concatenate([result_real, result_imag], axis=1)


def gather_direction(own_tiles):
    return lax.all_gather(own_tiles, ("seg", "coil", "tile"), axis=0, tiled=True)


def shards(
    right_side, sensitivity, field_map, seg_map, sample_rows, density, step_alpha, step_beta
):
    seg_local = sample_rows.shape[0]
    tile_count = field_map.shape[0]
    first_segment = lax.axis_index("seg") * seg_local
    col_cos, col_sin = column_tables(TV)
    prepared = []
    for local_seg in range(seg_local):
        segment = first_segment + local_seg
        listed, valid_slots = tile_list(seg_map, segment, CAP)
        row_cos, row_sin = row_tables(sample_rows[local_seg], listed, valid_slots, tile_count)
        seg_time = (segment.astype(jnp.float32) + 0.5) / jnp.float32(SEGS)
        prepared.append(
            (
                listed,
                row_cos,
                row_sin,
                seg_time,
                sensitivity[:, listed],
                field_map[listed],
                density[local_seg],
            )
        )
    direction = right_side
    solution_field = jnp.zeros_like(right_side)
    residual = right_side
    for step in range(ITERS):
        gathered = gather_direction(direction)
        partial_value = jnp.zeros(gathered.shape, jnp.float32)
        for (
            local_listed,
            local_row_cos,
            local_row_sin,
            local_seg_time,
            sens_rows,
            field_rows,
            weights,
        ) in prepared:
            contrib = segment_normal(
                gathered[local_listed],
                sens_rows,
                field_rows,
                local_seg_time,
                local_row_cos,
                local_row_sin,
                col_cos,
                col_sin,
                weights,
            )
            partial_value = partial_value.at[local_listed].add(contrib)
        image = (
            lax.psum_scatter(
                partial_value, ("seg", "coil", "tile"), scatter_dimension=0, tiled=True
            )
            + ridge_weight * direction
        )
        solution_field = solution_field + step_alpha[step] * direction
        residual = residual - step_alpha[step] * image
        direction = residual + step_beta[step] * direction
    return (solution_field, residual)


def solution(mesh):
    placed = (
        P(("seg", "coil", "tile"), None),
        P("coil", None, None),
        P(),
        P(),
        P("seg", "tile"),
        P("seg", "tile", None),
        P(),
        P(),
    )
    return jax.shard_map(
        shards,
        mesh=mesh,
        in_specs=placed,
        out_specs=(P(("seg", "coil", "tile"), None), P(("seg", "coil", "tile"), None)),
        check_vma=False,
    )
```

profile of v0, /device:TPU:1, one launch (start us, length us, event | category | flops | bytes accessed | tf_op | source)
XLA Modules:
  0.0 2121.3 jit_solution(18167346693493669759)
XLA Ops:
  9.3 4.4 sort.47
  16.2 613.7 %all-gather = f32[256,4,128]{2,1,0:T(4,128)S(1)} all-gather(f32[1,4,128]{2,1,0:T(4,128)S(1)} %bitcast.389), channel_id=1, replica_groups=mesh['seg'=8,'coil'=16,'tile'=2] {'seg','coil','tile'}, dimensions={0}, use_global_device_ids=true | all-gather | bytes 526336 | tf_op jit(solution)/shard_map/all_gather | solution.py:93
  633.7 4.9 fusion.67
  638.6 6.3 fusion.65
  645.0 4.9 fusion.4
  651.4 4.4 sort.46
  657.8 1.7 gather_fusion.4
  660.4 1.7 copy.114
  667.0 6.5 fusion.89
  673.5 4.9 fusion.91
  678.5 4.9 fusion.2
  687.9 4.4 sort.45
  698.3 6.1 fusion.113
  704.4 4.9 fusion.115
  709.3 4.9 fusion
  717.5 5.3 fusion.5
  726.7 4.7 fusion.63
  732.1 4.5 fusion.61
  736.7 4.6 fusion.30
  741.3 4.8 subtract_reduce_fusion.3
  747.4 4.9 fusion.3
  756.8 4.5 fusion.87
  762.1 4.5 fusion.85
  766.6 4.8 fusion.32
  771.4 4.6 subtract_reduce_fusion.4
  777.3 6.7 fusion.1
  788.1 4.5 fusion.111
  793.4 4.9 fusion.109
  798.3 4.6 fusion.34
  803.0 4.6 subtract_reduce_fusion.5
  808.0 1.9 scatter_custom_fusion
  809.8 2.1 scatter_fusion
  812.0 2.1 scatter_fusion.1
  816.3 259.0 %all-reduce.5.cloned.1.call-done = f32[1024,128]{1,0:T(8,128)} async-done(((f32[1024,128]{1,0:T(8,128)}), f32[1024,128]{1,0:T(8,128)}) %all-reduce.5.cloned.1.call-update) | async-done | bytes 524304
  1077.4 609.9 %all-gather.1 = f32[256,4,128]{2,1,0:T(4,128)S(1)} all-gather(f32[1,4,128]{2,1,0:T(4,128)S(1)} %fusion.641), channel_id=1, replica_groups=mesh['seg'=8,'coil'=16,'tile'=2] {'seg','coil','tile'}, dimensions={0}, use_global_device_ids=true | all-gather | bytes 526336 | tf_op jit(solution)/shard_map/all_gather | solution.py:93
  1689.2 6.4 fusion.57
  1695.6 4.9 fusion.59
  1700.5 4.9 fusion.10
  1710.4 6.2 fusion.81
  1716.5 4.9 fusion.83
  1721.4 4.9 fusion.8
  1731.5 6.2 fusion.105
  1737.6 4.9 fusion.107
  1742.5 4.9 fusion.6
  1749.3 5.3 fusion.11
  1758.8 4.7 fusion.55
  1764.2 4.5 fusion.53
  1768.8 4.6 fusion.24
  1773.4 5.6 subtract_reduce_fusion
  1780.2 6.5 fusion.9
  1790.8 4.5 fusion.79
  1796.1 4.7 fusion.77
  1800.8 4.6 fusion.26
  1805.4 4.6 subtract_reduce_fusion.1
  1811.3 6.9 fusion.7
  1821.9 4.5 fusion.103
  1827.2 4.7 fusion.101
  1831.9 4.6 fusion.28
  1836.5 4.6 subtract_reduce_fusion.2
  1841.6 1.9 scatter_custom_fusion.3
  1843.5 2.1 scatter_fusion.2
  1845.6 2.1 scatter_fusion.3
  1848.6 262.4 %all-reduce.7.cloned.1.call-done = f32[1024,128]{1,0:T(8,128)} async-done(((f32[1024,128]{1,0:T(8,128)}), f32[1024,128]{1,0:T(8,128)}) %all-reduce.7.cloned.1.call-update) | async-done | bytes 524304
  2111.7 2.6 fusion.206
  (310 shorter events, 84.2 us)
Async XLA Ops:
  7.2 623.8 %copy-start = (f32[2,1024,128]{2,1,0:T(8,128)S(1)}, f32[2,1024,128]{2,1,0:T(8,128)}, u32[]{:S(2)}) copy-start(f32[2,1024,128]{2,1,0:T(8,128)} %param.9) | copy-start | bytes 3145732
  7.2 1068.2 %all-reduce.5.cloned.1.call-start = ((), (), s32[]{:S(2)}) async-start(), calls=%async_computation | async-start | bytes 1048576
  13.7 631.3 %copy-start.67 = (s32[256]{0:T(256)}, s32[256]{0:T(256)S(1)}, u32[]{:S(2)}) copy-start(s32[256]{0:T(256)S(1)} %get-tuple-element.67) | copy-start | bytes 3076
  632.1 12.8 copy-start.17
  632.8 12.1 copy-start.77
  633.4 11.5 copy-start.60
  633.7 11.3 copy-start.25
  633.7 11.3 copy-start.27
  656.4 1.5 copy-start.50
  660.4 3.3 copy-start.14
  664.5 1.9 copy-start.19
  665.2 13.3 copy-start.81
  666.3 12.1 copy-start.29
  666.3 12.1 copy-start.31
  693.4 1.6 copy-start.51
  696.1 1.1 copy-start.11
  696.5 12.8 copy-start.21
  697.2 12.1 copy-start.84
  697.5 11.8 copy-start.37
  697.5 11.8 copy-start.39
  715.8 1.6 copy-start.18
  715.8 1.6 copy-start.26
  715.8 1.6 copy-start.28
  715.8 1.6 copy-start.61
  715.8 1.6 copy-start.68
  715.8 1.6 copy-start.78
  715.8 1.6 copy-start.87
  717.4 5.4 copy-start.15
  741.3 5.3 copy-start.88
  746.4 1.0 copy-start.20
  746.4 0.9 copy-start.30
  746.4 0.9 copy-start.32
  746.4 0.9 copy-start.58
  747.4 5.0 copy-start.4
  753.1 1.0 copy-start.3
  776.3 1.0 copy-start.22
  776.3 0.9 copy-start.38
  776.3 0.9 copy-start.40
  776.3 0.9 copy-start.55
  776.4 0.9 copy-start.75
  777.3 6.8 copy-start.6
  784.8 1.0 copy-start.5
  802.9 4.6 copy-start.12
  815.0 1296.0 %all-reduce.7.cloned.1.call-start = ((), (), s32[]{:S(2)}) async-start(), calls=%async_computation.1 | async-start | bytes 1048576
  1687.3 1.3 copy-start.79
  1688.5 11.9 copy-start.45
  1688.5 11.9 copy-start.47
  1710.3 11.1 copy-start.41
  1710.4 11.1 copy-start.43
  1730.5 1.0 copy-start.23
  1731.1 11.5 copy-start.33
  1731.1 11.5 copy-start.35
  1748.3 1.1 copy-start.89
  1749.3 5.3 copy-start.10
  1755.5 1.0 copy-start.9
  1780.2 6.5 copy-start.8
  1787.5 1.0 copy-start.7
  1810.3 1.0 copy-start.24
  1810.3 0.9 copy-start.34
  1810.3 0.9 copy-start.36
  1810.3 0.9 copy-start.56
  1810.4 0.9 copy-start.76
  1836.5 4.6 copy-start.13
  1843.5 2.2 copy-start.16
  (28 other events, 21.7 us)
Sparse Core Ops, SparseCore 0:
  815.1 260.2 all-reduce.4
  1848.7 262.2 all-reduce.6
where the time goes:
time: 2130 us; the launch traced here: 2120 us
  blocking collectives  1220 us (57%)
  waiting for transfers between devices  521 us (24%)
  matrix products  287 us (13%)
  other arithmetic  40 us (2%)
  local copies, waits for them, and re-layouts  32.9 us (2%)
    all_gather x2, blocking collectives, gather_direction(): lax.all_gather(own_tiles, ('seg', 'coil', 'tile'), axis=0, tiled=True)  1220 us
    unnamed x4, waiting for transfers between devices  521 us
  transfers between devices with their start and end apart: 2, of which 2 were waited for; matrix products, arithmetic and copies ran while one was open for 0% of the time, Pallas kernels for 0%

commit v1 on v0

--- a/solution.py
+++ b/solution.py
@@ -9,6 +9,7 @@
 TV = 64
 ITERS = 2
 CAP = 256
+DEVICES = 256
 
 
 ridge_weight = 0.25
@@ -90,7 +91,13 @@
 
 
 def gather_direction(own_tiles):
-    return lax.all_gather(own_tiles, ("seg", "coil", "tile"), axis=0, tiled=True)
+    copies = jnp.tile(own_tiles, (DEVICES, 1))
+    return lax.all_to_all(copies, ("seg", "coil", "tile"), 0, 0, tiled=True)
+
+
+def sum_to_owners(partial_value):
+    parts = lax.all_to_all(partial_value, ("seg", "coil", "tile"), 0, 0, tiled=True)
+    return jnp.sum(parts.reshape(DEVICES, -1, parts.shape[1]), axis=0)
 
 
 def shards(
@@ -145,9 +152,7 @@
             )
             partial_value = partial_value.at[local_listed].add(contrib)
         image = (
-            lax.psum_scatter(
-                partial_value, ("seg", "coil", "tile"), scatter_dimension=0, tiled=True
-            )
+            sum_to_owners(partial_value)
             + ridge_weight * direction
         )
         solution_field = solution_field + step_alpha[step] * direction

time: 2130 us -> 476 us (0.22)
  blocking collectives: 1220 us -> 52.6 us
  waiting for transfers between devices: 521 us -> 20.5 us
  starting transfers between devices: 0.08 us -> 29.4 us
    all_gather x2 -> x0, blocking collectives: 1220 us -> none  [gather_direction(): lax.all_gather(own_tiles, ('seg', 'coil', 'tile'), axis=0, tiled=True)]
    unnamed x4 -> x0, waiting for transfers between devices: 521 us -> none
    all_to_all x0 -> x2, blocking collectives: none -> 52.6 us  [the longest x1 26.3 us: gather_direction(): return lax.all_to_all(copies, ('seg', 'coil', 'tile'), 0, 0, tiled=True)]
    all_to_all x0 -> x2, starting transfers between devices: none -> 29.4 us  [the longest x1 15.7 us: gather_direction(): return lax.all_to_all(copies, ('seg', 'coil', 'tile'), 0, 0, tiled=True)]
  transfers between devices with their start and end apart: 2 -> 2, of which waited for: 2 -> 1; matrix products, arithmetic and copies ran while one was open for 0% -> 6% of each run, Pallas kernels for 0% -> 0%
where the time goes in v1:
time: 476 us; the launch traced here: 467 us
  matrix products  289 us (61%)
  blocking collectives  52.6 us (11%)
  other arithmetic  43 us (9%)
  starting transfers between devices  29.4 us (6%)
  local copies, waits for them, and re-layouts  29.3 us (6%)
  waiting for transfers between devices  20.5 us (4%)
    dot_general x6, matrix products, segment_normal(): jnp.einsum('mn,cnv->cmv', row_cos, coil_imag, precision=highest)  37.9 us
    dot_general x6, matrix products, segment_normal(): jnp.einsum('mn,cnv->cmv', row_sin, coil_real, precision=highest)  37.1 us
    dot_general x6, matrix products, segment_normal(): jnp.einsum('mn,cnv->cmv', row_sin, coil_imag, precision=highest)  29.6 us
    dot_general x6, matrix products, segment_normal(): jnp.einsum('mn,cmv->cnv', row_sin, back_imag, precision=highest)  29.4 us
    dot_general x6, matrix products, segment_normal(): jnp.einsum('mn,cnv->cmv', row_cos, coil_real, precision=highest)  29.2 us
    dot_general x6, matrix products, segment_normal(): jnp.einsum('mn,cmv->cnv', row_cos, back_imag, precision=highest)  28.2 us
    dot_general x6, matrix products, segment_normal(): jnp.einsum('mn,cmv->cnv', row_cos, back_real, precision=highest)  27.8 us
    dot_general x6, matrix products, segment_normal(): jnp.einsum('mn,cmv->cnv', row_sin, back_real, precision=highest)  27.6 us
  transfers between devices with their start and end apart: 2, of which 1 were waited for; matrix products, arithmetic and copies ran while one was open for 6% of the time, Pallas kernels for 0%

profile of v1, /device:TPU:1, one launch (start us, length us, event | category | flops | bytes accessed | tf_op | source)
XLA Modules:
  0.0 466.9 jit_solution(7838437623566823040)
XLA Ops:
  0.6 1.6 tile.4
  2.3 15.7 %all-to-all-start = ((f32[256,4,128]{2,1,0:T(4,128)}), f32[256,4,128]{2,1,0:T(4,128)S(1)}, u32[]{:S(2)}, u32[]{:S(2)}) async-start(f32[256,4,128]{2,1,0:T(4,128)} %tile.4), calls=%async_computation | async-start | bytes 1048576 | tf_op jit(solution)/shard_map/all_to_all | solution.py:95
  19.4 4.4 sort.47
  26.3 4.4 sort.46
  33.7 4.4 sort.45
  49.9 4.9 %fusion.67 = f32[2,64,1024]{2,1,0:T(8,128)S(1)} fusion(f32[256]{0:T(256)S(1)} %copy-done.82, s32[256]{0:T(256)S(1)} %copy-done.70, s32[1024]{0:T(1024)S(1)} %bitcast.421, f32[2,256,128]{1,2,0:T(8,128)S(1)} %bitcast.379, f32[256,64]{0,1:T(8,128)S(1)} %get-tuple-element.41, f32[256,64]{0,1:T(8,128)S(1)} %get-tuple-element.40), kind=kOutput, calls=%fused_computation.148 | convolution fusion | flops 406683648 | bytes 923648 | tf_op jit(solution)/shard_map/mn,cnv->cmv/dot_general | solution.py:60
  54.8 6.4 %fusion.65 = f32[2,64,1024]{2,1,0:T(8,128)} fusion(f32[256]{0:T(256)S(1)} %copy-done.82, s32[256]{0:T(256)S(1)} %copy-done.70, s32[1024]{0:T(1024)S(1)} %bitcast.422, f32[2,256,128]{1,2,0:T(8,128)S(1)} %bitcast.380, f32[256,64]{0,1:T(8,128)S(1)} %get-tuple-element.41, f32[256,64]{0,1:T(8,128)S(1)} %get-tuple-element.40), kind=kOutput, calls=%fused_computation.146 | convolution fusion | flops 406683648 | bytes 923648 | tf_op jit(solution)/shard_map/mn,cnv->cmv/dot_general | solution.py:63
  61.2 4.9 %fusion.4 = f32[2,1024,64]{1,2,0:T(8,128)S(1)} fusion(f32[2,64,1024]{2,1,0:T(8,128)S(1)} %fusion.67, f32[256]{0:T(256)S(1)} %copy-done.82, s32[256]{0:T(256)S(1)} %copy-done.70, s32[1024]{0:T(1024)S(1)} %bitcast.423, f32[2,256,128]{1,2,0:T(8,128)S(1)} %bitcast.381, f32[256,64]{0,1:T(8,128)S(1)} %get-tuple-element.41, f32[256,64]{0,1:T(8,128)S(1)} %get-tuple-element.40), kind=kOutput, calls=%fused_computation.49 | convolution fusion | flops 407076864 | bytes 1447936 | tf_op jit(solution)/shard_map/mn,cnv->cmv/dot_general | solution.py:60
  71.3 6.6 %fusion.89 = f32[2,64,1024]{2,1,0:T(8,128)} fusion(f32[256]{0:T(256)S(1)} %copy-done.78, s32[256]{0:T(256)S(1)} %copy-done.66, s32[1024]{0:T(1024)S(1)} %bitcast.406, f32[2,256,128]{1,2,0:T(8,128)S(1)} %bitcast.369, f32[256,64]{0,1:T(8,128)S(1)} %get-tuple-element.45, f32[256,64]{0,1:T(8,128)S(1)} %get-tuple-element.44), kind=kOutput, calls=%fused_computation.170 | convolution fusion | flops 406683648 | bytes 923648 | tf_op jit(solution)/shard_map/mn,cnv->cmv/dot_general | solution.py:63
  77.8 4.9 %fusion.91 = f32[2,64,1024]{2,1,0:T(8,128)S(1)} fusion(f32[256]{0:T(256)S(1)} %copy-done.78, s32[256]{0:T(256)S(1)} %copy-done.66, s32[1024]{0:T(1024)S(1)} %bitcast.407, f32[2,256,128]{1,2,0:T(8,128)S(1)} %bitcast.370, f32[256,64]{0,1:T(8,128)S(1)} %get-tuple-element.45, f32[256,64]{0,1:T(8,128)S(1)} %get-tuple-element.44), kind=kOutput, calls=%fused_computation.172 | convolution fusion | flops 406683648 | bytes 923648 | tf_op jit(solution)/shard_map/mn,cnv->cmv/dot_general | solution.py:60
  82.7 4.9 %fusion.2 = f32[2,1024,64]{1,2,0:T(8,128)S(1)} fusion(f32[2,64,1024]{2,1,0:T(8,128)S(1)} %fusion.91, f32[256]{0:T(256)S(1)} %copy-done.78, s32[256]{0:T(256)S(1)} %copy-done.66, s32[1024]{0:T(1024)S(1)} %bitcast.408, f32[2,256,128]{1,2,0:T(8,128)S(1)} %bitcast.371, f32[256,64]{0,1:T(8,128)S(1)} %get-tuple-element.45, f32[256,64]{0,1:T(8,128)S(1)} %get-tuple-element.44), kind=kOutput, calls=%fused_computation.47 | convolution fusion | flops 407076864 | bytes 1447936 | tf_op jit(solution)/shard_map/mn,cnv->cmv/dot_general | solution.py:60
  93.0 6.1 %fusion.113 = f32[2,64,1024]{2,1,0:T(8,128)} fusion(f32[256]{0:T(256)S(1)} %copy-done.74, s32[256]{0:T(256)S(1)} %copy-done.62, s32[1024]{0:T(1024)S(1)} %bitcast.389, f32[2,256,128]{1,2,0:T(8,128)S(1)} %bitcast.359, f32[256,64]{0,1:T(8,128)S(1)} %get-tuple-element.49, f32[256,64]{0,1:T(8,128)S(1)} %get-tuple-element.48), kind=kOutput, calls=%fused_computation.194 | convolution fusion | flops 406683648 | bytes 923648 | tf_op jit(solution)/shard_map/mn,cnv->cmv/dot_general | solution.py:63
  99.1 4.9 %fusion.115 = f32[2,64,1024]{2,1,0:T(8,128)S(1)} fusion(f32[256]{0:T(256)S(1)} %copy-done.74, s32[256]{0:T(256)S(1)} %copy-done.62, s32[1024]{0:T(1024)S(1)} %bitcast.390, f32[2,256,128]{1,2,0:T(8,128)S(1)} %bitcast.360, f32[256,64]{0,1:T(8,128)S(1)} %get-tuple-element.49, f32[256,64]{0,1:T(8,128)S(1)} %get-tuple-element.48), kind=kOutput, calls=%fused_computation.196 | convolution fusion | flops 406683648 | bytes 923648 | tf_op jit(solution)/shard_map/mn,cnv->cmv/dot_general | solution.py:60
  104.0 4.9 %fusion = f32[2,1024,64]{1,2,0:T(8,128)S(1)} fusion(f32[2,64,1024]{2,1,0:T(8,128)S(1)} %fusion.115, f32[256]{0:T(256)S(1)} %copy-done.74, s32[256]{0:T(256)S(1)} %copy-done.62, s32[1024]{0:T(1024)S(1)} %bitcast.391, f32[2,256,128]{1,2,0:T(8,128)S(1)} %bitcast.361, f32[256,64]{0,1:T(8,128)S(1)} %get-tuple-element.49, f32[256,64]{0,1:T(8,128)S(1)} %get-tuple-element.48), kind=kOutput, calls=%fused_computation.45 | convolution fusion | flops 407076864 | bytes 1447936 | tf_op jit(solution)/shard_map/mn,cnv->cmv/dot_general | solution.py:60
  110.9 5.3 %fusion.5 = f32[2,1024,64]{1,2,0:T(8,128)S(1)} fusion(f32[2,64,1024]{2,1,0:T(8,128)S(1)} %copy-done.86, f32[256]{0:T(256)S(1)} %copy-done.83, s32[256]{0:T(256)S(1)} %copy-done.71, s32[1024]{0:T(1024)S(1)} %bitcast.424, f32[2,256,128]{1,2,0:T(8,128)S(1)} %bitcast.382, f32[256,64]{0,1:T(8,128)S(1)} %copy-done.37, f32[256,64]{0,1:T(8,128)S(1)} %copy-done.35), kind=kOutput, calls=%fused_computation.50 | convolution fusion | flops 407076864 | bytes 1447936 | tf_op jit(solution)/shard_map/mn,cnv->cmv/dot_general | solution.py:63
  120.4 4.7 %fusion.63 = f32[2,64,256]{2,1,0:T(8,128)S(1)} fusion(f32[2,1024,64]{1,2,0:T(8,128)S(1)} %convolution_add_fusion.12, f32[256]{0:T(256)S(1)} %copy-done.83, s32[256]{0:T(256)S(1)} %copy-done.71, s32[1024]{0:T(1024)S(1)} %bitcast.425), kind=kOutput, calls=%fused_computation.144 | convolution fusion | flops 406585344 | bytes 661504 | tf_op jit(solution)/shard_map/mn,cmv->cnv/dot_general | solution.py:80
  125.8 4.5 fusion.61
  130.4 4.6 fusion.30
  135.0 5.6 %subtract_reduce_fusion.3 = (f32[256,64]{0,1:T(8,128)S(1)}, f32[256,64]{0,1:T(8,128)S(1)}) fusion(f32[2,256,64]{1,2,0:T(8,128)S(1)} %fusion.30, f32[2,256,128]{1,2,0:T(8,128)S(1)} %bitcast.383, f32[2,64,256]{2,1,0:T(8,128)S(1)} %fusion.63, f32[2,1024,64]{1,2,0:T(8,128)S(1)} %convolution_subtract_fusion.12, f32[256]{0:T(256)S(1)} %copy-done.83, ...), kind=kOutput, calls=%fused_computation.229 | convolution fusion | flops 407109632 | bytes 1185792 | tf_op jit(solution)/shard_map/mn,cmv->cnv/dot_general | solution.py:80
  141.0 6.5 %fusion.3 = f32[2,1024,64]{1,2,0:T(8,128)S(1)} fusion(f32[2,64,1024]{2,1,0:T(8,128)} %fusion.89, f32[256]{0:T(256)} %compare_select_fusion.4, s32[256]{0:T(256)} %get-tuple-element.69, s32[1024]{0:T(1024)S(1)} %bitcast.409, f32[2,256,128]{1,2,0:T(8,128)S(1)} %bitcast.372, f32[256,64]{0,1:T(8,128)} %copy-done.33, f32[256,64]{0,1:T(8,128)} %copy-done.32), kind=kOutput, calls=%fused_computation.48 | convolution fusion | flops 407076864 | bytes 1447936 | tf_op jit(solution)/shard_map/mn,cnv->cmv/dot_general | solution.py:63
  151.7 4.5 fusion.87
  156.9 4.7 %fusion.85 = f32[2,64,256]{2,1,0:T(8,128)S(1)} fusion(f32[2,1024,64]{1,2,0:T(8,128)S(1)} %convolution_subtract_fusion.14, f32[256]{0:T(256)S(1)} %copy-done.79, s32[256]{0:T(256)S(1)} %copy-done.67, s32[1024]{0:T(1024)S(1)} %bitcast.411), kind=kOutput, calls=%fused_computation.166 | convolution fusion | flops 406585344 | bytes 661504 | tf_op jit(solution)/shard_map/mn,cmv->cnv/dot_general | solution.py:83
  161.7 4.6 fusion.32
  166.3 4.6 subtract_reduce_fusion.4
  172.1 7.0 %fusion.1 = f32[2,1024,64]{1,2,0:T(8,128)S(1)} fusion(f32[2,64,1024]{2,1,0:T(8,128)} %fusion.113, f32[256]{0:T(256)} %compare_select_fusion.5, s32[256]{0:T(256)S(1)} %copy-done.63, s32[1024]{0:T(1024)S(1)} %bitcast.392, f32[2,256,128]{1,2,0:T(8,128)} %bitcast.362, f32[256,64]{0,1:T(8,128)S(1)} %copy-done.29, f32[256,64]{0,1:T(8,128)S(1)} %copy-done.27), kind=kOutput, calls=%fused_computation.46 | convolution fusion | flops 407076864 | bytes 1447936 | tf_op jit(solution)/shard_map/mn,cnv->cmv/dot_general | solution.py:63
  182.9 4.5 fusion.111
  188.2 4.7 %fusion.109 = f32[2,64,256]{2,1,0:T(8,128)S(1)} fusion(f32[2,1024,64]{1,2,0:T(8,128)S(1)} %convolution_subtract_fusion.16, f32[256]{0:T(256)S(1)} %copy-done.75, s32[256]{0:T(256)S(1)} %copy-done.63, s32[1024]{0:T(1024)S(1)} %bitcast.394), kind=kOutput, calls=%fused_computation.190 | convolution fusion | flops 406585344 | bytes 661504 | tf_op jit(solution)/shard_map/mn,cmv->cnv/dot_general | solution.py:83
  192.9 4.6 fusion.34
  197.5 4.6 subtract_reduce_fusion.5
  202.5 2.6 scatter_custom_fusion
  205.1 3.6 scatter_fusion
  208.7 3.6 scatter_fusion.1
  212.3 13.7 %all-to-all-start.1 = ((f32[256,4,128]{2,1,0:T(4,128)}), f32[256,4,128]{2,1,0:T(4,128)S(1)}, u32[]{:S(2)}, u32[]{:S(2)}) async-start(f32[256,4,128]{2,1,0:T(4,128)} %bitcast.32), calls=%async_computation.1 | async-start | bytes 1048576 | tf_op jit(solution)/shard_map/all_to_all | solution.py:99
  226.6 20.5 %all-to-all-done.1 = f32[256,4,128]{2,1,0:T(4,128)S(1)} async-done(((f32[256,4,128]{2,1,0:T(4,128)}), f32[256,4,128]{2,1,0:T(4,128)S(1)}, u32[]{:S(2)}, u32[]{:S(2)}) %all-to-all-start.1) | async-done | bytes 524320 | tf_op jit(solution)/shard_map/all_to_all | solution.py:99
  248.9 26.3 %all_to_all.36 = f32[256,4,128]{2,1,0:T(4,128)S(1)} all-to-all(f32[256,4,128]{2,1,0:T(4,128)S(1)} %tile.5), channel_id=1, replica_groups=mesh['seg'=8,'coil'=16,'tile'=2] {'seg','coil','tile'}, dimensions={0} | all-to-all | bytes 1048576 | tf_op jit(solution)/shard_map/all_to_all | solution.py:95
  278.2 6.5 %fusion.57 = f32[2,64,1024]{2,1,0:T(8,128)} fusion(f32[256]{0:T(256)S(1)} %copy-done.84, s32[256]{0:T(256)S(1)} %copy-done.72, s32[1024]{0:T(1024)S(1)} %bitcast.429, f32[2,256,128]{1,2,0:T(8,128)S(1)} %bitcast.384, f32[256,64]{0,1:T(8,128)S(1)} %get-tuple-element.29, f32[256,64]{0,1:T(8,128)S(1)} %get-tuple-element.28), kind=kOutput, calls=%fused_computation.138 | convolution fusion | flops 406683648 | bytes 923648 | tf_op jit(solution)/shard_map/mn,cnv->cmv/dot_general | solution.py:63
  284.7 4.9 %fusion.59 = f32[2,64,1024]{2,1,0:T(8,128)S(1)} fusion(f32[256]{0:T(256)S(1)} %copy-done.84, s32[256]{0:T(256)S(1)} %copy-done.72, s32[1024]{0:T(1024)S(1)} %bitcast.430, f32[2,256,128]{1,2,0:T(8,128)S(1)} %bitcast.385, f32[256,64]{0,1:T(8,128)S(1)} %get-tuple-element.29, f32[256,64]{0,1:T(8,128)S(1)} %get-tuple-element.28), kind=kOutput, calls=%fused_computation.140 | convolution fusion | flops 406683648 | bytes 923648 | tf_op jit(solution)/shard_map/mn,cnv->cmv/dot_general | solution.py:60
  289.6 4.9 %fusion.10 = f32[2,1024,64]{1,2,0:T(8,128)S(1)} fusion(f32[2,64,1024]{2,1,0:T(8,128)S(1)} %fusion.59, f32[256]{0:T(256)S(1)} %copy-done.84, s32[256]{0:T(256)S(1)} %copy-done.72, s32[1024]{0:T(1024)S(1)} %bitcast.431, f32[2,256,128]{1,2,0:T(8,128)S(1)} %bitcast.386, f32[256,64]{0,1:T(8,128)S(1)} %get-tuple-element.29, f32[256,64]{0,1:T(8,128)S(1)} %get-tuple-element.28), kind=kOutput, calls=%fused_computation.55 | convolution fusion | flops 407076864 | bytes 1447936 | tf_op jit(solution)/shard_map/mn,cnv->cmv/dot_general | solution.py:60
  300.1 6.2 %fusion.81 = f32[2,64,1024]{2,1,0:T(8,128)} fusion(f32[256]{0:T(256)S(1)} %copy-done.80, s32[256]{0:T(256)S(1)} %copy-done.68, s32[1024]{0:T(1024)S(1)} %bitcast.414, f32[2,256,128]{1,2,0:T(8,128)S(1)} %bitcast.374, f32[256,64]{0,1:T(8,128)S(1)} %get-tuple-element.33, f32[256,64]{0,1:T(8,128)S(1)} %get-tuple-element.32), kind=kOutput, calls=%fused_computation.162 | convolution fusion | flops 406683648 | bytes 923648 | tf_op jit(solution)/shard_map/mn,cnv->cmv/dot_general | solution.py:63
  306.3 4.9 %fusion.83 = f32[2,64,1024]{2,1,0:T(8,128)S(1)} fusion(f32[256]{0:T(256)S(1)} %copy-done.80, s32[256]{0:T(256)S(1)} %copy-done.68, s32[1024]{0:T(1024)S(1)} %bitcast.415, f32[2,256,128]{1,2,0:T(8,128)S(1)} %bitcast.375, f32[256,64]{0,1:T(8,128)S(1)} %get-tuple-element.33, f32[256,64]{0,1:T(8,128)S(1)} %get-tuple-element.32), kind=kOutput, calls=%fused_computation.164 | convolution fusion | flops 406683648 | bytes 923648 | tf_op jit(solution)/shard_map/mn,cnv->cmv/dot_general | solution.py:60
  311.1 4.9 %fusion.8 = f32[2,1024,64]{1,2,0:T(8,128)S(1)} fusion(f32[2,64,1024]{2,1,0:T(8,128)S(1)} %fusion.83, f32[256]{0:T(256)S(1)} %copy-done.80, s32[256]{0:T(256)S(1)} %copy-done.68, s32[1024]{0:T(1024)S(1)} %bitcast.416, f32[2,256,128]{1,2,0:T(8,128)S(1)} %bitcast.376, f32[256,64]{0,1:T(8,128)S(1)} %get-tuple-element.33, f32[256,64]{0,1:T(8,128)S(1)} %get-tuple-element.32), kind=kOutput, calls=%fused_computation.53 | convolution fusion | flops 407076864 | bytes 1447936 | tf_op jit(solution)/shard_map/mn,cnv->cmv/dot_general | solution.py:60
  321.9 6.1 %fusion.105 = f32[2,64,1024]{2,1,0:T(8,128)} fusion(f32[256]{0:T(256)S(1)} %copy-done.76, s32[256]{0:T(256)S(1)} %copy-done.64, s32[1024]{0:T(1024)S(1)} %bitcast.397, f32[2,256,128]{1,2,0:T(8,128)S(1)} %bitcast.364, f32[256,64]{0,1:T(8,128)S(1)} %get-tuple-element.37, f32[256,64]{0,1:T(8,128)S(1)} %get-tuple-element.36), kind=kOutput, calls=%fused_computation.186 | convolution fusion | flops 406683648 | bytes 923648 | tf_op jit(solution)/shard_map/mn,cnv->cmv/dot_general | solution.py:63
  328.0 4.9 %fusion.107 = f32[2,64,1024]{2,1,0:T(8,128)S(1)} fusion(f32[256]{0:T(256)S(1)} %copy-done.76, s32[256]{0:T(256)S(1)} %copy-done.64, s32[1024]{0:T(1024)S(1)} %bitcast.398, f32[2,256,128]{1,2,0:T(8,128)S(1)} %bitcast.365, f32[256,64]{0,1:T(8,128)S(1)} %get-tuple-element.37, f32[256,64]{0,1:T(8,128)S(1)} %get-tuple-element.36), kind=kOutput, calls=%fused_computation.188 | convolution fusion | flops 406683648 | bytes 923648 | tf_op jit(solution)/shard_map/mn,cnv->cmv/dot_general | solution.py:60
  332.9 4.9 %fusion.6 = f32[2,1024,64]{1,2,0:T(8,128)S(1)} fusion(f32[2,64,1024]{2,1,0:T(8,128)S(1)} %fusion.107, f32[256]{0:T(256)S(1)} %copy-done.76, s32[256]{0:T(256)S(1)} %copy-done.64, s32[1024]{0:T(1024)S(1)} %bitcast.399, f32[2,256,128]{1,2,0:T(8,128)S(1)} %bitcast.366, f32[256,64]{0,1:T(8,128)S(1)} %get-tuple-element.37, f32[256,64]{0,1:T(8,128)S(1)} %get-tuple-element.36), kind=kOutput, calls=%fused_computation.51 | convolution fusion | flops 407076864 | bytes 1447936 | tf_op jit(solution)/shard_map/mn,cnv->cmv/dot_general | solution.py:60
  339.8 5.1 %fusion.11 = f32[2,1024,64]{1,2,0:T(8,128)S(1)} fusion(f32[2,64,1024]{2,1,0:T(8,128)S(1)} %copy-done.87, f32[256]{0:T(256)S(1)} %copy-done.85, s32[256]{0:T(256)S(1)} %copy-done.73, s32[1024]{0:T(1024)S(1)} %bitcast.432, f32[2,256,128]{1,2,0:T(8,128)S(1)} %bitcast.387, f32[256,64]{0,1:T(8,128)S(1)} %copy-done.41, f32[256,64]{0,1:T(8,128)S(1)} %copy-done.39), kind=kOutput, calls=%fused_computation.56 | convolution fusion | flops 407076864 | bytes 1447936 | tf_op jit(solution)/shard_map/mn,cnv->cmv/dot_general | solution.py:63
  349.0 4.9 %fusion.55 = f32[2,64,256]{2,1,0:T(8,128)S(1)} fusion(f32[2,1024,64]{1,2,0:T(8,128)S(1)} %convolution_add_fusion.6, f32[256]{0:T(256)S(1)} %copy-done.85, s32[256]{0:T(256)S(1)} %copy-done.73, s32[1024]{0:T(1024)S(1)} %bitcast.433), kind=kOutput, calls=%fused_computation.136 | convolution fusion | flops 406585344 | bytes 661504 | tf_op jit(solution)/shard_map/mn,cmv->cnv/dot_general | solution.py:80
  354.7 4.5 fusion.53
  359.3 4.6 fusion.24
  363.9 5.4 %subtract_reduce_fusion = (f32[256,64]{0,1:T(8,128)S(1)}, f32[256,64]{0,1:T(8,128)S(1)}) fusion(f32[2,256,64]{1,2,0:T(8,128)S(1)} %fusion.24, f32[2,256,128]{1,2,0:T(8,128)S(1)} %bitcast.388, f32[2,64,256]{2,1,0:T(8,128)S(1)} %fusion.55, f32[2,1024,64]{1,2,0:T(8,128)S(1)} %convolution_subtract_fusion.6, f32[256]{0:T(256)S(1)} %copy-done.85, ...), kind=kOutput, calls=%fused_computation.217 | convolution fusion | flops 407109632 | bytes 1185792 | tf_op jit(solution)/shard_map/mn,cmv->cnv/dot_general | solution.py:80
  369.7 6.5 %fusion.9 = f32[2,1024,64]{1,2,0:T(8,128)S(1)} fusion(f32[2,64,1024]{2,1,0:T(8,128)} %fusion.81, f32[256]{0:T(256)} %compare_select_fusion.4, s32[256]{0:T(256)} %get-tuple-element.69, s32[1024]{0:T(1024)} %bitcast.405, f32[2,256,128]{1,2,0:T(8,128)S(1)} %bitcast.377, f32[256,64]{0,1:T(8,128)} %copy-done.31, f32[256,64]{0,1:T(8,128)} %copy-done.30), kind=kOutput, calls=%fused_computation.54 | convolution fusion | flops 407076864 | bytes 1447936 | tf_op jit(solution)/shard_map/mn,cnv->cmv/dot_general | solution.py:63
  380.3 4.5 fusion.79
  385.6 4.9 %fusion.77 = f32[2,64,256]{2,1,0:T(8,128)S(1)} fusion(f32[2,1024,64]{1,2,0:T(8,128)S(1)} %convolution_subtract_fusion.8, f32[256]{0:T(256)S(1)} %copy-done.81, s32[256]{0:T(256)S(1)} %copy-done.69, s32[1024]{0:T(1024)S(1)} %bitcast.418), kind=kOutput, calls=%fused_computation.158 | convolution fusion | flops 406585344 | bytes 661504 | tf_op jit(solution)/shard_map/mn,cmv->cnv/dot_general | solution.py:83
  390.5 4.6 fusion.26
  395.2 4.6 subtract_reduce_fusion.1
  400.9 6.6 %fusion.7 = f32[2,1024,64]{1,2,0:T(8,128)S(1)} fusion(f32[2,64,1024]{2,1,0:T(8,128)} %fusion.105, f32[256]{0:T(256)S(1)} %copy-done.77, s32[256]{0:T(256)S(1)} %copy-done.65, s32[1024]{0:T(1024)S(1)} %bitcast.400, f32[2,256,128]{1,2,0:T(8,128)S(1)} %bitcast.367, f32[256,64]{0,1:T(8,128)S(1)} %copy-done.25, f32[256,64]{0,1:T(8,128)S(1)} %copy-done.23), kind=kOutput, calls=%fused_computation.52 | convolution fusion | flops 407076864 | bytes 1447936 | tf_op jit(solution)/shard_map/mn,cnv->cmv/dot_general | solution.py:63
  411.4 4.5 fusion.103
  416.7 4.7 %fusion.101 = f32[2,64,256]{2,1,0:T(8,128)S(1)} fusion(f32[2,1024,64]{1,2,0:T(8,128)S(1)} %convolution_subtract_fusion.10, f32[256]{0:T(256)S(1)} %copy-done.77, s32[256]{0:T(256)S(1)} %copy-done.65, s32[1024]{0:T(1024)S(1)} %bitcast.402), kind=kOutput, calls=%fused_computation.182 | convolution fusion | flops 406585344 | bytes 661504 | tf_op jit(solution)/shard_map/mn,cmv->cnv/dot_general | solution.py:83
  421.4 4.6 fusion.28
  426.0 4.6 subtract_reduce_fusion.2
  431.0 1.9 scatter_custom_fusion.3
  433.0 2.1 scatter_fusion.2
  435.1 2.1 scatter_fusion.3
  437.3 26.3 %all_to_all.37 = f32[256,4,128]{2,1,0:T(4,128)S(1)} all-to-all(f32[256,4,128]{2,1,0:T(4,128)S(1)} %bitcast.358), channel_id=1, replica_groups=mesh['seg'=8,'coil'=16,'tile'=2] {'seg','coil','tile'}, dimensions={0} | all-to-all | bytes 1048576 | tf_op jit(solution)/shard_map/all_to_all | solution.py:99
  464.5 1.9 multiply_subtract_fusion.18
  (308 shorter events, 81.7 us)
Async XLA Ops:
  0.6 24.7 %copy-start = (f32[2,1024,128]{2,1,0:T(8,128)S(1)}, f32[2,1024,128]{2,1,0:T(8,128)}, u32[]{:S(2)}) copy-start(f32[2,1024,128]{2,1,0:T(8,128)} %param.9) | copy-start | bytes 3145732
  2.3 22.0 %copy-start.13 = (f32[1024,64]{0,1:T(8,128)S(1)}, f32[1024,64]{0,1:T(8,128)}, u32[]{:S(2)}) copy-start(f32[1024,64]{0,1:T(8,128)} %param.10) | copy-start | bytes 786436
  2.3 45.5 %all-to-all-start = ((f32[256,4,128]{2,1,0:T(4,128)}), f32[256,4,128]{2,1,0:T(4,128)S(1)}, u32[]{:S(2)}, u32[]{:S(2)}) async-start(f32[256,4,128]{2,1,0:T(4,128)} %tile.4), calls=%async_computation | async-start | bytes 1048576 | tf_op jit(solution)/shard_map/all_to_all | solution.py:95
  24.3 0.9 copy-start.46
  31.2 38.0 %copy-start.45 = (s32[1024]{0:T(1024)}, s32[1024]{0:T(1024)S(1)}, u32[]{:S(2)}) copy-start(s32[1024]{0:T(1024)S(1)} %pad_clamp_fusion.1) | copy-start | bytes 12292
  39.2 51.6 %copy-start.44 = (s32[1024]{0:T(1024)}, s32[1024]{0:T(1024)S(1)}, u32[]{:S(2)}) copy-start(s32[1024]{0:T(1024)S(1)} %pad_clamp_fusion.2) | copy-start | bytes 12292
  41.0 7.9 %copy-start.9 = (f32[256,64]{0,1:T(8,128)}, f32[256,64]{0,1:T(8,128)S(1)}, u32[]{:S(2)}) copy-start(f32[256,64]{0,1:T(8,128)S(1)} %copy.207) | copy-start | bytes 196612
  42.1 124.2 %copy-start.16 = (f32[256,2,128]{0,2,1:T(8,128)}, f32[256,2,128]{0,2,1:T(8,128)S(1)}, u32[]{:S(2)}) copy-start(f32[256,2,128]{0,2,1:T(8,128)S(1)} %copy.202) | copy-start | bytes 786436
  42.2 3.8 copy-start.47
  42.3 61.7 %copy-start.14 = (f32[256,2,128]{0,2,1:T(8,128)}, f32[256,2,128]{0,2,1:T(8,128)S(1)}, u32[]{:S(2)}) copy-start(f32[256,2,128]{0,2,1:T(8,128)S(1)} %copy.196) | copy-start | bytes 786436
  48.9 1.0 copy-start.18
  48.9 0.9 copy-start.82
  49.2 12.0 %copy-start.34 = (f32[256,64]{0,1:T(8,128)}, f32[256,64]{0,1:T(8,128)S(1)}, u32[]{:S(2)}) copy-start(f32[256,64]{0,1:T(8,128)S(1)} %get-tuple-element.40) | copy-start | bytes 196612
  49.2 12.0 %copy-start.36 = (f32[256,64]{0,1:T(8,128)}, f32[256,64]{0,1:T(8,128)S(1)}, u32[]{:S(2)}) copy-start(f32[256,64]{0,1:T(8,128)S(1)} %get-tuple-element.41) | copy-start | bytes 196612
  70.5 12.2 %copy-start.32 = (f32[256,64]{0,1:T(8,128)}, f32[256,64]{0,1:T(8,128)S(1)}, u32[]{:S(2)}) copy-start(f32[256,64]{0,1:T(8,128)S(1)} %get-tuple-element.44) | copy-start | bytes 196612
  70.6 12.2 %copy-start.33 = (f32[256,64]{0,1:T(8,128)}, f32[256,64]{0,1:T(8,128)S(1)}, u32[]{:S(2)}) copy-start(f32[256,64]{0,1:T(8,128)S(1)} %get-tuple-element.45) | copy-start | bytes 196612
  92.2 11.8 %copy-start.26 = (f32[256,64]{0,1:T(8,128)}, f32[256,64]{0,1:T(8,128)S(1)}, u32[]{:S(2)}) copy-start(f32[256,64]{0,1:T(8,128)S(1)} %get-tuple-element.48) | copy-start | bytes 196612
  92.2 11.8 %copy-start.28 = (f32[256,64]{0,1:T(8,128)}, f32[256,64]{0,1:T(8,128)S(1)}, u32[]{:S(2)}) copy-start(f32[256,64]{0,1:T(8,128)S(1)} %get-tuple-element.49) | copy-start | bytes 196612
  109.7 1.0 copy-start.19
  109.7 0.9 copy-start.35
  109.7 0.9 copy-start.37
  109.7 0.9 copy-start.56
  109.8 0.9 copy-start.71
  109.8 0.9 copy-start.83
  109.8 1.2 copy-start.86
  110.9 5.3 %copy-start.7 = (f32[2,1024,64]{1,2,0:T(8,128)S(1)}, f32[2,1024,64]{1,2,0:T(8,128)}, u32[]{:S(2)}) copy-start(f32[2,1024,64]{1,2,0:T(8,128)} %fusion.180) | copy-start | bytes 1572868
  117.0 1.0 copy-start.5
  135.0 5.6 %copy-start.10 = (f32[256,64]{0,1:T(8,128)S(1)}, f32[256,64]{0,1:T(8,128)}, u32[]{:S(2)}) copy-start(f32[256,64]{0,1:T(8,128)} %copy-done.9) | copy-start | bytes 196612
  141.0 6.6 %copy-start.4 = (f32[2,1024,64]{1,2,0:T(8,128)S(1)}, f32[2,1024,64]{1,2,0:T(8,128)}, u32[]{:S(2)}) copy-start(f32[2,1024,64]{1,2,0:T(8,128)} %fusion.187) | copy-start | bytes 1572868
  148.3 1.0 copy-start.3
  171.2 0.8 copy-start.27
  171.2 0.9 copy-start.29
  171.2 0.9 copy-start.63
  192.9 4.6 copy-start.15
  212.3 13.7 %copy-start.61 = (f32[2]{0:T(128)S(1)}, f32[2]{0:T(128)}, u32[]{:S(2)}) copy-start(f32[2]{0:T(128)} %param.14) | copy-start | bytes 28
  212.3 34.8 %all-to-all-start.1 = ((f32[256,4,128]{2,1,0:T(4,128)}), f32[256,4,128]{2,1,0:T(4,128)S(1)}, u32[]{:S(2)}, u32[]{:S(2)}) async-start(f32[256,4,128]{2,1,0:T(4,128)} %bitcast.32), calls=%async_computation.1 | async-start | bytes 1048576 | tf_op jit(solution)/shard_map/all_to_all | solution.py:99
  275.2 2.3 copy-start.84
  276.4 1.1 copy-start.20
  277.5 12.1 %copy-start.38 = (f32[256,64]{0,1:T(8,128)}, f32[256,64]{0,1:T(8,128)S(1)}, u32[]{:S(2)}) copy-start(f32[256,64]{0,1:T(8,128)S(1)} %get-tuple-element.28) | copy-start | bytes 196612
  277.5 12.1 %copy-start.40 = (f32[256,64]{0,1:T(8,128)}, f32[256,64]{0,1:T(8,128)S(1)}, u32[]{:S(2)}) copy-start(f32[256,64]{0,1:T(8,128)S(1)} %get-tuple-element.29) | copy-start | bytes 196612
  297.6 1.8 copy-start.80
  298.8 1.0 copy-start.17
  298.9 0.9 copy-start.53
  299.4 11.8 %copy-start.30 = (f32[256,64]{0,1:T(8,128)}, f32[256,64]{0,1:T(8,128)S(1)}, u32[]{:S(2)}) copy-start(f32[256,64]{0,1:T(8,128)S(1)} %get-tuple-element.32) | copy-start | bytes 196612
  299.4 11.8 %copy-start.31 = (f32[256,64]{0,1:T(8,128)}, f32[256,64]{0,1:T(8,128)S(1)}, u32[]{:S(2)}) copy-start(f32[256,64]{0,1:T(8,128)S(1)} %get-tuple-element.33) | copy-start | bytes 196612
  319.2 2.0 copy-start.76
  321.1 11.8 %copy-start.22 = (f32[256,64]{0,1:T(8,128)}, f32[256,64]{0,1:T(8,128)S(1)}, u32[]{:S(2)}) copy-start(f32[256,64]{0,1:T(8,128)S(1)} %get-tuple-element.36) | copy-start | bytes 196612
  321.1 11.8 %copy-start.24 = (f32[256,64]{0,1:T(8,128)}, f32[256,64]{0,1:T(8,128)S(1)}, u32[]{:S(2)}) copy-start(f32[256,64]{0,1:T(8,128)S(1)} %get-tuple-element.37) | copy-start | bytes 196612
  338.6 1.0 copy-start.21
  338.6 0.9 copy-start.39
  338.6 0.9 copy-start.41
  338.6 0.9 copy-start.58
  338.6 0.9 copy-start.73
  338.6 0.9 copy-start.85
  338.7 1.2 copy-start.87
  339.8 5.1 %copy-start.8 = (f32[2,1024,64]{1,2,0:T(8,128)S(1)}, f32[2,1024,64]{1,2,0:T(8,128)}, u32[]{:S(2)}) copy-start(f32[2,1024,64]{1,2,0:T(8,128)} %fusion.159) | copy-start | bytes 1572868
  345.7 1.0 copy-start.6
  363.9 5.4 %copy-start.12 = (f32[256,64]{0,1:T(8,128)S(1)}, f32[256,64]{0,1:T(8,128)}, u32[]{:S(2)}) copy-start(f32[256,64]{0,1:T(8,128)} %copy-done.9) | copy-start | bytes 196612
  369.6 6.5 %copy-start.2 = (f32[2,1024,64]{1,2,0:T(8,128)S(1)}, f32[2,1024,64]{1,2,0:T(8,128)}, u32[]{:S(2)}) copy-start(f32[2,1024,64]{1,2,0:T(8,128)} %fusion.166) | copy-start | bytes 1572868
  376.9 1.0 copy-start.1
  400.1 0.8 copy-start.23
  400.1 0.9 copy-start.25
  400.1 0.9 copy-start.51
  400.1 0.8 copy-start.65
  (26 other events, 18.7 us)

commit v2 on v1

v2 whole, which is shorter than its diff:
```python
import math

import jax
import jax.numpy as jnp
import ml_dtypes
import numpy as np
from jax import lax
from jax.experimental import pallas as pl
from jax.experimental.pallas import tpu as pltpu
from jax.sharding import PartitionSpec as P

SEGS = 24
TV = 64
ITERS = 2
DEVICES = 256
TILES = 1024
BLOCKS = 8
SPAN = TILES // BLOCKS
LANES = 2 * TV
AXES = ("seg", "coil", "tile")

ridge_weight = 0.25
half_root = math.sqrt(0.5)


def split_constant(matrix):
    high = matrix.astype(np.float32).astype(ml_dtypes.bfloat16)
    low = (matrix - high.astype(np.float64)).astype(np.float32).astype(ml_dtypes.bfloat16)
    return high, low


def complex_block(real, imag):
    return np.block([[real, -imag], [imag, real]])


def transform_constants():
    steps = np.arange(SPAN)
    row = np.exp(-2j * np.pi * (np.outer(steps, steps) % SPAN) / SPAN)
    row_high, row_low = split_constant(complex_block(row.real, row.imag))
    back_high, back_low = split_constant(complex_block(row.real, -row.imag))
    row_ahead = np.concatenate([row_high, row_low, row_high], axis=1)
    row_back = np.concatenate([back_high, back_low, back_high], axis=1)
    steps = np.arange(TV)
    column = np.exp(-2j * np.pi * (np.outer(steps, steps) % TV) / TV)
    column = np.kron(np.eye(2), column)
    column_high, column_low = split_constant(complex_block(column.real, -column.imag))
    conj_high, conj_low = split_constant(complex_block(column.real, column.imag))
    column_ahead = np.concatenate([column_high, column_high, column_low], axis=0)
    column_back = np.concatenate([conj_high, conj_high, conj_low], axis=0)
    twist = np.exp(-2j * np.pi * np.outer(np.arange(BLOCKS), np.arange(SPAN)) / TILES).reshape(TILES, 1)
    twist = np.stack([twist.real, twist.imag]).astype(np.float32)
    return row_ahead, row_back, column_ahead, column_back, twist


def split(value):
    high = value.astype(jnp.bfloat16)
    low = (value - high.astype(jnp.float32)).astype(jnp.bfloat16)
    return high, low


def four_point(real, imag):
    sum_a, dif_a = (real[0] + real[2], imag[0] + imag[2]), (real[0] - real[2], imag[0] - imag[2])
    sum_b, dif_b = (real[1] + real[3], imag[1] + imag[3]), (real[1] - real[3], imag[1] - imag[3])
    return (
        (sum_a[0] + sum_b[0], sum_a[1] + sum_b[1]),
        (dif_a[0] + dif_b[1], dif_a[1] - dif_b[0]),
        (sum_a[0] - sum_b[0], sum_a[1] - sum_b[1]),
        (dif_a[0] - dif_b[1], dif_a[1] + dif_b[0]),
    )


def eight_point(real, imag):
    even = four_point([real[j] + real[j + 4] for j in range(4)], [imag[j] + imag[j + 4] for j in range(4)])
    dif_real = [real[j] - real[j + 4] for j in range(4)]
    dif_imag = [imag[j] - imag[j + 4] for j in range(4)]
    odd = four_point(
        [
            dif_real[0],
            (dif_real[1] + dif_imag[1]) * half_root,
            dif_imag[2],
            (dif_imag[3] - dif_real[3]) * half_root,
        ],
        [
            dif_imag[0],
            (dif_imag[1] - dif_real[1]) * half_root,
            -dif_real[2],
            (dif_real[3] + dif_imag[3]) * -half_root,
        ],
    )
    return [even[0], odd[0], even[1], odd[1], even[2], odd[2], even[3], odd[3]]


def weights_kernel(rows_ref, density_ref, weights_ref):
    for segment in range(rows_ref.shape[0]):
        rows_here = rows_ref[segment : segment + 1, :]
        density = density_ref[segment]
        high, low = split(jnp.concatenate([density, density], axis=1))
        pieces = jnp.concatenate([high, low], axis=1)
        for block in range(BLOCKS):
            grid_rows = lax.broadcasted_iota(jnp.int32, (SPAN, rows_here.shape[1]), 0) * BLOCKS + block
            chosen = jnp.where(grid_rows == rows_here, 1.0, 0.0).astype(jnp.bfloat16)
            summed = jnp.dot(chosen, pieces, preferred_element_type=jnp.float32)
            weights_ref[segment, pl.ds(block * SPAN, SPAN), :] = (
                summed[:, :LANES] + summed[:, LANES:]
            ) * (1.0 / (TILES * TV))


CHUNK = 16


def normal_kernel(
    dir_ref, maps_ref, weights_ref, twist_ref, row_ref, row_back_ref, col_ref, col_back_ref,
    out_ref, dir_dup, turned, left, left_back, right, back, total,
):
    direction = dir_ref[...]
    rolled = pltpu.roll(direction, TV, 1)
    first_half = lax.broadcasted_iota(jnp.int32, direction.shape, 1) < TV
    dir_dup[0] = jnp.where(first_half, direction, rolled)
    dir_dup[1] = jnp.where(first_half, rolled, direction)
    for segment in range(maps_ref.shape[0]):
        for chunk in range(SPAN // CHUNK):
            at = [pl.ds(block * SPAN + chunk * CHUNK, CHUNK) for block in range(BLOCKS)]
            real, imag = [], []
            for rows in at:
                map_real, map_imag = maps_ref[segment, 0, rows, :], maps_ref[segment, 1, rows, :]
                dir_real, dir_imag = dir_dup[0, rows, :], dir_dup[1, rows, :]
                real.append(map_real * dir_real - map_imag * dir_imag)
                imag.append(map_real * dir_imag + map_imag * dir_real)
            for block, (value_real, value_imag) in enumerate(eight_point(real, imag)):
                if block > 0:
                    twist_real, twist_imag = twist_ref[0, at[block], :], twist_ref[1, at[block], :]
                    value_real, value_imag = (
                        value_real * twist_real - value_imag * twist_imag,
                        value_real * twist_imag + value_imag * twist_real,
                    )
                lanes = pl.ds(block * LANES, LANES)
                for part, value in enumerate((value_real, value_imag)):
                    high, low = split(value)
                    start = part * SPAN + chunk * CHUNK
                    turned[pl.ds(start, CHUNK), lanes] = high
                    turned[pl.ds(2 * SPAN + start, CHUNK), lanes] = high
                    turned[pl.ds(4 * SPAN + start, CHUNK), lanes] = low
        for pair in range(BLOCKS // 2):
            grid = jnp.dot(
                row_ref[...], turned[:, pl.ds(pair * 2 * LANES, 2 * LANES)], preferred_element_type=jnp.float32
            )
            for side in range(2):
                rows = pl.ds((2 * pair + side) * SPAN, SPAN)
                for part in range(2):
                    high, low = split(grid[part * SPAN : (part + 1) * SPAN, side * LANES : (side + 1) * LANES])
                    left[rows, pl.ds(part * LANES, LANES)] = high
                    left[rows, pl.ds((2 + part) * LANES, LANES)] = low
                    left[rows, pl.ds((4 + part) * LANES, LANES)] = high
        for pair in range(BLOCKS // 2):
            rows = pl.ds(pair * 2 * SPAN, 2 * SPAN)
            kspace = jnp.dot(left[rows, :], col_ref[...], preferred_element_type=jnp.float32)
            weights = weights_ref[segment, rows, :]
            high, low = split(kspace * jnp.concatenate([weights, weights], axis=1))
            left_back[rows, pl.ds(0, 2 * LANES)] = high
            left_back[rows, pl.ds(2 * LANES, 2 * LANES)] = low
            left_back[rows, pl.ds(4 * LANES, 2 * LANES)] = high
        for pair in range(BLOCKS // 2):
            rows = pl.ds(pair * 2 * SPAN, 2 * SPAN)
            grid = jnp.dot(left_back[rows, :], col_back_ref[...], preferred_element_type=jnp.float32)
            high, low = split(grid)
            for side in range(2):
                lanes = pl.ds((2 * pair + side) * LANES, LANES)
                for part in range(2):
                    piece = (slice(side * SPAN, (side + 1) * SPAN), slice(part * LANES, (part + 1) * LANES))
                    right[pl.ds(part * SPAN, SPAN), lanes] = high[piece]
                    right[pl.ds((2 + part) * SPAN, SPAN), lanes] = high[piece]
                    right[pl.ds((4 + part) * SPAN, SPAN), lanes] = low[piece]
        for pair in range(BLOCKS // 2):
            lanes = pl.ds(pair * 2 * LANES, 2 * LANES)
            back[:, lanes] = jnp.dot(row_back_ref[...], right[:, lanes], preferred_element_type=jnp.float32)
        for chunk in range(SPAN // CHUNK):
            real, imag = [], []
            for block in range(BLOCKS):
                lanes = pl.ds(block * LANES, LANES)
                value_real = back[pl.ds(chunk * CHUNK, CHUNK), lanes]
                value_imag = back[pl.ds(SPAN + chunk * CHUNK, CHUNK), lanes]
                if block > 0:
                    rows = pl.ds(block * SPAN + chunk * CHUNK, CHUNK)
                    twist_real, twist_imag = twist_ref[0, rows, :], twist_ref[1, rows, :]
                    value_real, value_imag = (
                        value_real * twist_real + value_imag * twist_imag,
                        value_imag * twist_real - value_real * twist_imag,
                    )
                real.append(value_real)
                imag.append(value_imag)
            for block, (value_imag, value_real) in enumerate(eight_point(imag, real)):
                rows = pl.ds(block * SPAN + chunk * CHUNK, CHUNK)
                map_real, map_imag = maps_ref[segment, 0, rows, :], maps_ref[segment, 1, rows, :]
                add_real = map_real * value_real + map_imag * value_imag
                add_imag = map_real * value_imag - map_imag * value_real
                if segment > 0:
                    add_real += total[0, rows, :]
                    add_imag += total[1, rows, :]
                total[0, rows, :] = add_real
                total[1, rows, :] = add_imag
    real, imag = total[0], total[1]
    out_ref[...] = jnp.where(first_half, real + pltpu.roll(real, TV, 1), imag + pltpu.roll(imag, TV, 1))


def in_vmem(count):
    return [pl.BlockSpec(memory_space=pltpu.VMEM)] * count


def sample_weights(sample_rows, density):
    return pl.pallas_call(
        weights_kernel,
        out_shape=jax.ShapeDtypeStruct((sample_rows.shape[0], TILES, LANES), jnp.float32),
        in_specs=in_vmem(2),
        out_specs=pl.BlockSpec(memory_space=pltpu.VMEM),
        compiler_params=pltpu.CompilerParams(vmem_limit_bytes=40 << 20),
        name="sample_weights",
    )(sample_rows, density)


def apply_normal(*operands):
    return pl.pallas_call(
        normal_kernel,
        out_shape=jax.ShapeDtypeStruct((TILES, LANES), jnp.float32),
        in_specs=in_vmem(8),
        out_specs=pl.BlockSpec(memory_space=pltpu.VMEM),
        scratch_shapes=[
            pltpu.VMEM((2, TILES, LANES), jnp.float32),
            pltpu.VMEM((6 * SPAN, BLOCKS * LANES), jnp.bfloat16),
            pltpu.VMEM((TILES, 6 * LANES), jnp.bfloat16),
            pltpu.VMEM((TILES, 6 * LANES), jnp.bfloat16),
            pltpu.VMEM((6 * SPAN, BLOCKS * LANES), jnp.bfloat16),
            pltpu.VMEM((2 * SPAN, BLOCKS * LANES), jnp.float32),
            pltpu.VMEM((2, TILES, LANES), jnp.float32),
        ],
        compiler_params=pltpu.CompilerParams(vmem_limit_bytes=48 << 20),
        name="apply_normal",
    )(*operands)


def coil_maps(sensitivity, field_map, seg_map, first_segment, seg_local):
    sens_real = jnp.concatenate([sensitivity[0, :, :TV], sensitivity[1, :, :TV]], axis=1)
    sens_imag = jnp.concatenate([sensitivity[0, :, TV:], sensitivity[1, :, TV:]], axis=1)
    maps = []
    for local_seg in range(seg_local):
        segment = first_segment + local_seg
        listed = jnp.any(seg_map == segment, axis=1, keepdims=True).astype(jnp.float32)
        angle = field_map * ((segment.astype(jnp.float32) + 0.5) / jnp.float32(SEGS))
        cosine, sine = jnp.cos(angle) * listed, jnp.sin(angle) * listed
        cosine, sine = jnp.concatenate([cosine, cosine], axis=1), jnp.concatenate([sine, sine], axis=1)
        maps.append(jnp.stack([sens_real * cosine + sens_imag * sine, sens_imag * cosine - sens_real * sine]))
    return jnp.stack(maps)


def gather_direction(own_tiles):
    copies = jnp.tile(own_tiles, (DEVICES, 1))
    return lax.all_to_all(copies, AXES, 0, 0, tiled=True)


def sum_to_owners(partial_value):
    parts = lax.all_to_all(partial_value, AXES, 0, 0, tiled=True)
    return jnp.sum(parts.reshape(DEVICES, -1, parts.shape[1]), axis=0)


def shards(
    right_side, sensitivity, field_map, seg_map, sample_rows, density, step_alpha, step_beta
):
    seg_local = sample_rows.shape[0]
    first_segment = lax.axis_index("seg") * seg_local
    row_ahead, row_back, column_ahead, column_back, twist = map(jnp.asarray, transform_constants())
    twist = jnp.broadcast_to(twist, (2, TILES, LANES))
    direction = right_side
    gathered = gather_direction(direction)
    maps = coil_maps(sensitivity, field_map, seg_map, first_segment, seg_local)
    weights = sample_weights(sample_rows, density)
    solution_field = jnp.zeros_like(right_side)
    residual = right_side
    for step in range(ITERS):
        partial_value = apply_normal(
            gathered, maps, weights, twist, row_ahead, row_back, column_ahead, column_back
        )
        image = sum_to_owners(partial_value) + ridge_weight * direction
        solution_field = solution_field + step_alpha[step] * direction
        residual = residual - step_alpha[step] * image
        direction = residual + step_beta[step] * direction
        if step + 1 < ITERS:
            gathered = gather_direction(direction)
    return (solution_field, residual)


def solution(mesh):
    placed = (
        P(AXES, None),
        P("coil", None, None),
        P(),
        P(),
        P("seg", "tile"),
        P("seg", "tile", None),
        P(),
        P(),
    )
    return jax.shard_map(
        shards,
        mesh=mesh,
        in_specs=placed,
        out_specs=(P(AXES, None), P(AXES, None)),
        check_vma=False,
    )
```

time: 476 us -> 155 us (0.33); the launches traced: 467 us -> 154 us
  matrix products: 289 us -> 0 us
  other arithmetic: 43 us -> 14.6 us
  Pallas kernels: 0 us -> 22.7 us
  local copies, waits for them, and re-layouts: 29.3 us -> 11.9 us
    dot_general x96 -> x0, matrix products: 289 us -> none  [the longest x6 37.9 us: segment_normal(): jnp.einsum('mn,cnv->cmv', row_cos, coil_imag, precision=highest)]
    pallas_call x0 -> x3, Pallas kernels: none -> 22.7 us  [the longest x2 20.8 us: apply_normal(): pl.pallas_call(normal_kernel, out_shape=jax.ShapeDtypeStruct((TILES, LANE...]
    scatter-add x6 -> x0, other arithmetic: 16 us -> none  [shards(): partial_value = partial_value.at[local_listed].add(contrib)]
    sort x3 -> x0, other arithmetic: 13.1 us -> none  [tile_list(): sorted_tiles = jnp.argsort(sort_keys)]
    gather x18 -> x0, local copies, waits for them, and re-layouts: 11.8 us -> none  [the longest x6 5.32 us: shards(): gathered[local_listed]]
    concatenate x6 -> x1, other arithmetic: 0.07 us -> 5.95 us  [coil_maps(): jnp.concatenate([cosine, cosine], axis=1)]
    unnamed x189 -> x36, local copies, waits for them, and re-layouts: 12.3 us -> 7.58 us
  transfers between devices with their start and end apart: 2 -> 2, of which waited for: 1 -> 2; matrix products, arithmetic and copies ran while one was open for 6% -> 11% of each run, Pallas kernels for 0% -> 1%
where the time goes in v2:
time: 155 us; the launch traced here: 154 us
  blocking collectives  52.9 us (34%)
  starting transfers between devices  29 us (19%)
  Pallas kernels  22.7 us (15%)
  waiting for transfers between devices  21.9 us (14%)
  other arithmetic  14.6 us (9%)
  local copies, waits for them, and re-layouts  11.9 us (8%)
    all_to_all x1, blocking collectives, gather_direction(): return lax.all_to_all(copies, AXES, 0, 0, tiled=True)  26.5 us
    all_to_all x1, blocking collectives, sum_to_owners(): parts = lax.all_to_all(partial_value, AXES, 0, 0, tiled=True)  26.3 us
    pallas_call x2, Pallas kernels, apply_normal(): pl.pallas_call(normal_kernel, out_shape=jax.ShapeDtypeStruct((TILES, LANE...  20.8 us
    all_to_all x1, waiting for transfers between devices, sum_to_owners(): parts = lax.all_to_all(partial_value, AXES, 0, 0, tiled=True)  19.5 us
    all_to_all x1, starting transfers between devices, gather_direction(): return lax.all_to_all(copies, AXES, 0, 0, tiled=True)  16.7 us
    all_to_all x1, starting transfers between devices, sum_to_owners(): parts = lax.all_to_all(partial_value, AXES, 0, 0, tiled=True)  12.4 us
    unnamed x36, local copies, waits for them, and re-layouts  7.58 us
    concatenate x1, other arithmetic, coil_maps(): jnp.concatenate([cosine, cosine], axis=1)  5.95 us
  transfers between devices with their start and end apart: 2, of which 2 were waited for; matrix products, arithmetic and copies ran while one was open for 11% of the time, Pallas kernels for 1%

profile of v2, /device:TPU:1, one launch (start us, length us, event | category | flops | bytes accessed | tf_op | source)
XLA Modules:
  0.0 153.9 jit_solution(3985647610356464782)
XLA Ops:
  0.6 0.0 copy-start.7
  0.6 1.6 %tile.4 = f32[256,4,128]{2,1,0:T(4,128)} broadcast(f32[4,128]{1,0:T(4,128)} %param.13), dimensions={1,2} | broadcast | bytes 526336 | tf_op jit(solution)/shard_map/tile | solution.py:255
  2.3 16.7 %all-to-all-start = ((f32[256,4,128]{2,1,0:T(4,128)}), f32[256,4,128]{2,1,0:T(4,128)}, u32[]{:S(2)}, u32[]{:S(2)}) async-start(f32[256,4,128]{2,1,0:T(4,128)} %tile.4), calls=%async_computation | async-start | bytes 1048576 | tf_op jit(solution)/shard_map/all_to_all | solution.py:256
  18.9 0.8 compare_reduce_fusion.2
  19.8 1.9 %copy.15 = f32[1024,64]{1,0:T(8,128)} copy(f32[1024,64]{0,1:T(8,128)} %param.15) | data formatting | bytes 524288 | tf_op args[2]
  21.7 0.0 copy-done.7
  21.7 0.0 copy-start.6
  21.7 1.6 %fusion = (f32[1,1024,64]{2,1,0:T(8,128)}, f32[1,1024,64]{2,1,0:T(8,128)}, f32[1,1024,64]{2,1,0:T(8,128)}, f32[1,1024,64]{2,1,0:T(8,128)}) fusion(f32[2,1024,128]{2,1,0:T(8,128)S(1)} %copy-done.7), kind=kLoop, calls=%fused_computation.31 | loop fusion | bytes 2097152 | tf_op jit(solution)/shard_map/slice | solution.py:241
  23.3 1.6 %copy.18.density_ref = f32[3,1024,64]{2,1,0:T(8,128)S(1)} copy(f32[3,1024,64]{1,2,0:T(8,128)} %param.18) | data formatting | bytes 1572864 | tf_op args[5]
  24.9 0.0 copy-done.6
  25.0 0.0 copy-start.8
  25.0 0.0 copy-start.9
  25.0 0.0 copy-start.10
  25.0 0.0 copy-start.11
  25.0 0.0 copy-start.12
  25.0 1.9 %sample_weights.1.weights_ref = f32[3,1024,128]{2,1,0:T(8,128)S(1)} custom-call(s32[3,1024]{1,0:T(4,128)S(1)} %copy-done.6, f32[3,1024,64]{2,1,0:T(8,128)S(1)} %copy.18.density_ref), custom_call_target="tpu_custom_call" | custom-call | tf_op jit(solution)/shard_map/sample_weights/pallas_call | solution.py:210
  26.9 0.0 copy-done.8
  26.9 6.0 %multiply_bitcast_fusion.3 = (f32[1,1024,64]{2,1,0:T(8,128)S(1)}, f32[1,1024,64]{2,1,0:T(8,128)S(1)}, f32[1,1024,64]{2,1,0:T(8,128)S(1)}, f32[1,1024,64]{2,1,0:T...) fusion(f32[1024,64]{1,0:T(8,128)S(1)} %copy-done.8, f32[1024]{0:T(1024)S(1)} %convert_element_type.36, ...), kind=kLoop, calls=%fused_computation.19 | loop fusion | flops 589824 | bytes 1847308 | tf_op jit(solution)/shard_map/concatenate | solution.py:249
  32.9 0.0 copy-done.9
  32.9 0.0 copy-done.10
  32.9 0.0 copy-done.11
  32.9 0.0 copy-done.12
  32.9 0.6 multiply_add_fusion.2
  33.5 0.4 multiply_add_fusion.1
  33.9 0.1 maximum_bitcast_fusion.1
  34.1 0.6 multiply_add_fusion
  34.7 0.1 maximum_bitcast_fusion
  34.8 0.0 copy-start.14
  34.9 0.0 copy-start
  34.9 0.0 copy-start.1
  34.9 1.9 %pad_maximum_fusion.maps_ref = f32[3,2,1024,128]{3,2,1,0:T(8,128)} fusion(f32[1,2,1024,128]{3,2,1,0:T(8,128)S(1)} %get-tuple-element.32, f32[1,2,1024,128]{3,2,1,0:T(8,128)S(1)} %maximum_bitcast_fusion.1, f32[1,2,1024,128]{3,2,1,0:T(8,128)S(1)} %get-tuple-element.31), kind=kLoop, calls=%fused_computation | loop fusion | flops 1572864 | bytes 6291456 | tf_op jit(solution)/shard_map/stack | solution.py:251
  36.8 2.3 %all-to-all-done = f32[256,4,128]{2,1,0:T(4,128)} async-done(((f32[256,4,128]{2,1,0:T(4,128)}), f32[256,4,128]{2,1,0:T(4,128)}, u32[]{:S(2)}, u32[]{:S(2)}) %all-to-all-start) | async-done | bytes 524320 | tf_op jit(solution)/shard_map/all_to_all | solution.py:256
  39.1 0.0 copy-done.14
  39.1 0.3 broadcast_in_dim.5.twist_ref
  39.5 0.0 copy-done
  39.5 0.0 copy-done.1
  39.5 0.0 copy-start.2
  39.5 1.0 copy-done.2
  40.5 0.0 copy-start.4
  40.5 1.0 copy-done.4
  41.5 0.0 copy-start.16
  41.5 0.0 copy-start.13
  41.5 0.0 copy-start.15
  41.5 10.9 %apply_normal.2 = f32[1024,128]{1,0:T(8,128)} custom-call(f32[1024,128]{1,0:T(8,128)} %bitcast.2.dir_ref, f32[3,2,1024,128]{3,2,1,0:T(8,128)} %pad_maximum_fusion.maps_ref, f32[3,1024,128]{2,1,0:T(8,128)S(1)} %sample_weights.1.weights_ref, f32[2,1024,128]{2,1,0:T(8,128)S(1)} %broadcast_in_dim.5.twist_ref, bf16[256,768]{1,0:T(8,128)(2,1)S(1)} %copy-done, ...), custom_call_target="tpu_custom_call" | custom-call | tf_op jit(solution)/shard_map/apply_normal/pallas_call | solution.py:221
  52.4 12.4 %all-to-all-start.1 = ((f32[256,4,128]{2,1,0:T(4,128)}), f32[256,4,128]{2,1,0:T(4,128)}, u32[]{:S(2)}, u32[]{:S(2)}) async-start(f32[256,4,128]{2,1,0:T(4,128)} %bitcast.12), calls=%async_computation.1 | async-start | bytes 1048576 | tf_op jit(solution)/shard_map/all_to_all | solution.py:260
  64.8 0.0 copy-done.16
  64.8 0.7 fusion.1
  65.5 19.5 %all-to-all-done.1 = f32[256,4,128]{2,1,0:T(4,128)} async-done(((f32[256,4,128]{2,1,0:T(4,128)}), f32[256,4,128]{2,1,0:T(4,128)}, u32[]{:S(2)}, u32[]{:S(2)}) %all-to-all-start.1) | async-done | bytes 524320 | tf_op jit(solution)/shard_map/all_to_all | solution.py:260
  85.0 1.3 reduce_sum.18
  86.3 0.0 copy-done.13
  86.3 0.0 copy-done.15
  86.3 0.6 multiply_add_fusion.4
  86.9 0.1 tile.5
  87.0 26.5 %all_to_all.34 = f32[256,4,128]{2,1,0:T(4,128)S(1)} all-to-all(f32[256,4,128]{2,1,0:T(4,128)S(1)} %tile.5), channel_id=1, replica_groups=mesh['seg'=8,'coil'=16,'tile'=2] {'seg','coil','tile'}, dimensions={0} | all-to-all | bytes 1048576 | tf_op jit(solution)/shard_map/all_to_all | solution.py:256
  113.6 0.0 copy-start.3
  113.6 1.0 copy-done.3
  114.6 0.0 copy-start.5
  114.6 1.0 copy-done.5
  115.6 9.9 %apply_normal.3 = f32[1024,128]{1,0:T(8,128)S(1)} custom-call(f32[1024,128]{1,0:T(8,128)S(1)} %bitcast.26, f32[3,2,1024,128]{3,2,1,0:T(8,128)} %pad_maximum_fusion.maps_ref, f32[3,1024,128]{2,1,0:T(8,128)S(1)} %sample_weights.1.weights_ref, f32[2,1024,128]{2,1,0:T(8,128)S(1)} %broadcast_in_dim.5.twist_ref, bf16[256,768]{1,0:T(8,128)(2,1)S(1)} %copy-done, ...), custom_call_target="tpu_custom_call" | custom-call | tf_op jit(solution)/shard_map/apply_normal/pallas_call | solution.py:221
  125.5 26.3 %all_to_all.35 = f32[256,4,128]{2,1,0:T(4,128)S(1)} all-to-all(f32[256,4,128]{2,1,0:T(4,128)S(1)} %bitcast.27), channel_id=1, replica_groups=mesh['seg'=8,'coil'=16,'tile'=2] {'seg','coil','tile'}, dimensions={0} | all-to-all | bytes 1048576 | tf_op jit(solution)/shard_map/all_to_all | solution.py:260
  151.8 0.3 reduce_sum.19
  152.1 1.9 %multiply_subtract_fusion.3 = (f32[4,128]{1,0:T(4,128)}, f32[4,128]{1,0:T(4,128)}) fusion(f32[4,128]{1,0:T(4,128)S(1)} %reduce_sum.19, f32[4,128]{1,0:T(4,128)S(1)} %copy-done.13, f32[4,128]{1,0:T(4,128)S(1)} %reduce_sum.18, f32[]{:T(128)} %bitcast.1, f32[]{:T(128)} %bitcast, f32[]{:T(128)S(1)} %bitcast.29), kind=kLoop, calls=%fused_computation.27 | loop fusion | flops 6656 | bytes 10252 | tf_op jit(solution)/shard_map/sub | solution.py:283
  (3 shorter events, 0.0 us)
Async XLA Ops:
  0.6 21.1 %copy-start.7 = (f32[2,1024,128]{2,1,0:T(8,128)S(1)}, f32[2,1024,128]{2,1,0:T(8,128)}, u32[]{:S(2)}) copy-start(f32[2,1024,128]{2,1,0:T(8,128)} %param.14) | copy-start | bytes 3145732
  2.3 36.9 %all-to-all-start = ((f32[256,4,128]{2,1,0:T(4,128)}), f32[256,4,128]{2,1,0:T(4,128)}, u32[]{:S(2)}, u32[]{:S(2)}) async-start(f32[256,4,128]{2,1,0:T(4,128)} %tile.4), calls=%async_computation | async-start | bytes 1048576 | tf_op jit(solution)/shard_map/all_to_all | solution.py:256
  21.7 3.2 %copy-start.6 = (s32[3,1024]{1,0:T(4,128)S(1)}, s32[3,1024]{1,0:T(4,128)}, u32[]{:S(2)}) copy-start(s32[3,1024]{1,0:T(4,128)} %rows_ref.1) | copy-start | bytes 36868
  25.0 2.0 %copy-start.8 = (f32[1024,64]{1,0:T(8,128)S(1)}, f32[1024,64]{1,0:T(8,128)}, u32[]{:S(2)}) copy-start(f32[1024,64]{1,0:T(8,128)} %copy.15) | copy-start | bytes 786436
  25.0 7.9 %copy-start.9 = (f32[1,1024,64]{2,1,0:T(8,128)S(1)}, f32[1,1024,64]{2,1,0:T(8,128)}, u32[]{:S(2)}) copy-start(f32[1,1024,64]{2,1,0:T(8,128)} %get-tuple-element.13) | copy-start | bytes 786436
  25.0 7.9 %copy-start.10 = (f32[1,1024,64]{2,1,0:T(8,128)S(1)}, f32[1,1024,64]{2,1,0:T(8,128)}, u32[]{:S(2)}) copy-start(f32[1,1024,64]{2,1,0:T(8,128)} %get-tuple-element.14) | copy-start | bytes 786436
  25.0 7.9 %copy-start.11 = (f32[1,1024,64]{2,1,0:T(8,128)S(1)}, f32[1,1024,64]{2,1,0:T(8,128)}, u32[]{:S(2)}) copy-start(f32[1,1024,64]{2,1,0:T(8,128)} %get-tuple-element.15) | copy-start | bytes 786436
  25.0 7.9 %copy-start.12 = (f32[1,1024,64]{2,1,0:T(8,128)S(1)}, f32[1,1024,64]{2,1,0:T(8,128)}, u32[]{:S(2)}) copy-start(f32[1,1024,64]{2,1,0:T(8,128)} %get-tuple-element.16) | copy-start | bytes 786436
  34.8 4.3 %copy-start.14 = (f32[2,1024]{1,0:T(2,128)S(1)}, f32[2,1024]{1,0:T(2,128)}, u32[]{:S(2)}) copy-start(f32[2,1024]{1,0:T(2,128)} %constant.44) | copy-start | bytes 24580
  34.9 4.6 %copy-start = (bf16[256,768]{1,0:T(8,128)(2,1)S(1)}, bf16[256,768]{1,0:T(8,128)(2,1)}, u32[]{:S(2)}) copy-start(bf16[256,768]{1,0:T(8,128)(2,1)} %constant.35.clone.row_ref) | copy-start | bytes 1179652
  34.9 4.6 %copy-start.1 = (bf16[256,768]{1,0:T(8,128)(2,1)S(1)}, bf16[256,768]{1,0:T(8,128)(2,1)}, u32[]{:S(2)}) copy-start(bf16[256,768]{1,0:T(8,128)(2,1)} %constant.36.clone.row_back_ref) | copy-start | bytes 1179652
  39.5 1.0 copy-start.2
  40.5 1.0 copy-start.4
  41.5 23.3 %copy-start.16 = (f32[2]{0:T(128)S(1)}, f32[2]{0:T(128)}, u32[]{:S(2)}) copy-start(f32[2]{0:T(128)} %param.19) | copy-start | bytes 28
  41.5 44.8 %copy-start.13 = (f32[4,128]{1,0:T(4,128)S(1)}, f32[4,128]{1,0:T(4,128)}, u32[]{:S(2)}) copy-start(f32[4,128]{1,0:T(4,128)} %param.13) | copy-start | bytes 6148
  41.5 44.8 %copy-start.15 = (f32[2]{0:T(128)S(1)}, f32[2]{0:T(128)}, u32[]{:S(2)}) copy-start(f32[2]{0:T(128)} %param.20) | copy-start | bytes 28
  52.4 32.6 %all-to-all-start.1 = ((f32[256,4,128]{2,1,0:T(4,128)}), f32[256,4,128]{2,1,0:T(4,128)}, u32[]{:S(2)}, u32[]{:S(2)}) async-start(f32[256,4,128]{2,1,0:T(4,128)} %bitcast.12), calls=%async_computation.1 | async-start | bytes 1048576 | tf_op jit(solution)/shard_map/all_to_all | solution.py:260
  113.6 1.0 copy-start.3
  114.6 1.0 copy-start.5

commit v3 on v2

--- a/solution.py
+++ b/solution.py
@@ -1,3 +1,4 @@
+import functools
 import math
 
 import jax
@@ -11,13 +12,12 @@
 
 SEGS = 24
 TV = 64
-ITERS = 2
 DEVICES = 256
 TILES = 1024
 BLOCKS = 8
 SPAN = TILES // BLOCKS
 LANES = 2 * TV
-AXES = ("seg", "coil", "tile")
+SAME_CORE = ("y", "x", "z_lo", "z_hi")
 
 ridge_weight = 0.25
 half_root = math.sqrt(0.5)
@@ -90,17 +90,57 @@
     return [even[0], odd[0], even[1], odd[1], even[2], odd[2], even[3], odd[3]]
 
 
-def weights_kernel(rows_ref, density_ref, weights_ref):
-    for segment in range(rows_ref.shape[0]):
-        rows_here = rows_ref[segment : segment + 1, :]
-        density = density_ref[segment]
+def cosine_sine(angle):
+    turns = jnp.round(angle * (2.0 / math.pi))
+    rest = angle - turns * 1.5703125
+    rest = rest - turns * 4.837512969970703e-4
+    rest = rest - turns * 7.549789948768648e-8
+    square = rest * rest
+    sine = rest + rest * square * (
+        -1.6666654611e-1 + square * (8.3321608736e-3 + square * -1.9515295891e-4)
+    )
+    cosine = 1.0 - 0.5 * square + square * square * (
+        4.166664568298827e-2 + square * (-1.388731625493765e-3 + square * 2.443315711809948e-5)
+    )
+    quarter = turns.astype(jnp.int32)
+    swapped = (quarter & 1) == 1
+    flip_cosine = ((quarter + 1) & 2) == 2
+    flip_sine = (quarter & 2) == 2
+    cosine, sine = jnp.where(swapped, sine, cosine), jnp.where(swapped, cosine, sine)
+    return jnp.where(flip_cosine, -cosine, cosine), jnp.where(flip_sine, -sine, sine)
+
+
+def prepare_kernel(
+    first_ref, sens_ref, field_ref, seg_map_ref, rows_ref, density_ref, maps_ref, weights_ref
+):
+    seg_local = rows_ref.shape[0]
+    for block in range(BLOCKS):
+        at = pl.ds(block * SPAN, SPAN)
+        field = field_ref[at, :]
+        field = jnp.concatenate([field, field], axis=1)
+        named = seg_map_ref[at, :]
+        sens = [sens_ref[coil, at, :] for coil in range(2)]
+        sens_real = jnp.concatenate([sens[0][:, :TV], sens[1][:, :TV]], axis=1)
+        sens_imag = jnp.concatenate([sens[0][:, TV:], sens[1][:, TV:]], axis=1)
+        for local_seg in range(seg_local):
+            segment = first_ref[0] + local_seg
+            member = jnp.where(named == segment, 1.0, 0.0)
+            listed = jnp.where(jnp.sum(member, axis=1, keepdims=True) > 0.0, 1.0, 0.0)
+            seg_time = (segment.astype(jnp.float32) + 0.5) / SEGS
+            cosine, sine = cosine_sine(field * seg_time)
+            cosine, sine = cosine * listed, sine * listed
+            maps_ref[local_seg, 0, at, :] = sens_real * cosine + sens_imag * sine
+            maps_ref[local_seg, 1, at, :] = sens_imag * cosine - sens_real * sine
+    for local_seg in range(seg_local):
+        rows_here = rows_ref[local_seg : local_seg + 1, :]
+        density = density_ref[local_seg]
         high, low = split(jnp.concatenate([density, density], axis=1))
         pieces = jnp.concatenate([high, low], axis=1)
         for block in range(BLOCKS):
             grid_rows = lax.broadcasted_iota(jnp.int32, (SPAN, rows_here.shape[1]), 0) * BLOCKS + block
             chosen = jnp.where(grid_rows == rows_here, 1.0, 0.0).astype(jnp.bfloat16)
             summed = jnp.dot(chosen, pieces, preferred_element_type=jnp.float32)
-            weights_ref[segment, pl.ds(block * SPAN, SPAN), :] = (
+            weights_ref[local_seg, pl.ds(block * SPAN, SPAN), :] = (
                 summed[:, :LANES] + summed[:, LANES:]
             ) * (1.0 / (TILES * TV))
 
@@ -108,15 +148,28 @@
 CHUNK = 16
 
 
-def normal_kernel(
-    dir_ref, maps_ref, weights_ref, twist_ref, row_ref, row_back_ref, col_ref, col_back_ref,
-    out_ref, dir_dup, turned, left, left_back, right, back, total,
-):
-    direction = dir_ref[...]
-    rolled = pltpu.roll(direction, TV, 1)
-    first_half = lax.broadcasted_iota(jnp.int32, direction.shape, 1) < TV
-    dir_dup[0] = jnp.where(first_half, direction, rolled)
-    dir_dup[1] = jnp.where(first_half, rolled, direction)
+def normal_kernel(further, core_ref, *refs):
+    if further:
+        alpha_ref, beta_ref, mine_ref, other_ref, mine_sum_ref, other_sum_ref = refs[:6]
+        refs = refs[6:]
+    else:
+        mine_ref, other_ref = refs[:2]
+        refs = refs[2:]
+    maps_ref, weights_ref, twist_ref, row_ref, row_back_ref, col_ref, col_back_ref = refs[:7]
+    keep_ref, send_ref, dir_dup, turned, left, left_back, right, back, total = refs[7:]
+    core = core_ref[0]
+    first_half = lax.broadcasted_iota(jnp.int32, (SPAN, LANES), 1) < TV
+    for pair in range(BLOCKS // 2):
+        for whose in range(2):
+            from_rows = pl.ds(pair * SPAN, SPAN)
+            to_rows = pl.ds((2 * pair + (core if whose == 0 else 1 - core)) * SPAN, SPAN)
+            direction = (mine_ref, other_ref)[whose][from_rows, :]
+            if further:
+                image = (mine_sum_ref, other_sum_ref)[whose][from_rows, :] + ridge_weight * direction
+                direction = direction - alpha_ref[0] * image + beta_ref[0] * direction
+            rolled = pltpu.roll(direction, TV, 1)
+            dir_dup[0, to_rows, :] = jnp.where(first_half, direction, rolled)
+            dir_dup[1, to_rows, :] = jnp.where(first_half, rolled, direction)
     for segment in range(maps_ref.shape[0]):
         for chunk in range(SPAN // CHUNK):
             at = [pl.ds(block * SPAN + chunk * CHUNK, CHUNK) for block in range(BLOCKS)]
@@ -198,31 +251,41 @@
                     add_imag += total[1, rows, :]
                 total[0, rows, :] = add_real
                 total[1, rows, :] = add_imag
-    real, imag = total[0], total[1]
-    out_ref[...] = jnp.where(first_half, real + pltpu.roll(real, TV, 1), imag + pltpu.roll(imag, TV, 1))
-
-
-def in_vmem(count):
-    return [pl.BlockSpec(memory_space=pltpu.VMEM)] * count
-
-
-def sample_weights(sample_rows, density):
+    for pair in range(BLOCKS // 2):
+        for whose, out_ref in enumerate((keep_ref, send_ref)):
+            rows = pl.ds((2 * pair + (core if whose == 0 else 1 - core)) * SPAN, SPAN)
+            real, imag = total[0, rows, :], total[1, rows, :]
+            out_ref[pl.ds(pair * SPAN, SPAN), :] = jnp.where(
+                first_half, real + pltpu.roll(real, TV, 1), imag + pltpu.roll(imag, TV, 1)
+            )
+
+
+def specs(scalars, arrays):
+    return [pl.BlockSpec(memory_space=pltpu.SMEM)] * scalars + [pl.BlockSpec(memory_space=pltpu.VMEM)] * arrays
+
+
+def prepare(first_segment, sensitivity, field_map, seg_map, sample_rows, density):
+    seg_local = sample_rows.shape[0]
     return pl.pallas_call(
-        weights_kernel,
-        out_shape=jax.ShapeDtypeStruct((sample_rows.shape[0], TILES, LANES), jnp.float32),
-        in_specs=in_vmem(2),
-        out_specs=pl.BlockSpec(memory_space=pltpu.VMEM),
-        compiler_params=pltpu.CompilerParams(vmem_limit_bytes=40 << 20),
-        name="sample_weights",
-    )(sample_rows, density)
-
-
-def apply_normal(*operands):
+        prepare_kernel,
+        out_shape=(
+            jax.ShapeDtypeStruct((seg_local, 2, TILES, LANES), jnp.float32),
+            jax.ShapeDtypeStruct((seg_local, TILES, LANES), jnp.float32),
+        ),
+        in_specs=specs(1, 5),
+        out_specs=tuple(specs(0, 2)),
+        compiler_params=pltpu.CompilerParams(vmem_limit_bytes=16 << 20),
+        name="maps_and_weights",
+    )(first_segment, sensitivity, field_map, seg_map, sample_rows, density)
+
+
+def apply_normal(core, steps, directions, tables):
+    half = jax.ShapeDtypeStruct((TILES // 2, LANES), jnp.float32)
     return pl.pallas_call(
-        normal_kernel,
-        out_shape=jax.ShapeDtypeStruct((TILES, LANES), jnp.float32),
-        in_specs=in_vmem(8),
-        out_specs=pl.BlockSpec(memory_space=pltpu.VMEM),
+        functools.partial(normal_kernel, len(steps) > 0),
+        out_shape=(half, half),
+        in_specs=specs(1 + len(steps), len(directions) + len(tables)),
+        out_specs=tuple(specs(0, 2)),
         scratch_shapes=[
             pltpu.VMEM((2, TILES, LANES), jnp.float32),
             pltpu.VMEM((6 * SPAN, BLOCKS * LANES), jnp.bfloat16),
@@ -232,76 +295,85 @@
             pltpu.VMEM((2 * SPAN, BLOCKS * LANES), jnp.float32),
             pltpu.VMEM((2, TILES, LANES), jnp.float32),
         ],
-        compiler_params=pltpu.CompilerParams(vmem_limit_bytes=48 << 20),
+        compiler_params=pltpu.CompilerParams(vmem_limit_bytes=20 << 20),
         name="apply_normal",
-    )(*operands)
-
-
-def coil_maps(sensitivity, field_map, seg_map, first_segment, seg_local):
-    sens_real = jnp.concatenate([sensitivity[0, :, :TV], sensitivity[1, :, :TV]], axis=1)
-    sens_imag = jnp.concatenate([sensitivity[0, :, TV:], sensitivity[1, :, TV:]], axis=1)
-    maps = []
-    for local_seg in range(seg_local):
-        segment = first_segment + local_seg
-        listed = jnp.any(seg_map == segment, axis=1, keepdims=True).astype(jnp.float32)
-        angle = field_map * ((segment.astype(jnp.float32) + 0.5) / jnp.float32(SEGS))
-        cosine, sine = jnp.cos(angle) * listed, jnp.sin(angle) * listed
-        cosine, sine = jnp.concatenate([cosine, cosine], axis=1), jnp.concatenate([sine, sine], axis=1)
-        maps.append(jnp.stack([sens_real * cosine + sens_imag * sine, sens_imag * cosine - sens_real * sine]))
-    return jnp.stack(maps)
+    )(core, *steps, *directions, *tables)
+
+
+def swap_cores(value):
+    return lax.ppermute(value, "core", [(0, 1), (1, 0)])
+
+
+def exchange(value, axes):
+    return lax.all_to_all(value, axes, 0, 0, tiled=True)
+
+
+def summed(parts, count):
+    return jnp.sum(parts.reshape(count, -1, LANES), axis=0)
 
 
 def gather_direction(own_tiles):
-    copies = jnp.tile(own_tiles, (DEVICES, 1))
-    return lax.all_to_all(copies, AXES, 0, 0, tiled=True)
-
-
-def sum_to_owners(partial_value):
-    parts = lax.all_to_all(partial_value, AXES, 0, 0, tiled=True)
-    return jnp.sum(parts.reshape(DEVICES, -1, parts.shape[1]), axis=0)
+    mine = exchange(jnp.tile(own_tiles, (DEVICES // 2, 1)), SAME_CORE)
+    return mine, swap_cores(mine)
+
+
+def sum_to_owners(keep, send):
+    return summed(exchange(keep + swap_cores(send), SAME_CORE), DEVICES // 2)
+
+
+def sum_for_all(keep, send):
+    share = summed(exchange(keep + swap_cores(send), ("y", "x")), 16)
+    share = summed(exchange(jnp.tile(share, (8, 1)), ("z_lo", "z_hi")), 8)
+    mine = exchange(jnp.tile(share, (16, 1)), ("y", "x"))
+    return mine, swap_cores(mine)
 
 
 def shards(
     right_side, sensitivity, field_map, seg_map, sample_rows, density, step_alpha, step_beta
 ):
     seg_local = sample_rows.shape[0]
-    first_segment = lax.axis_index("seg") * seg_local
+    first_segment = lax.axis_index(("y", "core")) * seg_local
+    core = lax.axis_index("core").reshape(1)
     row_ahead, row_back, column_ahead, column_back, twist = map(jnp.asarray, transform_constants())
     twist = jnp.broadcast_to(twist, (2, TILES, LANES))
-    direction = right_side
-    gathered = gather_direction(direction)
-    maps = coil_maps(sensitivity, field_map, seg_map, first_segment, seg_local)
-    weights = sample_weights(sample_rows, density)
-    solution_field = jnp.zeros_like(right_side)
-    residual = right_side
-    for step in range(ITERS):
-        partial_value = apply_normal(
-            gathered, maps, weights, twist, row_ahead, row_back, column_ahead, column_back
-        )
-        image = sum_to_owners(partial_value) + ridge_weight * direction
-        solution_field = solution_field + step_alpha[step] * direction
-        residual = residual - step_alpha[step] * image
-        direction = residual + step_beta[step] * direction
-        if step + 1 < ITERS:
-            gathered = gather_direction(direction)
+    gathered = gather_direction(right_side)
+    maps, weights = prepare(
+        first_segment.reshape(1), sensitivity, field_map, seg_map, sample_rows, density
+    )
+    tables = (maps, weights, twist, row_ahead, row_back, column_ahead, column_back)
+    sums = sum_for_all(*apply_normal(core, (), gathered, tables))
+    own_tiles = right_side.shape[0]
+    own_start = lax.axis_index(SAME_CORE) * own_tiles
+    own_sum = lax.dynamic_slice_in_dim(sums[0], own_start, own_tiles, 0)
+    solution_field = step_alpha[0] * right_side
+    residual = right_side - step_alpha[0] * (own_sum + ridge_weight * right_side)
+    direction = residual + step_beta[0] * right_side
+    last_sum = sum_to_owners(
+        *apply_normal(core, (step_alpha, step_beta), (*gathered, *sums), tables)
+    )
+    solution_field = solution_field + step_alpha[1] * direction
+    residual = residual - step_alpha[1] * (last_sum + ridge_weight * direction)
     return (solution_field, residual)
 
 
 def solution(mesh):
+    axes = ("y", "core", "x", "z_lo", "z_hi")
+    fine_mesh = jax.sharding.Mesh(mesh.devices.reshape(4, 2, 4, 4, 2), axes)
+    seg, coil, tile = ("y", "core"), ("x", "z_lo"), "z_hi"
     placed = (
-        P(AXES, None),
-        P("coil", None, None),
+        P(axes, None),
+        P(coil, None, None),
         P(),
         P(),
-        P("seg", "tile"),
-        P("seg", "tile", None),
+        P(seg, tile),
+        P(seg, tile, None),
         P(),
         P(),
     )
     return jax.shard_map(
         shards,
-        mesh=mesh,
+        mesh=fine_mesh,
         in_specs=placed,
-        out_specs=(P(AXES, None), P(AXES, None)),
+        out_specs=(P(axes, None), P(axes, None)),
         check_vma=False,
     )

time: 155 us -> 139 us (0.90)
  starting transfers between devices: 29 us -> 13.1 us
  other arithmetic: 14.6 us -> 5.03 us
  blocking collectives: 52.9 us -> 60.3 us
  local copies, waits for them, and re-layouts: 11.9 us -> 18.7 us
  waiting for transfers between devices: 21.9 us -> 16.7 us
    all_to_all x2 -> x1, starting transfers between devices: 29 us -> 6.18 us  [exchange(): return lax.all_to_all(value, axes, 0, 0, tiled=True)]
    all_to_all x2 -> x1, waiting for transfers between devices: 21.9 us -> 12.8 us  [exchange(): return lax.all_to_all(value, axes, 0, 0, tiled=True)]
    unnamed x36 -> x51, local copies, waits for them, and re-layouts: 7.58 us -> 16.2 us
    all_to_all x2 -> x4, blocking collectives: 52.9 us -> 60.3 us  [exchange(): return lax.all_to_all(value, axes, 0, 0, tiled=True)]
    ppermute x0 -> x4, starting transfers between devices: none -> 6.96 us  [swap_cores(): return lax.ppermute(value, 'core', [(0, 1), (1, 0)])]
    concatenate x1 -> x0, other arithmetic: 5.95 us -> none  [coil_maps(): jnp.concatenate([cosine, cosine], axis=1)]
    ppermute x0 -> x4, waiting for transfers between devices: none -> 3.85 us  [swap_cores(): return lax.ppermute(value, 'core', [(0, 1), (1, 0)])]
    another operation x3 -> x0, other arithmetic: 2.22 us -> none  [coil_maps(): return jnp.stack(maps)]
  transfers between devices with their start and end apart: 2 -> 5, of which waited for: 2 -> 4; matrix products, arithmetic and copies ran while one was open for 11% -> 4% of each run, Pallas kernels for 1% -> 3%
where the time goes in v3:
time: 139 us; the launch traced here: 138 us
  blocking collectives  60.3 us (43%)
  Pallas kernels  23.5 us (17%)
  local copies, waits for them, and re-layouts  18.7 us (13%)
  waiting for transfers between devices  16.7 us (12%)
  starting transfers between devices  13.1 us (9%)
  other arithmetic  5.03 us (4%)
    all_to_all x4, blocking collectives, exchange(): return lax.all_to_all(value, axes, 0, 0, tiled=True)  60.3 us
    pallas_call x2, Pallas kernels, apply_normal(): pl.pallas_call(functools.partial(normal_kernel, len(steps) > 0), out_shap...  19 us
    unnamed x51, local copies, waits for them, and re-layouts  16.2 us
    all_to_all x1, waiting for transfers between devices, exchange(): return lax.all_to_all(value, axes, 0, 0, tiled=True)  12.8 us
    ppermute x4, starting transfers between devices, swap_cores(): return lax.ppermute(value, 'core', [(0, 1), (1, 0)])  6.96 us
    all_to_all x1, starting transfers between devices, exchange(): return lax.all_to_all(value, axes, 0, 0, tiled=True)  6.18 us
    pallas_call x1, Pallas kernels, prepare(): pl.pallas_call(prepare_kernel, out_shape=(jax.ShapeDtypeStruct((seg_local...  4.47 us
    ppermute x4, waiting for transfers between devices, swap_cores(): return lax.ppermute(value, 'core', [(0, 1), (1, 0)])  3.85 us
  transfers between devices with their start and end apart: 5, of which 4 were waited for; matrix products, arithmetic and copies ran while one was open for 4% of the time, Pallas kernels for 3%

profile of v3, /device:TPU:1, one launch (start us, length us, event | category | flops | bytes accessed | tf_op | source)
XLA Modules:
  0.0 138.2 jit_solution(9143491889963975181)
XLA Ops:
  0.6 0.0 copy-start.20
  0.6 0.8 tile.6
  1.4 29.1 %all_to_all.40 = f32[128,4,128]{2,1,0:T(4,128)S(1)} all-to-all(f32[128,4,128]{2,1,0:T(4,128)S(1)} %tile.6), channel_id=1, replica_groups=mesh['y'=4,'core'=2,'x'=4,'z_lo'=4,'z_hi'=2] {'y','x','z_lo','z_hi'}, dimensions={0} | all-to-all | bytes 524288 | tf_op jit(solution)/shard_map/all_to_all | solution.py:308
  30.5 2.8 %collective-permute-start = (f32[512,128]{1,0:T(8,128)S(1)}, f32[512,128]{1,0:T(8,128)}, u32[]{:S(2)}, u32[]{:S(2)}) collective-permute-start(f32[512,128]{1,0:T(8,128)S(1)} %bitcast.10), channel_id=1, source_target_pairs={{0,32},{32,0},{1,33},{33,1},{2,34},{34,2},{3,35},{35,3},{4,36},{36... | collective-permute-start | bytes 786440 | tf_op jit(solution)/shard_map/ppermute | solution.py:304
  33.3 0.0 copy-start.21
  33.3 0.0 copy-start.17
  33.3 2.8 %copy.20.density_ref = f32[3,1024,64]{2,1,0:T(8,128)} copy(f32[3,1024,64]{1,2,0:T(8,128)} %param.18) | data formatting | bytes 1572864 | tf_op args[5]
  36.1 0.0 copy-done.20
  36.1 1.0 copy.18.field_ref
  37.1 0.0 copy-done.21
  37.1 1.0 copy.19.seg_map_ref
  38.1 0.0 copy-done.17
  38.1 0.0 copy-start.2
  38.1 1.4 %copy-done.2 = f32[3,1024,64]{2,1,0:T(8,128)S(1)} copy-done((f32[3,1024,64]{2,1,0:T(8,128)S(1)}, f32[3,1024,64]{2,1,0:T(8,128)}, u32[]{:S(2)}) %copy-start.2) | copy-done | bytes 786456
  39.5 0.0 copy-start.5
  39.5 1.0 copy-done.5
  40.6 0.0 copy-start.6
  40.6 1.0 copy-done.6
  41.6 1.2 copy-done.16
  42.8 0.0 copy-start.13
  42.9 4.5 %maps_and_weights.1 = (f32[3,2,1024,128]{3,2,1,0:T(8,128)S(1)}, f32[3,1024,128]{2,1,0:T(8,128)S(1)}) custom-call(s32[1]{0:T(128)} %bitcast.4.first_ref, f32[2,1024,128]{2,1,0:T(8,128)S(1)} %copy-done.16, f32[1024,64]{1,0:T(8,128)S(1)} %copy-done.5, s32[1024,4]{1,0:T(8,128)S(1)} %copy-done.6, s32[3,1024]{1,0:T(4,128)S(1)} %copy-done.17, ...), custom_call_target="tpu_custom_call" | custom-call | tf_op jit(solution)/shard_map/maps_and_weights/pallas_call | solution.py:269
  47.3 0.0 collective-permute-done.refs_1_.refs_3_
  47.3 0.0 copy-done.22
  47.3 0.3 broadcast_in_dim.8.refs_4_.refs_8_
  47.7 0.0 copy-done.7
  47.7 0.0 copy-done.9
  47.7 0.0 copy-done.11
  47.7 0.0 copy-done.13
  47.7 0.0 copy-start
  47.7 9.7 %apply_normal.2 = (f32[512,128]{1,0:T(8,128)S(1)}, f32[512,128]{1,0:T(8,128)S(1)}) custom-call(s32[1]{0:T(128)} %bitcast.2.core_ref, f32[512,128]{1,0:T(8,128)S(1)} %bitcast.11, f32[512,128]{1,0:T(8,128)} %collective-permute-done.refs_1_.refs_3_, f32[3,2,1024,128]{3,2,1,0:T(8,128)S(1)} %get-tuple-element.8.refs_2_.refs_6_, ...), custom_call_target="tpu_custom_call" | custom-call | tf_op jit(solution)/shard_map/apply_normal/pallas_call | solution.py:284
  57.4 0.0 copy-done.3
  57.4 0.0 copy-done
  57.4 0.0 copy-start.18
  57.4 0.0 copy-start.19
  57.5 0.1 collective-permute-start.1
  57.6 1.5 %collective-permute-done.1 = f32[512,128]{1,0:T(8,128)S(1)} collective-permute-done((f32[512,128]{1,0:T(8,128)S(1)}, f32[512,128]{1,0:T(8,128)S(1)}, u32[]{:S(2)}, u32[]{:S(2)}) %collective-permute-start.1) | collective-permute-done | bytes 262176 | tf_op jit(solution)/shard_map/ppermute | solution.py:304
  59.1 11.8 %all_to_all.41 = f32[16,32,128]{2,1,0:T(8,128)} all-to-all(f32[16,32,128]{2,1,0:T(8,128)S(1)} %bitcast.17), channel_id=1, replica_groups=mesh['y'=4,'core'=2,'x'=4,'z_lo'=4,'z_hi'=2] {'y','x'}, dimensions={0} | all-to-all | bytes 524288 | tf_op jit(solution)/shard_map/all_to_all | solution.py:308
  70.9 1.0 reduce_sum.27
  71.9 9.2 %all_to_all.42 = f32[8,32,128]{2,1,0:T(8,128)S(1)} all-to-all(f32[8,32,128]{2,1,0:T(8,128)S(1)} %tile.7), channel_id=1, replica_groups=mesh['y'=4,'core'=2,'x'=4,'z_lo'=4,'z_hi'=2] {'z_lo','z_hi'}, dimensions={0} | all-to-all | bytes 262144 | tf_op jit(solution)/shard_map/all_to_all | solution.py:308
  81.1 0.6 reduce_sum.28
  81.7 0.7 tile.8
  82.4 10.3 %all_to_all.43 = f32[16,32,128]{2,1,0:T(8,128)S(1)} all-to-all(f32[16,32,128]{2,1,0:T(8,128)S(1)} %tile.8), channel_id=1, replica_groups=mesh['y'=4,'core'=2,'x'=4,'z_lo'=4,'z_hi'=2] {'y','x'}, dimensions={0} | all-to-all | bytes 524288 | tf_op jit(solution)/shard_map/all_to_all | solution.py:308
  92.7 3.7 %collective-permute-start.2 = (f32[512,128]{1,0:T(8,128)S(1)}, f32[512,128]{1,0:T(8,128)S(1)}, u32[]{:S(2)}, u32[]{:S(2)}) collective-permute-start(f32[512,128]{1,0:T(8,128)S(1)} %bitcast.13), channel_id=1, source_target_pairs={{0,32},{32,0},{1,33},{33,1},{2,34},{34,2},{3,35},{35,3},{4,36},{36... | collective-permute-start | bytes 786440 | tf_op jit(solution)/shard_map/ppermute | solution.py:304
  96.4 1.2 collective-permute-done.2.refs_5_
  97.5 0.0 copy-done.18
  97.5 0.0 copy-done.19
  97.5 1.2 copy-done.1
  98.8 1.4 %copy-done.4 = f32[3,1024,128]{2,1,0:T(8,128)S(1)} copy-done((f32[3,1024,128]{2,1,0:T(8,128)S(1)}, f32[3,1024,128]{2,1,0:T(8,128)}, u32[]{:S(2)}) %copy-start.4) | copy-done | bytes 1572888
  100.2 1.0 copy-done.8
  101.2 1.0 copy-done.10
  102.2 1.0 copy-done.12
  103.2 1.0 copy-done.14
  104.2 9.3 %apply_normal.3 = (f32[512,128]{1,0:T(8,128)S(1)}, f32[512,128]{1,0:T(8,128)S(1)}) custom-call(s32[1]{0:T(128)} %bitcast.2.core_ref, f32[2]{0:T(128)S(1)} %copy-done.18, f32[2]{0:T(128)S(1)} %copy-done.19, f32[512,128]{1,0:T(8,128)S(1)} %bitcast.12, f32[512,128]{1,0:T(8,128)} %collective-permute-done.refs_1_.refs_3_, f32[512,128]{1,0:T(8,128)S(1)} %bitcast.14, ...), custom_call_target="tpu_custom_call" | custom-call | tf_op jit(solution)/shard_map/apply_normal/pallas_call | solution.py:284
  113.5 0.0 copy-done.15
  113.5 0.0 copy-start.23
  113.5 0.5 collective-permute-start.3
  114.0 1.2 collective-permute-done.3
  115.1 0.7 add.42
  115.9 6.2 %all-to-all-start.4 = ((f32[128,4,128]{2,1,0:T(4,128)}), f32[128,4,128]{2,1,0:T(4,128)S(1)}, u32[]{:S(2)}, u32[]{:S(2)}) async-start(f32[128,4,128]{2,1,0:T(4,128)} %bitcast.8), calls=%async_computation.4 | async-start | bytes 524288 | tf_op jit(solution)/shard_map/all_to_all | solution.py:308
  122.1 0.6 fusion
  122.7 12.8 %all-to-all-done.4 = f32[128,4,128]{2,1,0:T(4,128)S(1)} async-done(((f32[128,4,128]{2,1,0:T(4,128)}), f32[128,4,128]{2,1,0:T(4,128)S(1)}, u32[]{:S(2)}, u32[]{:S(2)}) %all-to-all-start.4) | async-done | bytes 262176 | tf_op jit(solution)/shard_map/all_to_all | solution.py:308
  135.5 0.1 reduce_sum.29
  135.7 0.0 copy-done.23
  135.7 2.5 %multiply_subtract_fusion = (f32[4,128]{1,0:T(4,128)}, f32[4,128]{1,0:T(4,128)}) fusion(f32[4,128]{1,0:T(4,128)S(1)} %reduce_sum.29, f32[4,128]{1,0:T(4,128)S(1)} %copy-done.23, f32[]{:T(128)S(1)} %bitcast.16, f32[512,128]{1,0:T(8,128)} %bitcast.15, s32[]{:T(128)S(6)} %select_n.3, f32[]{:T(128)} %bitcast.1, f32[]{:T(128)} %bitcast), kind=kLoop, calls=%fused_computation | loop fusion | flops 6656 | bytes 10256 | tf_op jit(solution)/shard_map/sub | solution.py:355
  (15 shorter events, 0.1 us)
Async XLA Ops:
  0.6 35.4 %copy-start.20 = (f32[1024,64]{0,1:T(8,128)S(1)}, f32[1024,64]{0,1:T(8,128)}, u32[]{:S(2)}) copy-start(f32[1024,64]{0,1:T(8,128)} %param.15) | copy-start | bytes 786436
  30.5 16.8 %collective-permute-start = (f32[512,128]{1,0:T(8,128)S(1)}, f32[512,128]{1,0:T(8,128)}, u32[]{:S(2)}, u32[]{:S(2)}) collective-permute-start(f32[512,128]{1,0:T(8,128)S(1)} %bitcast.10), channel_id=1, source_target_pairs={{0,32},{32,0},{1,33},{33,1},{2,34},{34,2},{3,35},{35,3},{4,36},{36... | collective-permute-start | bytes 786440 | tf_op jit(solution)/shard_map/ppermute | solution.py:304
  33.3 3.8 %copy-start.21 = (s32[1024,4]{0,1:T(4,128)S(1)}, s32[1024,4]{0,1:T(4,128)}, u32[]{:S(2)}) copy-start(s32[1024,4]{0,1:T(4,128)} %param.16) | copy-start | bytes 49156
  33.3 4.9 %copy-start.17 = (s32[3,1024]{1,0:T(4,128)S(1)}, s32[3,1024]{1,0:T(4,128)}, u32[]{:S(2)}) copy-start(s32[3,1024]{1,0:T(4,128)} %rows_ref.1) | copy-start | bytes 36868
  38.1 1.4 %copy-start.2 = (f32[3,1024,64]{2,1,0:T(8,128)S(1)}, f32[3,1024,64]{2,1,0:T(8,128)}, u32[]{:S(2)}) copy-start(f32[3,1024,64]{2,1,0:T(8,128)} %copy.20.density_ref) | copy-start | bytes 2359300
  39.5 1.0 copy-start.5
  40.6 1.0 copy-start.6
  41.6 1.2 copy-start.16
  42.8 4.5 %copy-start.22 = (f32[2,1024]{1,0:T(2,128)S(1)}, f32[2,1024]{1,0:T(2,128)}, u32[]{:S(2)}) copy-start(f32[2,1024]{1,0:T(2,128)} %constant.56) | copy-start | bytes 24580
  42.8 4.8 %copy-start.7 = (bf16[256,768]{1,0:T(8,128)(2,1)S(1)}, bf16[256,768]{1,0:T(8,128)(2,1)}, u32[]{:S(2)}) copy-start(bf16[256,768]{1,0:T(8,128)(2,1)} %constant.47.clone.refs_5_.refs_9_) | copy-start | bytes 1179652
  42.8 4.9 %copy-start.9 = (bf16[256,768]{1,0:T(8,128)(2,1)S(1)}, bf16[256,768]{1,0:T(8,128)(2,1)}, u32[]{:S(2)}) copy-start(bf16[256,768]{1,0:T(8,128)(2,1)} %constant.48.clone.refs_6_.refs_10_) | copy-start | bytes 1179652
  42.8 4.9 %copy-start.11 = (bf16[768,256]{1,0:T(8,128)(2,1)S(1)}, bf16[768,256]{1,0:T(8,128)(2,1)}, u32[]{:S(2)}) copy-start(bf16[768,256]{1,0:T(8,128)(2,1)} %constant.49.clone.refs_7_.refs_11_) | copy-start | bytes 1179652
  42.8 4.9 %copy-start.13 = (bf16[768,256]{1,0:T(8,128)(2,1)S(1)}, bf16[768,256]{1,0:T(8,128)(2,1)}, u32[]{:S(2)}) copy-start(bf16[768,256]{1,0:T(8,128)(2,1)} %constant.50.clone.refs_8_.refs_12_) | copy-start | bytes 1179652
  47.3 10.1 %copy-start.3 = (f32[3,1024,128]{2,1,0:T(8,128)}, f32[3,1024,128]{2,1,0:T(8,128)S(1)}, u32[]{:S(2)}) copy-start(f32[3,1024,128]{2,1,0:T(8,128)S(1)} %get-tuple-element.9.refs_3_.refs_7_) | copy-start | bytes 4718596
  47.7 9.7 %copy-start = (f32[2,1024,128]{2,1,0:T(8,128)}, f32[2,1024,128]{2,1,0:T(8,128)S(1)}, u32[]{:S(2)}) copy-start(f32[2,1024,128]{2,1,0:T(8,128)S(1)} %broadcast_in_dim.8.refs_4_.refs_8_) | copy-start | bytes 3145732
  57.4 40.1 %copy-start.18 = (f32[2]{0:T(128)S(1)}, f32[2]{0:T(128)}, u32[]{:S(2)}) copy-start(f32[2]{0:T(128)} %refs_0_.1) | copy-start | bytes 28
  57.4 40.1 %copy-start.19 = (f32[2]{0:T(128)S(1)}, f32[2]{0:T(128)}, u32[]{:S(2)}) copy-start(f32[2]{0:T(128)} %refs_1_.1) | copy-start | bytes 28
  57.5 1.6 %collective-permute-start.1 = (f32[512,128]{1,0:T(8,128)S(1)}, f32[512,128]{1,0:T(8,128)S(1)}, u32[]{:S(2)}, u32[]{:S(2)}) collective-permute-start(f32[512,128]{1,0:T(8,128)S(1)} %get-tuple-element.11), channel_id=1, source_target_pairs={{0,32},{32,0},{1,33},{33,1},{2,34},{34,2},{3,35},{35,3},{4,36},{36... | collective-permute-start | bytes 786440 | tf_op jit(solution)/shard_map/ppermute | solution.py:304
  92.7 20.8 %copy-start.15 = (f32[16,32,128]{2,1,0:T(8,128)}, f32[16,32,128]{2,1,0:T(8,128)S(1)}, u32[]{:S(2)}) copy-start(f32[16,32,128]{2,1,0:T(8,128)S(1)} %all_to_all.43) | copy-start | bytes 786436
  92.7 4.8 %collective-permute-start.2 = (f32[512,128]{1,0:T(8,128)S(1)}, f32[512,128]{1,0:T(8,128)S(1)}, u32[]{:S(2)}, u32[]{:S(2)}) collective-permute-start(f32[512,128]{1,0:T(8,128)S(1)} %bitcast.13), channel_id=1, source_target_pairs={{0,32},{32,0},{1,33},{33,1},{2,34},{34,2},{3,35},{35,3},{4,36},{36... | collective-permute-start | bytes 786440 | tf_op jit(solution)/shard_map/ppermute | solution.py:304
  97.5 1.2 copy-start.1
  98.8 1.4 %copy-start.4 = (f32[3,1024,128]{2,1,0:T(8,128)S(1)}, f32[3,1024,128]{2,1,0:T(8,128)}, u32[]{:S(2)}) copy-start(f32[3,1024,128]{2,1,0:T(8,128)} %copy-done.3) | copy-start | bytes 4718596
  100.2 1.0 copy-start.8
  101.2 1.0 copy-start.10
  102.2 1.0 copy-start.12
  103.2 1.0 copy-start.14
  113.5 22.2 %copy-start.23 = (f32[4,128]{1,0:T(4,128)S(1)}, f32[4,128]{1,0:T(4,128)}, u32[]{:S(2)}) copy-start(f32[4,128]{1,0:T(4,128)} %param.13) | copy-start | bytes 6148
  113.5 1.6 %collective-permute-start.3 = (f32[512,128]{1,0:T(8,128)S(1)}, f32[512,128]{1,0:T(8,128)S(1)}, u32[]{:S(2)}, u32[]{:S(2)}) collective-permute-start(f32[512,128]{1,0:T(8,128)S(1)} %get-tuple-element.13), channel_id=1, source_target_pairs={{0,32},{32,0},{1,33},{33,1},{2,34},{34,2},{3,35},{35,3},{4,36},{36... | collective-permute-start | bytes 786440 | tf_op jit(solution)/shard_map/ppermute | solution.py:304
  115.9 19.6 %all-to-all-start.4 = ((f32[128,4,128]{2,1,0:T(4,128)}), f32[128,4,128]{2,1,0:T(4,128)S(1)}, u32[]{:S(2)}, u32[]{:S(2)}) async-start(f32[128,4,128]{2,1,0:T(4,128)} %bitcast.8), calls=%async_computation.4 | async-start | bytes 524288 | tf_op jit(solution)/shard_map/all_to_all | solution.py:308

commit v4 on v3

--- a/solution.py
+++ b/solution.py
@@ -47,7 +47,7 @@
     conj_high, conj_low = split_constant(complex_block(column.real, column.imag))
     column_ahead = np.concatenate([column_high, column_high, column_low], axis=0)
     column_back = np.concatenate([conj_high, conj_high, conj_low], axis=0)
-    twist = np.exp(-2j * np.pi * np.outer(np.arange(BLOCKS), np.arange(SPAN)) / TILES).reshape(TILES, 1)
+    twist = np.exp(-2j * np.pi * np.outer(np.arange(BLOCKS), np.arange(SPAN)) / TILES)
     twist = np.stack([twist.real, twist.imag]).astype(np.float32)
     return row_ahead, row_back, column_ahead, column_back, twist
 
@@ -111,38 +111,64 @@
 
 
 def prepare_kernel(
-    first_ref, sens_ref, field_ref, seg_map_ref, rows_ref, density_ref, maps_ref, weights_ref
+    first_ref, sens_ref, field_ref, seg_map_ref, rows_ref, density_ref, turns_ref,
+    maps_ref, weights_ref, twist_ref,
 ):
     seg_local = rows_ref.shape[0]
     for block in range(BLOCKS):
         at = pl.ds(block * SPAN, SPAN)
-        field = field_ref[at, :]
-        field = jnp.concatenate([field, field], axis=1)
-        named = seg_map_ref[at, :]
+        for part in range(2):
+            twist_ref[part, at, :] = jnp.broadcast_to(turns_ref[part, block : block + 1, :], (SPAN, LANES)).T
+        field = field_ref[:, at]
+        field = jnp.concatenate([field, field], axis=0).T
+        named = seg_map_ref[:, at]
+        listed = []
+        for local_seg in range(seg_local):
+            member = jnp.where(named == first_ref[0] + local_seg, 1.0, 0.0)
+            listed.append(jnp.where(jnp.sum(member, axis=0, keepdims=True) > 0.0, 1.0, 0.0))
+        listed.append(jnp.zeros((8 - seg_local, SPAN), jnp.float32))
+        listed = jnp.concatenate(listed, axis=0).T
         sens = [sens_ref[coil, at, :] for coil in range(2)]
         sens_real = jnp.concatenate([sens[0][:, :TV], sens[1][:, :TV]], axis=1)
         sens_imag = jnp.concatenate([sens[0][:, TV:], sens[1][:, TV:]], axis=1)
         for local_seg in range(seg_local):
             segment = first_ref[0] + local_seg
-            member = jnp.where(named == segment, 1.0, 0.0)
-            listed = jnp.where(jnp.sum(member, axis=1, keepdims=True) > 0.0, 1.0, 0.0)
             seg_time = (segment.astype(jnp.float32) + 0.5) / SEGS
             cosine, sine = cosine_sine(field * seg_time)
-            cosine, sine = cosine * listed, sine * listed
+            live = listed[:, local_seg : local_seg + 1]
+            cosine, sine = cosine * live, sine * live
             maps_ref[local_seg, 0, at, :] = sens_real * cosine + sens_imag * sine
             maps_ref[local_seg, 1, at, :] = sens_imag * cosine - sens_real * sine
     for local_seg in range(seg_local):
         rows_here = rows_ref[local_seg : local_seg + 1, :]
-        density = density_ref[local_seg]
-        high, low = split(jnp.concatenate([density, density], axis=1))
-        pieces = jnp.concatenate([high, low], axis=1)
+        high, low = split(density_ref[local_seg])
+        pieces = jnp.concatenate([high, high, low, low], axis=0)
         for block in range(BLOCKS):
             grid_rows = lax.broadcasted_iota(jnp.int32, (SPAN, rows_here.shape[1]), 0) * BLOCKS + block
             chosen = jnp.where(grid_rows == rows_here, 1.0, 0.0).astype(jnp.bfloat16)
-            summed = jnp.dot(chosen, pieces, preferred_element_type=jnp.float32)
+            summed = lax.dot_general(
+                chosen, pieces, (((1,), (1,)), ((), ())), preferred_element_type=jnp.float32
+            )
             weights_ref[local_seg, pl.ds(block * SPAN, SPAN), :] = (
                 summed[:, :LANES] + summed[:, LANES:]
             ) * (1.0 / (TILES * TV))
+
+
+def share_kernel(parts_ref, out_ref):
+    value = jnp.sum(parts_ref[...], axis=0)
+    for copy in range(out_ref.shape[0]):
+        out_ref[copy] = value
+
+
+def update_kernel(alpha_ref, beta_ref, parts_ref, right_ref, own_ref, solution_ref, residual_ref):
+    eight = jnp.sum(parts_ref[...], axis=0)
+    own_rows = right_ref.shape[0]
+    last_sum = eight[:own_rows] + eight[own_rows:]
+    right = right_ref[...]
+    residual = right - alpha_ref[0] * (own_ref[...] + ridge_weight * right)
+    direction = residual + beta_ref[0] * right
+    solution_ref[...] = alpha_ref[0] * right + alpha_ref[1] * direction
+    residual_ref[...] = residual - alpha_ref[1] * (last_sum + ridge_weight * direction)
 
 
 CHUNK = 16
@@ -155,8 +181,30 @@
     else:
         mine_ref, other_ref = refs[:2]
         refs = refs[2:]
-    maps_ref, weights_ref, twist_ref, row_ref, row_back_ref, col_ref, col_back_ref = refs[:7]
-    keep_ref, send_ref, dir_dup, turned, left, left_back, right, back, total = refs[7:]
+    sources = refs[:7]
+    keep_ref, send_ref, dir_dup, turned, left, left_back, right, back, total = refs[7:16]
+    held, arrived = refs[16:23], refs[23]
+    maps_ref, weights_ref, twist_ref, row_ref, row_back_ref, col_ref, col_back_ref = held
+    copies = {}
+
+    def fetch(table, part=None):
+        source, target = sources[table], held[table]
+        if part is not None:
+            source, target = source.at[part], target.at[part]
+        copy = pltpu.make_async_copy(source, target, arrived.at[len(copies)])
+        copy.start()
+        copies[table, part] = copy
+
+    fetch(0, 0)
+    fetch(2)
+    fetch(3)
+    fetch(5)
+    fetch(1, 0)
+    fetch(6)
+    fetch(4)
+    for segment in range(1, maps_ref.shape[0]):
+        fetch(0, segment)
+        fetch(1, segment)
     core = core_ref[0]
     first_half = lax.broadcasted_iota(jnp.int32, (SPAN, LANES), 1) < TV
     for pair in range(BLOCKS // 2):
@@ -171,6 +219,9 @@
             dir_dup[0, to_rows, :] = jnp.where(first_half, direction, rolled)
             dir_dup[1, to_rows, :] = jnp.where(first_half, rolled, direction)
     for segment in range(maps_ref.shape[0]):
+        copies[0, segment].wait()
+        if segment == 0:
+            copies[2, None].wait()
         for chunk in range(SPAN // CHUNK):
             at = [pl.ds(block * SPAN + chunk * CHUNK, CHUNK) for block in range(BLOCKS)]
             real, imag = [], []
@@ -193,6 +244,8 @@
                     turned[pl.ds(start, CHUNK), lanes] = high
                     turned[pl.ds(2 * SPAN + start, CHUNK), lanes] = high
                     turned[pl.ds(4 * SPAN + start, CHUNK), lanes] = low
+        if segment == 0:
+            copies[3, None].wait()
         for pair in range(BLOCKS // 2):
             grid = jnp.dot(
                 row_ref[...], turned[:, pl.ds(pair * 2 * LANES, 2 * LANES)], preferred_element_type=jnp.float32
@@ -204,6 +257,11 @@
                     left[rows, pl.ds(part * LANES, LANES)] = high
                     left[rows, pl.ds((2 + part) * LANES, LANES)] = low
                     left[rows, pl.ds((4 + part) * LANES, LANES)] = high
+        copies[1, segment].wait()
+        if segment == 0:
+            copies[5, None].wait()
+            copies[6, None].wait()
+            copies[4, None].wait()
         for pair in range(BLOCKS // 2):
             rows = pl.ds(pair * 2 * SPAN, 2 * SPAN)
             kspace = jnp.dot(left[rows, :], col_ref[...], preferred_element_type=jnp.float32)
@@ -260,31 +318,42 @@
             )
 
 
-def specs(scalars, arrays):
-    return [pl.BlockSpec(memory_space=pltpu.SMEM)] * scalars + [pl.BlockSpec(memory_space=pltpu.VMEM)] * arrays
-
-
-def prepare(first_segment, sensitivity, field_map, seg_map, sample_rows, density):
-    seg_local = sample_rows.shape[0]
+def specs(scalars, arrays, in_place=0):
+    return (
+        [pl.BlockSpec(memory_space=pltpu.SMEM)] * scalars
+        + [pl.BlockSpec(memory_space=pltpu.VMEM)] * arrays
+        + [pl.BlockSpec(memory_space=pltpu.HBM)] * in_place
+    )
+
+
+def prepare(first_segment, sensitivity, field_map, seg_map, sample_rows, density, turns):
+    seg_local, samples = sample_rows.shape
     return pl.pallas_call(
         prepare_kernel,
         out_shape=(
             jax.ShapeDtypeStruct((seg_local, 2, TILES, LANES), jnp.float32),
             jax.ShapeDtypeStruct((seg_local, TILES, LANES), jnp.float32),
+            jax.ShapeDtypeStruct((2, TILES, LANES), jnp.float32),
         ),
-        in_specs=specs(1, 5),
-        out_specs=tuple(specs(0, 2)),
+        in_specs=specs(1, 6),
+        out_specs=tuple(specs(0, 3)),
         compiler_params=pltpu.CompilerParams(vmem_limit_bytes=16 << 20),
+        cost_estimate=pl.CostEstimate(
+            flops=2 * seg_local * TILES * samples * 2 * LANES,
+            transcendentals=2 * seg_local * TILES * LANES,
+            bytes_accessed=4 * seg_local * (3 * TILES * LANES + samples * TV) + 8 * TILES * LANES,
+        ),
         name="maps_and_weights",
-    )(first_segment, sensitivity, field_map, seg_map, sample_rows, density)
+    )(first_segment, sensitivity, field_map.T, seg_map.T, sample_rows, jnp.swapaxes(density, 1, 2), turns)
 
 
 def apply_normal(core, steps, directions, tables):
     half = jax.ShapeDtypeStruct((TILES // 2, LANES), jnp.float32)
+    segments = tables[0].shape[0]
     return pl.pallas_call(
         functools.partial(normal_kernel, len(steps) > 0),
         out_shape=(half, half),
-        in_specs=specs(1 + len(steps), len(directions) + len(tables)),
+        in_specs=specs(1 + len(steps), len(directions), len(tables)),
         out_specs=tuple(specs(0, 2)),
         scratch_shapes=[
             pltpu.VMEM((2, TILES, LANES), jnp.float32),
@@ -294,8 +363,15 @@
             pltpu.VMEM((6 * SPAN, BLOCKS * LANES), jnp.bfloat16),
             pltpu.VMEM((2 * SPAN, BLOCKS * LANES), jnp.float32),
             pltpu.VMEM((2, TILES, LANES), jnp.float32),
-        ],
-        compiler_params=pltpu.CompilerParams(vmem_limit_bytes=20 << 20),
+        ]
+        + [pltpu.VMEM(table.shape, table.dtype) for table in tables]
+        + [pltpu.SemaphoreType.DMA((5 + 2 * segments,))],
+        compiler_params=pltpu.CompilerParams(vmem_limit_bytes=60 << 20),
+        cost_estimate=pl.CostEstimate(
+            flops=12 * segments * TILES * 6 * LANES * 4 * LANES,
+            transcendentals=0,
+            bytes_accessed=4 * segments * 4 * TILES * LANES,
+        ),
         name="apply_normal",
     )(core, *steps, *directions, *tables)
 
@@ -308,24 +384,42 @@
     return lax.all_to_all(value, axes, 0, 0, tiled=True)
 
 
-def summed(parts, count):
-    return jnp.sum(parts.reshape(count, -1, LANES), axis=0)
+def share(parts, count, copies):
+    rows = parts.shape[0] // count
+    shared = pl.pallas_call(
+        share_kernel,
+        out_shape=jax.ShapeDtypeStruct((copies, rows, LANES), jnp.float32),
+        in_specs=specs(0, 1),
+        out_specs=specs(0, 1)[0],
+        name="sum_and_copy",
+    )(parts.reshape(count, rows, LANES))
+    return shared.reshape(copies * rows, LANES)
 
 
 def gather_direction(own_tiles):
-    mine = exchange(jnp.tile(own_tiles, (DEVICES // 2, 1)), SAME_CORE)
+    return exchange(jnp.tile(own_tiles, (DEVICES // 2, 1)), SAME_CORE)
+
+
+def sum_to_owners(keep, send):
+    return exchange(keep + swap_cores(send), SAME_CORE)
+
+
+def sum_for_all(keep, send):
+    copies = share(exchange(keep + swap_cores(send), ("y", "x")), 16, 8)
+    copies = share(exchange(copies, ("z_lo", "z_hi")), 8, 16)
+    mine = exchange(copies, ("y", "x"))
     return mine, swap_cores(mine)
 
 
-def sum_to_owners(keep, send):
-    return summed(exchange(keep + swap_cores(send), SAME_CORE), DEVICES // 2)
-
-
-def sum_for_all(keep, send):
-    share = summed(exchange(keep + swap_cores(send), ("y", "x")), 16)
-    share = summed(exchange(jnp.tile(share, (8, 1)), ("z_lo", "z_hi")), 8)
-    mine = exchange(jnp.tile(share, (16, 1)), ("y", "x"))
-    return mine, swap_cores(mine)
+def update(step_alpha, step_beta, parts, right_side, own_sum):
+    own = jax.ShapeDtypeStruct(right_side.shape, jnp.float32)
+    return pl.pallas_call(
+        update_kernel,
+        out_shape=(own, own),
+        in_specs=specs(2, 3),
+        out_specs=tuple(specs(0, 2)),
+        name="last_update",
+    )(step_alpha, step_beta, parts.reshape(-1, 2 * right_side.shape[0], LANES), right_side, own_sum)
 
 
 def shards(
@@ -334,26 +428,22 @@
     seg_local = sample_rows.shape[0]
     first_segment = lax.axis_index(("y", "core")) * seg_local
     core = lax.axis_index("core").reshape(1)
-    row_ahead, row_back, column_ahead, column_back, twist = map(jnp.asarray, transform_constants())
-    twist = jnp.broadcast_to(twist, (2, TILES, LANES))
+    row_ahead, row_back, column_ahead, column_back, turns = map(jnp.asarray, transform_constants())
     gathered = gather_direction(right_side)
-    maps, weights = prepare(
-        first_segment.reshape(1), sensitivity, field_map, seg_map, sample_rows, density
-    )
+    maps, weights, twist = prepare(
+        first_segment.reshape(1), sensitivity, field_map, seg_map, sample_rows, density, turns
+    )
+    gathered, maps, weights, twist = lax.optimization_barrier((gathered, maps, weights, twist))
+    gathered = (gathered, swap_cores(gathered))
     tables = (maps, weights, twist, row_ahead, row_back, column_ahead, column_back)
     sums = sum_for_all(*apply_normal(core, (), gathered, tables))
     own_tiles = right_side.shape[0]
     own_start = lax.axis_index(SAME_CORE) * own_tiles
     own_sum = lax.dynamic_slice_in_dim(sums[0], own_start, own_tiles, 0)
-    solution_field = step_alpha[0] * right_side
-    residual = right_side - step_alpha[0] * (own_sum + ridge_weight * right_side)
-    direction = residual + step_beta[0] * right_side
-    last_sum = sum_to_owners(
+    parts = sum_to_owners(
         *apply_normal(core, (step_alpha, step_beta), (*gathered, *sums), tables)
     )
-    solution_field = solution_field + step_alpha[1] * direction
-    residual = residual - step_alpha[1] * (last_sum + ridge_weight * direction)
-    return (solution_field, residual)
+    return update(step_alpha, step_beta, parts, right_side, own_sum)
 
 
 def solution(mesh):

time: 139 us -> 139 us (level)
  blocking collectives: 60.3 us -> 38.9 us
  starting transfers between devices: 13.1 us -> 28.4 us
  Pallas kernels: 23.5 us -> 36.3 us
  local copies, waits for them, and re-layouts: 18.7 us -> 14 us
  other arithmetic: 5.03 us -> 2.69 us
    all_to_all x4 -> x3, blocking collectives: 60.3 us -> 38.9 us  [exchange(): return lax.all_to_all(value, axes, 0, 0, tiled=True)]
    all_to_all x1 -> x2, starting transfers between devices: 6.18 us -> 22.5 us  [exchange(): return lax.all_to_all(value, axes, 0, 0, tiled=True)]
    pallas_call x2, Pallas kernels: 19 us -> 25.6 us  [apply_normal(): pl.pallas_call(functools.partial(normal_kernel, len(steps) > 0), out_shap...]
    pallas_call x0 -> x3, Pallas kernels: none -> 4.89 us  [the longest x2 3.26 us: share(): pl.pallas_call(share_kernel, out_shape=jax.ShapeDtypeStruct((copies, rows...]
    unnamed x51 -> x28, local copies, waits for them, and re-layouts: 16.2 us -> 11.4 us
    sub x1 -> x0, other arithmetic: 2.52 us -> none  [shards(): residual = residual - step_alpha[1] * (last_sum + ridge_weight * direction)]
    add x2, other arithmetic: 0.78 us -> 2.69 us  [the longest x1 1.7 us: sum_to_owners(): return exchange(keep + swap_cores(send), SAME_CORE)]
    reduce_sum x3 -> x0, other arithmetic: 1.73 us -> none  [summed(): return jnp.sum(parts.reshape(count, -1, LANES), axis=0)]
  transfers between devices with their start and end apart: 5 -> 6, of which waited for: 4 -> 5; matrix products, arithmetic and copies ran while one was open for 4% -> 1% of each run, Pallas kernels for 3% -> 4%
where the time goes in v4:
time: 139 us; the launch traced here: 138 us
  blocking collectives  38.9 us (28%)
  Pallas kernels  36.3 us (26%)
  starting transfers between devices  28.4 us (20%)
  waiting for transfers between devices  17.3 us (12%)
  local copies, waits for them, and re-layouts  14 us (10%)
  other arithmetic  2.69 us (2%)
    all_to_all x3, blocking collectives, exchange(): return lax.all_to_all(value, axes, 0, 0, tiled=True)  38.9 us
    pallas_call x2, Pallas kernels, apply_normal(): pl.pallas_call(functools.partial(normal_kernel, len(steps) > 0), out_shap...  25.6 us
    all_to_all x2, starting transfers between devices, exchange(): return lax.all_to_all(value, axes, 0, 0, tiled=True)  22.5 us
    all_to_all x2, waiting for transfers between devices, exchange(): return lax.all_to_all(value, axes, 0, 0, tiled=True)  12.2 us
    unnamed x28, local copies, waits for them, and re-layouts  11.4 us
    ppermute x4, starting transfers between devices, swap_cores(): return lax.ppermute(value, 'core', [(0, 1), (1, 0)])  5.85 us
    pallas_call x1, Pallas kernels, prepare(): pl.pallas_call(prepare_kernel, out_shape=(jax.ShapeDtypeStruct((seg_local...  5.8 us
    ppermute x4, waiting for transfers between devices, swap_cores(): return lax.ppermute(value, 'core', [(0, 1), (1, 0)])  5.07 us
  transfers between devices with their start and end apart: 6, of which 5 were waited for; matrix products, arithmetic and copies ran while one was open for 1% of the time, Pallas kernels for 4%

profile of v4, /device:TPU:1, one launch (start us, length us, event | category | flops | bytes accessed | tf_op | source)
XLA Modules:
  0.0 138.3 jit_solution(12127010637380723701)
XLA Ops:
  0.6 1.4 %tile.2 = f32[128,4,128]{2,1,0:T(4,128)} broadcast(f32[4,128]{1,0:T(4,128)} %right_ref.1), dimensions={1,2} | broadcast | bytes 264192 | tf_op jit(solution)/shard_map/tile | solution.py:400
  2.0 16.3 %all-to-all-start = ((f32[128,4,128]{2,1,0:T(4,128)}), f32[128,4,128]{2,1,0:T(4,128)S(1)}, u32[]{:S(2)}, u32[]{:S(2)}) async-start(f32[128,4,128]{2,1,0:T(4,128)} %tile.2), calls=%async_computation | async-start | bytes 524288 | tf_op jit(solution)/shard_map/all_to_all | solution.py:384
  18.4 0.0 copy-start
  18.4 1.2 copy-done
  19.6 0.0 copy-start.1
  19.6 1.1 copy-done.1
  20.8 0.0 copy-start.2
  20.8 0.9 copy-done.2
  21.7 0.0 copy-start.3
  21.7 0.7 copy-done.3
  22.4 0.0 copy-start.4
  22.4 0.7 copy-done.4
  23.1 0.0 copy-start.5
  23.1 0.7 copy-done.5
  23.8 5.8 %maps_and_weights.1 = (f32[3,2,1024,128]{3,2,1,0:T(8,128)S(1)}, f32[3,1024,128]{2,1,0:T(8,128)S(1)}, f32[2,1024,128]{2,1,0:T(8,128)S(1)}) custom-call(s32[1]{0:T(128)} %bitcast.2.first_ref, f32[2,1024,128]{2,1,0:T(8,128)S(1)} %copy-done, f32[64,1024]{1,0:T(8,128)S(1)} %bitcast.11, s32[4,1024]{1,0:T(4,128)S(1)} %bitcast.12, s32[3,1024]{1,0:T(4,128)S(1)} %copy-done.4, ...), custom_call_target="tpu_custom_call" | custom-call | flops 1610612736 | bytes 6553600 | tf_op jit(solution)/shard_map/maps_and_weights/pallas_call | solution.py:331
  29.6 0.0 copy-start.6
  29.7 1.6 %copy-done.6 = f32[3,2,1024,128]{3,2,1,0:T(8,128)} copy-done((f32[3,2,1024,128]{3,2,1,0:T(8,128)}, f32[3,2,1024,128]{3,2,1,0:T(8,128)S(1)}, u32[]{:S(2)}) %copy-start.6) | copy-done | bytes 3145752
  31.3 0.0 copy-start.7
  31.3 1.2 copy-done.7
  32.4 0.0 copy-start.8
  32.4 1.0 copy-done.8
  33.4 0.0 all-to-all-done
  33.4 0.0 copy-start.11
  33.4 1.0 collective-permute-start
  34.4 1.2 collective-permute-done.refs_1_.refs_3_
  35.6 0.0 copy-start.12
  35.6 0.0 copy-done.11
  35.6 0.7 copy-done.12
  36.3 12.7 %apply_normal.2 = (f32[512,128]{1,0:T(8,128)}, f32[512,128]{1,0:T(8,128)}) custom-call(s32[1]{0:T(128)} %bitcast.core_ref, f32[512,128]{1,0:T(8,128)} %bitcast.19, f32[512,128]{1,0:T(8,128)} %copy-done.12, f32[3,2,1024,128]{3,2,1,0:T(8,128)} %copy-done.6, f32[3,1024,128]{2,1,0:T(8,128)} %copy-done.7, f32[2,1024,128]{2,1,0:T(8,128)} %copy-done.8, ...), custom_call_target="tpu_custom_call" | custom-call | flops 14495514624 | bytes 6291456 | tf_op jit(solution)/shard_map/apply_normal/pallas_call | solution.py:353
  49.0 0.5 collective-permute-start.1
  49.4 1.4 collective-permute-done.1
  50.8 1.0 add.22
  51.8 14.6 %all_to_all.41.parts_ref = f32[16,32,128]{2,1,0:T(8,128)} all-to-all(f32[16,32,128]{2,1,0:T(8,128)S(1)} %bitcast.13), channel_id=1, replica_groups=mesh['y'=4,'core'=2,'x'=4,'z_lo'=4,'z_hi'=2] {'y','x'}, dimensions={0} | all-to-all | bytes 524288 | tf_op jit(solution)/shard_map/all_to_all | solution.py:384
  66.4 1.6 %sum_and_copy.2 = f32[8,32,128]{2,1,0:T(8,128)} custom-call(f32[16,32,128]{2,1,0:T(8,128)} %all_to_all.41.parts_ref), custom_call_target="tpu_custom_call" | custom-call | tf_op jit(solution)/shard_map/sum_and_copy/pallas_call | solution.py:389
  68.0 13.3 %all_to_all.42.parts_ref = f32[8,32,128]{2,1,0:T(8,128)} all-to-all(f32[8,32,128]{2,1,0:T(8,128)} %sum_and_copy.2), channel_id=1, replica_groups=mesh['y'=4,'core'=2,'x'=4,'z_lo'=4,'z_hi'=2] {'z_lo','z_hi'}, dimensions={0} | all-to-all | bytes 262144 | tf_op jit(solution)/shard_map/all_to_all | solution.py:384
  81.3 1.6 %sum_and_copy.3 = f32[16,32,128]{2,1,0:T(8,128)} custom-call(f32[8,32,128]{2,1,0:T(8,128)} %all_to_all.42.parts_ref), custom_call_target="tpu_custom_call" | custom-call | tf_op jit(solution)/shard_map/sum_and_copy/pallas_call | solution.py:389
  82.9 11.1 %all_to_all.43 = f32[16,32,128]{2,1,0:T(8,128)S(1)} all-to-all(f32[16,32,128]{2,1,0:T(8,128)} %sum_and_copy.3), channel_id=1, replica_groups=mesh['y'=4,'core'=2,'x'=4,'z_lo'=4,'z_hi'=2] {'y','x'}, dimensions={0} | all-to-all | bytes 524288 | tf_op jit(solution)/shard_map/all_to_all | solution.py:384
  94.0 0.0 copy-start.10
  94.0 4.0 %collective-permute-start.2 = (f32[512,128]{1,0:T(8,128)S(1)}, f32[512,128]{1,0:T(8,128)S(1)}, u32[]{:S(2)}, u32[]{:S(2)}) collective-permute-start(f32[512,128]{1,0:T(8,128)S(1)} %bitcast.15), channel_id=1, source_target_pairs={{0,32},{32,0},{1,33},{33,1},{2,34},{34,2},{3,35},{35,3},{4,36},{36... | collective-permute-start | bytes 786440 | tf_op jit(solution)/shard_map/ppermute | solution.py:380
  98.0 1.2 collective-permute-done.2.refs_5_
  99.1 0.0 copy-done.10
  99.1 0.0 copy-start.13
  99.2 0.7 copy-done.13
  99.9 12.9 %apply_normal.3 = (f32[512,128]{1,0:T(8,128)}, f32[512,128]{1,0:T(8,128)}) custom-call(s32[1]{0:T(128)} %bitcast.core_ref, f32[2]{0:T(128)} %alpha_ref.1, f32[2]{0:T(128)} %beta_ref.1, f32[512,128]{1,0:T(8,128)} %bitcast.20, f32[512,128]{1,0:T(8,128)} %copy-done.12, f32[512,128]{1,0:T(8,128)} %bitcast.16, f32[512,128]{1,0:T(8,128)} %copy-done.13, ...), custom_call_target="tpu_custom_call" | custom-call | flops 14495514624 | bytes 6291456 | tf_op jit(solution)/shard_map/apply_normal/pallas_call | solution.py:353
  112.7 0.5 collective-permute-start.3
  113.2 1.4 collective-permute-done.3
  114.6 1.7 %add.23 = f32[512,128]{1,0:T(8,128)} add(f32[512,128]{1,0:T(8,128)} %get-tuple-element.22, f32[512,128]{1,0:T(8,128)S(1)} %collective-permute-done.3) | non-fusion elementwise | flops 65536 | bytes 786432 | tf_op jit(solution)/shard_map/add | solution.py:404
  116.3 6.2 %all-to-all-start.4 = ((f32[128,4,128]{2,1,0:T(4,128)}), f32[128,4,128]{2,1,0:T(4,128)S(1)}, u32[]{:S(2)}, u32[]{:S(2)}) async-start(f32[128,4,128]{2,1,0:T(4,128)} %bitcast.8), calls=%async_computation.4 | async-start | bytes 524288 | tf_op jit(solution)/shard_map/all_to_all | solution.py:384
  122.5 1.3 constant_dynamic-slice_fusion.own_ref
  123.7 12.2 %all-to-all-done.4 = f32[128,4,128]{2,1,0:T(4,128)S(1)} async-done(((f32[128,4,128]{2,1,0:T(4,128)}), f32[128,4,128]{2,1,0:T(4,128)S(1)}, u32[]{:S(2)}, u32[]{:S(2)}) %all-to-all-start.4) | async-done | bytes 262176 | tf_op jit(solution)/shard_map/all_to_all | solution.py:384
  135.9 0.0 copy-start.9
  135.9 0.7 copy-done.9
  136.6 1.6 %last_update.1 = (f32[4,128]{1,0:T(4,128)}, f32[4,128]{1,0:T(4,128)}) custom-call(f32[2]{0:T(128)} %alpha_ref.1, f32[2]{0:T(128)} %beta_ref.1, f32[64,8,128]{2,1,0:T(8,128)} %bitcast.14, f32[4,128]{1,0:T(4,128)} %right_ref.1, f32[4,128]{1,0:T(4,128)} %constant_dynamic-slice_fusion.own_ref), custom_call_target="tpu_custom_call" | custom-call | tf_op jit(solution)/shard_map/last_update/pallas_call | solution.py:416
Async XLA Ops:
  2.0 31.4 %all-to-all-start = ((f32[128,4,128]{2,1,0:T(4,128)}), f32[128,4,128]{2,1,0:T(4,128)S(1)}, u32[]{:S(2)}, u32[]{:S(2)}) async-start(f32[128,4,128]{2,1,0:T(4,128)} %tile.2), calls=%async_computation | async-start | bytes 524288 | tf_op jit(solution)/shard_map/all_to_all | solution.py:384
  18.4 1.2 copy-start
  19.6 1.1 copy-start.1
  20.8 0.9 copy-start.2
  21.7 0.7 copy-start.3
  22.4 0.7 copy-start.4
  23.1 0.7 copy-start.5
  29.6 1.6 %copy-start.6 = (f32[3,2,1024,128]{3,2,1,0:T(8,128)}, f32[3,2,1024,128]{3,2,1,0:T(8,128)S(1)}, u32[]{:S(2)}) copy-start(f32[3,2,1024,128]{3,2,1,0:T(8,128)S(1)} %get-tuple-element.17.refs_2_.refs_6_) | copy-start | bytes 9437188
  31.3 1.2 copy-start.7
  32.4 1.0 copy-start.8
  33.4 2.1 %copy-start.11 = (f32[128,4,128]{2,1,0:T(4,128)}, f32[128,4,128]{2,1,0:T(4,128)S(1)}, u32[]{:S(2)}) copy-start(f32[128,4,128]{2,1,0:T(4,128)S(1)} %all-to-all-done) | copy-start | bytes 786436
  33.4 2.1 %collective-permute-start = (f32[512,128]{1,0:T(8,128)S(1)}, f32[512,128]{1,0:T(8,128)S(1)}, u32[]{:S(2)}, u32[]{:S(2)}) collective-permute-start(f32[512,128]{1,0:T(8,128)S(1)} %bitcast.18), channel_id=1, source_target_pairs={{0,32},{32,0},{1,33},{33,1},{2,34},{34,2},{3,35},{35,3},{4,36},{36... | collective-permute-start | bytes 786440 | tf_op jit(solution)/shard_map/ppermute | solution.py:380
  35.6 0.7 copy-start.12
  49.0 1.8 %collective-permute-start.1 = (f32[512,128]{1,0:T(8,128)}, f32[512,128]{1,0:T(8,128)S(1)}, u32[]{:S(2)}, u32[]{:S(2)}) collective-permute-start(f32[512,128]{1,0:T(8,128)} %get-tuple-element.21), channel_id=1, source_target_pairs={{0,32},{32,0},{1,33},{33,1},{2,34},{34,2},{3,35},{35,3},{4,36},{36... | collective-permute-start | bytes 786440 | tf_op jit(solution)/shard_map/ppermute | solution.py:380
  94.0 5.1 %copy-start.10 = (f32[16,32,128]{2,1,0:T(8,128)}, f32[16,32,128]{2,1,0:T(8,128)S(1)}, u32[]{:S(2)}) copy-start(f32[16,32,128]{2,1,0:T(8,128)S(1)} %all_to_all.43) | copy-start | bytes 786436
  94.0 5.1 %collective-permute-start.2 = (f32[512,128]{1,0:T(8,128)S(1)}, f32[512,128]{1,0:T(8,128)S(1)}, u32[]{:S(2)}, u32[]{:S(2)}) collective-permute-start(f32[512,128]{1,0:T(8,128)S(1)} %bitcast.15), channel_id=1, source_target_pairs={{0,32},{32,0},{1,33},{33,1},{2,34},{34,2},{3,35},{35,3},{4,36},{36... | collective-permute-start | bytes 786440 | tf_op jit(solution)/shard_map/ppermute | solution.py:380
  99.1 0.7 copy-start.13
  112.7 1.8 %collective-permute-start.3 = (f32[512,128]{1,0:T(8,128)}, f32[512,128]{1,0:T(8,128)S(1)}, u32[]{:S(2)}, u32[]{:S(2)}) collective-permute-start(f32[512,128]{1,0:T(8,128)} %get-tuple-element.23), channel_id=1, source_target_pairs={{0,32},{32,0},{1,33},{33,1},{2,34},{34,2},{3,35},{35,3},{4,36},{36... | collective-permute-start | bytes 786440 | tf_op jit(solution)/shard_map/ppermute | solution.py:380
  116.3 19.6 %all-to-all-start.4 = ((f32[128,4,128]{2,1,0:T(4,128)}), f32[128,4,128]{2,1,0:T(4,128)S(1)}, u32[]{:S(2)}, u32[]{:S(2)}) async-start(f32[128,4,128]{2,1,0:T(4,128)} %bitcast.8), calls=%async_computation.4 | async-start | bytes 524288 | tf_op jit(solution)/shard_map/all_to_all | solution.py:384
  135.9 0.7 copy-start.9

commit v5 on v4

--- a/solution.py
+++ b/solution.py
@@ -36,20 +36,17 @@
 def transform_constants():
     steps = np.arange(SPAN)
     row = np.exp(-2j * np.pi * (np.outer(steps, steps) % SPAN) / SPAN)
-    row_high, row_low = split_constant(complex_block(row.real, row.imag))
-    back_high, back_low = split_constant(complex_block(row.real, -row.imag))
-    row_ahead = np.concatenate([row_high, row_low, row_high], axis=1)
-    row_back = np.concatenate([back_high, back_low, back_high], axis=1)
+    row_ahead = complex_block(row.real, row.imag)
+    row_back = complex_block(row.real, -row.imag)
     steps = np.arange(TV)
     column = np.exp(-2j * np.pi * (np.outer(steps, steps) % TV) / TV)
     column = np.kron(np.eye(2), column)
-    column_high, column_low = split_constant(complex_block(column.real, -column.imag))
-    conj_high, conj_low = split_constant(complex_block(column.real, column.imag))
-    column_ahead = np.concatenate([column_high, column_high, column_low], axis=0)
-    column_back = np.concatenate([conj_high, conj_high, conj_low], axis=0)
-    twist = np.exp(-2j * np.pi * np.outer(np.arange(BLOCKS), np.arange(SPAN)) / TILES)
-    twist = np.stack([twist.real, twist.imag]).astype(np.float32)
-    return row_ahead, row_back, column_ahead, column_back, twist
+    column_ahead = complex_block(column.real, -column.imag)
+    column_back = complex_block(column.real, column.imag)
+    pieces = []
+    for matrix in (row_ahead, row_back, column_ahead, column_back):
+        pieces += split_constant(matrix)
+    return np.concatenate(pieces, axis=1)
 
 
 def split(value):
@@ -90,6 +87,13 @@
     return [even[0], odd[0], even[1], odd[1], even[2], odd[2], even[3], odd[3]]
 
 
+def table_parts(tables_ref):
+    segments = (tables_ref.shape[0] - 2) // 3
+    maps_ref = tables_ref.at[pl.ds(0, 2 * segments)]
+    weights_ref = tables_ref.at[pl.ds(2 * segments, segments)]
+    return maps_ref, weights_ref, tables_ref.at[pl.ds(3 * segments, 2)]
+
+
 def cosine_sine(angle):
     turns = jnp.round(angle * (2.0 / math.pi))
     rest = angle - turns * 1.5703125
@@ -111,14 +115,18 @@
 
 
 def prepare_kernel(
-    first_ref, sens_ref, field_ref, seg_map_ref, rows_ref, density_ref, turns_ref,
-    maps_ref, weights_ref, twist_ref,
+    first_ref, core_ref, sens_ref, field_ref, seg_map_ref, rows_ref, density_ref, tables_ref, core_out_ref
 ):
+    core_out_ref[0] = core_ref[0]
     seg_local = rows_ref.shape[0]
+    maps_ref, weights_ref, twist_ref = table_parts(tables_ref)
+    lane = lax.broadcasted_iota(jnp.int32, (SPAN, LANES), 0).astype(jnp.float32)
     for block in range(BLOCKS):
         at = pl.ds(block * SPAN, SPAN)
-        for part in range(2):
-            twist_ref[part, at, :] = jnp.broadcast_to(turns_ref[part, block : block + 1, :], (SPAN, LANES)).T
+        if block > 0:
+            twist_cosine, twist_sine = cosine_sine(lane * (2.0 * math.pi * block / TILES))
+            twist_ref[0, at, :] = twist_cosine
+            twist_ref[1, at, :] = -twist_sine
         field = field_ref[:, at]
         field = jnp.concatenate([field, field], axis=0).T
         named = seg_map_ref[:, at]
@@ -137,8 +145,8 @@
             cosine, sine = cosine_sine(field * seg_time)
             live = listed[:, local_seg : local_seg + 1]
             cosine, sine = cosine * live, sine * live
-            maps_ref[local_seg, 0, at, :] = sens_real * cosine + sens_imag * sine
-            maps_ref[local_seg, 1, at, :] = sens_imag * cosine - sens_real * sine
+            maps_ref[2 * local_seg, at, :] = sens_real * cosine + sens_imag * sine
+            maps_ref[2 * local_seg + 1, at, :] = sens_imag * cosine - sens_real * sine
     for local_seg in range(seg_local):
         rows_here = rows_ref[local_seg : local_seg + 1, :]
         high, low = split(density_ref[local_seg])
@@ -181,30 +189,16 @@
     else:
         mine_ref, other_ref = refs[:2]
         refs = refs[2:]
-    sources = refs[:7]
-    keep_ref, send_ref, dir_dup, turned, left, left_back, right, back, total = refs[7:16]
-    held, arrived = refs[16:23], refs[23]
-    maps_ref, weights_ref, twist_ref, row_ref, row_back_ref, col_ref, col_back_ref = held
-    copies = {}
-
-    def fetch(table, part=None):
-        source, target = sources[table], held[table]
-        if part is not None:
-            source, target = source.at[part], target.at[part]
-        copy = pltpu.make_async_copy(source, target, arrived.at[len(copies)])
-        copy.start()
-        copies[table, part] = copy
-
-    fetch(0, 0)
-    fetch(2)
-    fetch(3)
-    fetch(5)
-    fetch(1, 0)
-    fetch(6)
-    fetch(4)
-    for segment in range(1, maps_ref.shape[0]):
-        fetch(0, segment)
-        fetch(1, segment)
+    tables_ref, transforms_ref = refs[:2]
+    keep_ref, send_ref, dir_dup, turned, left, left_back, right, back, total = refs[2:]
+    maps_ref, weights_ref, twist_ref = table_parts(tables_ref)
+    segments = weights_ref.shape[0]
+
+    def transform(which, axis):
+        high = transforms_ref[:, pl.ds(4 * SPAN * which, 2 * SPAN)]
+        low = transforms_ref[:, pl.ds(4 * SPAN * which + 2 * SPAN, 2 * SPAN)]
+        return jnp.concatenate([high, low, high] if axis == 1 else [high, high, low], axis=axis)
+
     core = core_ref[0]
     first_half = lax.broadcasted_iota(jnp.int32, (SPAN, LANES), 1) < TV
     for pair in range(BLOCKS // 2):
@@ -218,15 +212,12 @@
             rolled = pltpu.roll(direction, TV, 1)
             dir_dup[0, to_rows, :] = jnp.where(first_half, direction, rolled)
             dir_dup[1, to_rows, :] = jnp.where(first_half, rolled, direction)
-    for segment in range(maps_ref.shape[0]):
-        copies[0, segment].wait()
-        if segment == 0:
-            copies[2, None].wait()
+    for segment in range(segments):
         for chunk in range(SPAN // CHUNK):
             at = [pl.ds(block * SPAN + chunk * CHUNK, CHUNK) for block in range(BLOCKS)]
             real, imag = [], []
             for rows in at:
-                map_real, map_imag = maps_ref[segment, 0, rows, :], maps_ref[segment, 1, rows, :]
+                map_real, map_imag = maps_ref[2 * segment, rows, :], maps_ref[2 * segment + 1, rows, :]
                 dir_real, dir_imag = dir_dup[0, rows, :], dir_dup[1, rows, :]
                 real.append(map_real * dir_real - map_imag * dir_imag)
                 imag.append(map_real * dir_imag + map_imag * dir_real)
@@ -244,11 +235,9 @@
                     turned[pl.ds(start, CHUNK), lanes] = high
                     turned[pl.ds(2 * SPAN + start, CHUNK), lanes] = high
                     turned[pl.ds(4 * SPAN + start, CHUNK), lanes] = low
-        if segment == 0:
-            copies[3, None].wait()
         for pair in range(BLOCKS // 2):
             grid = jnp.dot(
-                row_ref[...], turned[:, pl.ds(pair * 2 * LANES, 2 * LANES)], preferred_element_type=jnp.float32
+                transform(0, 1), turned[:, pl.ds(pair * 2 * LANES, 2 * LANES)], preferred_element_type=jnp.float32
             )
             for side in range(2):
                 rows = pl.ds((2 * pair + side) * SPAN, SPAN)
@@ -257,14 +246,9 @@
                     left[rows, pl.ds(part * LANES, LANES)] = high
                     left[rows, pl.ds((2 + part) * LANES, LANES)] = low
                     left[rows, pl.ds((4 + part) * LANES, LANES)] = high
-        copies[1, segment].wait()
-        if segment == 0:
-            copies[5, None].wait()
-            copies[6, None].wait()
-            copies[4, None].wait()
         for pair in range(BLOCKS // 2):
             rows = pl.ds(pair * 2 * SPAN, 2 * SPAN)
-            kspace = jnp.dot(left[rows, :], col_ref[...], preferred_element_type=jnp.float32)
+            kspace = jnp.dot(left[rows, :], transform(2, 0), preferred_element_type=jnp.float32)
             weights = weights_ref[segment, rows, :]
             high, low = split(kspace * jnp.concatenate([weights, weights], axis=1))
             left_back[rows, pl.ds(0, 2 * LANES)] = high
@@ -272,7 +256,7 @@
             left_back[rows, pl.ds(4 * LANES, 2 * LANES)] = high
         for pair in range(BLOCKS // 2):
             rows = pl.ds(pair * 2 * SPAN, 2 * SPAN)
-            grid = jnp.dot(left_back[rows, :], col_back_ref[...], preferred_element_type=jnp.float32)
+            grid = jnp.dot(left_back[rows, :], transform(3, 0), preferred_element_type=jnp.float32)
             high, low = split(grid)
             for side in range(2):
                 lanes = pl.ds((2 * pair + side) * LANES, LANES)
@@ -283,7 +267,7 @@
                     right[pl.ds((4 + part) * SPAN, SPAN), lanes] = low[piece]
         for pair in range(BLOCKS // 2):
             lanes = pl.ds(pair * 2 * LANES, 2 * LANES)
-            back[:, lanes] = jnp.dot(row_back_ref[...], right[:, lanes], preferred_element_type=jnp.float32)
+            back[:, lanes] = jnp.dot(transform(1, 1), right[:, lanes], preferred_element_type=jnp.float32)
         for chunk in range(SPAN // CHUNK):
             real, imag = [], []
             for block in range(BLOCKS):
@@ -301,7 +285,7 @@
                 imag.append(value_imag)
             for block, (value_imag, value_real) in enumerate(eight_point(imag, real)):
                 rows = pl.ds(block * SPAN + chunk * CHUNK, CHUNK)
-                map_real, map_imag = maps_ref[segment, 0, rows, :], maps_ref[segment, 1, rows, :]
+                map_real, map_imag = maps_ref[2 * segment, rows, :], maps_ref[2 * segment + 1, rows, :]
                 add_real = map_real * value_real + map_imag * value_imag
                 add_imag = map_real * value_imag - map_imag * value_real
                 if segment > 0:
@@ -322,38 +306,41 @@
     return (
         [pl.BlockSpec(memory_space=pltpu.SMEM)] * scalars
         + [pl.BlockSpec(memory_space=pltpu.VMEM)] * arrays
-        + [pl.BlockSpec(memory_space=pltpu.HBM)] * in_place
-    )
-
-
-def prepare(first_segment, sensitivity, field_map, seg_map, sample_rows, density, turns):
+        + [pl.BlockSpec(memory_space=pl.ANY)] * in_place
+    )
+
+
+def limit(mebibytes):
+    return pltpu.CompilerParams(vmem_limit_bytes=mebibytes << 20)
+
+
+def prepare(first_segment, core, sensitivity, field_map, seg_map, sample_rows, density):
     seg_local, samples = sample_rows.shape
     return pl.pallas_call(
         prepare_kernel,
         out_shape=(
-            jax.ShapeDtypeStruct((seg_local, 2, TILES, LANES), jnp.float32),
-            jax.ShapeDtypeStruct((seg_local, TILES, LANES), jnp.float32),
-            jax.ShapeDtypeStruct((2, TILES, LANES), jnp.float32),
+            jax.ShapeDtypeStruct((3 * seg_local + 2, TILES, LANES), jnp.float32),
+            jax.ShapeDtypeStruct((1,), jnp.int32),
         ),
-        in_specs=specs(1, 6),
-        out_specs=tuple(specs(0, 3)),
-        compiler_params=pltpu.CompilerParams(vmem_limit_bytes=16 << 20),
+        in_specs=specs(2, 5),
+        out_specs=(specs(0, 1)[0], specs(1, 0)[0]),
+        compiler_params=limit(8),
         cost_estimate=pl.CostEstimate(
             flops=2 * seg_local * TILES * samples * 2 * LANES,
             transcendentals=2 * seg_local * TILES * LANES,
             bytes_accessed=4 * seg_local * (3 * TILES * LANES + samples * TV) + 8 * TILES * LANES,
         ),
         name="maps_and_weights",
-    )(first_segment, sensitivity, field_map.T, seg_map.T, sample_rows, jnp.swapaxes(density, 1, 2), turns)
+    )(first_segment, core, sensitivity, field_map, seg_map, sample_rows, density)
 
 
 def apply_normal(core, steps, directions, tables):
     half = jax.ShapeDtypeStruct((TILES // 2, LANES), jnp.float32)
-    segments = tables[0].shape[0]
+    segments = (tables[0].shape[0] - 2) // 3
     return pl.pallas_call(
         functools.partial(normal_kernel, len(steps) > 0),
         out_shape=(half, half),
-        in_specs=specs(1 + len(steps), len(directions), len(tables)),
+        in_specs=specs(1 + len(steps), len(directions) + len(tables)),
         out_specs=tuple(specs(0, 2)),
         scratch_shapes=[
             pltpu.VMEM((2, TILES, LANES), jnp.float32),
@@ -363,10 +350,8 @@
             pltpu.VMEM((6 * SPAN, BLOCKS * LANES), jnp.bfloat16),
             pltpu.VMEM((2 * SPAN, BLOCKS * LANES), jnp.float32),
             pltpu.VMEM((2, TILES, LANES), jnp.float32),
-        ]
-        + [pltpu.VMEM(table.shape, table.dtype) for table in tables]
-        + [pltpu.SemaphoreType.DMA((5 + 2 * segments,))],
-        compiler_params=pltpu.CompilerParams(vmem_limit_bytes=60 << 20),
+        ],
+        compiler_params=limit(20),
         cost_estimate=pl.CostEstimate(
             flops=12 * segments * TILES * 6 * LANES * 4 * LANES,
             transcendentals=0,
@@ -391,13 +376,10 @@
         out_shape=jax.ShapeDtypeStruct((copies, rows, LANES), jnp.float32),
         in_specs=specs(0, 1),
         out_specs=specs(0, 1)[0],
+        compiler_params=limit(2),
         name="sum_and_copy",
     )(parts.reshape(count, rows, LANES))
     return shared.reshape(copies * rows, LANES)
-
-
-def gather_direction(own_tiles):
-    return exchange(jnp.tile(own_tiles, (DEVICES // 2, 1)), SAME_CORE)
 
 
 def sum_to_owners(keep, send):
@@ -418,6 +400,7 @@
         out_shape=(own, own),
         in_specs=specs(2, 3),
         out_specs=tuple(specs(0, 2)),
+        compiler_params=limit(2),
         name="last_update",
     )(step_alpha, step_beta, parts.reshape(-1, 2 * right_side.shape[0], LANES), right_side, own_sum)
 
@@ -428,14 +411,19 @@
     seg_local = sample_rows.shape[0]
     first_segment = lax.axis_index(("y", "core")) * seg_local
     core = lax.axis_index("core").reshape(1)
-    row_ahead, row_back, column_ahead, column_back, turns = map(jnp.asarray, transform_constants())
-    gathered = gather_direction(right_side)
-    maps, weights, twist = prepare(
-        first_segment.reshape(1), sensitivity, field_map, seg_map, sample_rows, density, turns
-    )
-    gathered, maps, weights, twist = lax.optimization_barrier((gathered, maps, weights, twist))
-    gathered = (gathered, swap_cores(gathered))
-    tables = (maps, weights, twist, row_ahead, row_back, column_ahead, column_back)
+    mine = exchange(jnp.tile(right_side, (DEVICES // 2, 1)), SAME_CORE)
+    tables, core = prepare(
+        first_segment.reshape(1),
+        core,
+        sensitivity,
+        field_map.T,
+        seg_map.T,
+        sample_rows,
+        jnp.swapaxes(density, 1, 2),
+    )
+    mine, core = lax.optimization_barrier((mine, core))
+    gathered = (mine, swap_cores(mine))
+    tables = (tables, jnp.asarray(transform_constants()))
     sums = sum_for_all(*apply_normal(core, (), gathered, tables))
     own_tiles = right_side.shape[0]
     own_start = lax.axis_index(SAME_CORE) * own_tiles

time: 139 us -> 125 us (0.90)
  Pallas kernels: 36.3 us -> 27.5 us
  local copies, waits for them, and re-layouts: 14 us -> 11.3 us
  other arithmetic: 2.69 us -> 0.76 us
  blocking collectives: 38.9 us -> 37 us
    pallas_call x2, Pallas kernels: 25.6 us -> 19.3 us  [apply_normal(): pl.pallas_call(functools.partial(normal_kernel, len(steps) > 0), out_shap...]
    pallas_call x2, Pallas kernels: 3.26 us -> 0.05 us  [share(): pl.pallas_call(share_kernel, out_shape=jax.ShapeDtypeStruct((copies, rows...]
    all_to_all x3, blocking collectives: 38.9 us -> 37 us  [exchange(): return lax.all_to_all(value, axes, 0, 0, tiled=True)]
    unnamed x28 -> x22, local copies, waits for them, and re-layouts: 11.4 us -> 9.88 us
  transfers between devices with their start and end apart: 6 -> 6, of which waited for: 5 -> 5; matrix products, arithmetic and copies ran while one was open for 1% -> 0% of each run, Pallas kernels for 4% -> 6%
where the time goes in v5:
time: 125 us
  blocking collectives  37 us (30%)
  starting transfers between devices  29.4 us (24%)
  Pallas kernels  27.5 us (22%)
  waiting for transfers between devices  18.1 us (14%)
  local copies, waits for them, and re-layouts  11.3 us (9%)
    all_to_all x3, blocking collectives, exchange(): return lax.all_to_all(value, axes, 0, 0, tiled=True)  37 us
    all_to_all x2, starting transfers between devices, exchange(): return lax.all_to_all(value, axes, 0, 0, tiled=True)  22.5 us
    pallas_call x2, Pallas kernels, apply_normal(): pl.pallas_call(functools.partial(normal_kernel, len(steps) > 0), out_shap...  19.3 us
    all_to_all x2, waiting for transfers between devices, exchange(): return lax.all_to_all(value, axes, 0, 0, tiled=True)  13.5 us
    unnamed x22, local copies, waits for them, and re-layouts  9.88 us
    pallas_call x1, Pallas kernels, prepare(): pl.pallas_call(prepare_kernel, out_shape=(jax.ShapeDtypeStruct((3 * seg_l...  6.94 us
    ppermute x4, starting transfers between devices, swap_cores(): return lax.ppermute(value, 'core', [(0, 1), (1, 0)])  6.88 us
    ppermute x4, waiting for transfers between devices, swap_cores(): return lax.ppermute(value, 'core', [(0, 1), (1, 0)])  4.65 us
  transfers between devices with their start and end apart: 6, of which 5 were waited for; matrix products, arithmetic and copies ran while one was open for 0% of the time, Pallas kernels for 6%

profile of v5, /device:TPU:1, one launch (start us, length us, event | category | flops | bytes accessed | tf_op | source)
XLA Modules:
  0.0 124.9 jit_solution(15634419128073583900)
XLA Ops:
  0.6 1.4 %tile.2 = f32[128,4,128]{2,1,0:T(4,128)} broadcast(f32[4,128]{1,0:T(4,128)} %right_ref.1), dimensions={1,2} | broadcast | bytes 264192 | tf_op jit(solution)/shard_map/tile | solution.py:414
  2.0 16.3 %all-to-all-start = ((f32[128,4,128]{2,1,0:T(4,128)}), f32[128,4,128]{2,1,0:T(4,128)S(1)}, u32[]{:S(2)}, u32[]{:S(2)}) async-start(f32[128,4,128]{2,1,0:T(4,128)} %tile.2), calls=%async_computation | async-start | bytes 524288 | tf_op jit(solution)/shard_map/all_to_all | solution.py:369
  18.4 0.0 copy-start.3
  18.4 1.2 copy-done.3
  19.6 0.0 copy-start.4
  19.6 1.1 copy-done.4
  20.8 0.0 copy-start.5
  20.8 0.9 copy-done.5
  21.7 0.0 copy-start.6
  21.7 0.7 copy-done.6
  22.4 0.0 copy-start.7
  22.4 0.7 copy-done.7
  23.1 0.0 copy-start.8
  23.1 6.9 %maps_and_weights.1 = (f32[11,1024,128]{2,1,0:T(8,128)S(1)}, s32[1]{0:T(128)}) custom-call(s32[1]{0:T(128)} %bitcast.1.first_ref, s32[1]{0:T(128)} %bitcast.2.core_ref, f32[2,1024,128]{2,1,0:T(8,128)S(1)} %copy-done.3, f32[64,1024]{1,0:T(8,128)S(1)} %bitcast.18, s32[4,1024]{1,0:T(4,128)S(1)} %bitcast.19, s32[3,1024]{1,0:T(4,128)S(1)} %copy-done.7, ...), custom_call_target="tpu_custom_call" | custom-call | flops 1610612736 | bytes 6553600 | tf_op jit(solution)/shard_map/maps_and_weights/pallas_call | solution.py:319
  30.1 0.0 copy-start.9
  30.1 2.5 %copy-done.9 = f32[11,1024,128]{2,1,0:T(8,128)} copy-done((f32[11,1024,128]{2,1,0:T(8,128)}, f32[11,1024,128]{2,1,0:T(8,128)S(1)}, u32[]{:S(2)}) %copy-start.9) | copy-done | bytes 5767192
  32.6 0.0 all-to-all-done
  32.6 1.5 %collective-permute-start = (f32[512,128]{1,0:T(8,128)S(1)}, f32[512,128]{1,0:T(8,128)S(1)}, u32[]{:S(2)}, u32[]{:S(2)}) collective-permute-start(f32[512,128]{1,0:T(8,128)S(1)} %bitcast.14), channel_id=1, source_target_pairs={{0,32},{32,0},{1,33},{33,1},{2,34},{34,2},{3,35},{35,3},{4,36},{36... | collective-permute-start | bytes 786440 | tf_op jit(solution)/shard_map/ppermute | solution.py:365
  34.1 1.2 collective-permute-done.refs_1_.refs_3_
  35.3 0.0 copy-done.8
  35.3 0.0 copy-start.10
  35.3 2.6 %copy-done.10 = f32[11,1024,128]{2,1,0:T(8,128)S(1)} copy-done((f32[11,1024,128]{2,1,0:T(8,128)S(1)}, f32[11,1024,128]{2,1,0:T(8,128)}, u32[]{:S(2)}) %copy-start.10) | copy-done | bytes 5767192
  37.9 0.0 copy-start.1
  37.9 0.0 copy-start.2
  37.9 9.4 %apply_normal.2 = (f32[512,128]{1,0:T(8,128)S(1)}, f32[512,128]{1,0:T(8,128)S(1)}) custom-call(s32[1]{0:T(128)} %get-tuple-element.11.core_ref, f32[512,128]{1,0:T(8,128)S(1)} %bitcast.15, f32[512,128]{1,0:T(8,128)S(1)} %collective-permute-done.refs_1_.refs_3_, f32[11,1024,128]{2,1,0:T(8,128)S(1)} %copy-done.10, bf16[256,2048]{1,0:T(8,128)(2,1)S(1)} %copy-done.8), custom_call_target="tpu_custom_call" | custom-call | flops 14495514624 | bytes 6291456 | tf_op jit(solution)/shard_map/apply_normal/pallas_call | solution.py:340
  47.3 0.5 collective-permute-start.1
  47.8 1.2 collective-permute-done.1
  49.0 13.9 %all_to_all.41.parts_ref = f32[16,32,128]{2,1,0:T(8,128)S(1)} all-to-all(f32[16,32,128]{2,1,0:T(8,128)S(1)} %bitcast.20), channel_id=1, replica_groups=mesh['y'=4,'core'=2,'x'=4,'z_lo'=4,'z_hi'=2] {'y','x'}, dimensions={0} | all-to-all | bytes 524288 | tf_op jit(solution)/shard_map/all_to_all | solution.py:369
  62.9 13.0 %all_to_all.42.parts_ref = f32[8,32,128]{2,1,0:T(8,128)S(1)} all-to-all(f32[8,32,128]{2,1,0:T(8,128)S(1)} %sum_and_copy.2), channel_id=1, replica_groups=mesh['y'=4,'core'=2,'x'=4,'z_lo'=4,'z_hi'=2] {'z_lo','z_hi'}, dimensions={0} | all-to-all | bytes 262144 | tf_op jit(solution)/shard_map/all_to_all | solution.py:369
  75.9 10.1 %all_to_all.43 = f32[16,32,128]{2,1,0:T(8,128)S(1)} all-to-all(f32[16,32,128]{2,1,0:T(8,128)S(1)} %sum_and_copy.3), channel_id=1, replica_groups=mesh['y'=4,'core'=2,'x'=4,'z_lo'=4,'z_hi'=2] {'y','x'}, dimensions={0} | all-to-all | bytes 524288 | tf_op jit(solution)/shard_map/all_to_all | solution.py:369
  86.1 0.0 copy-start
  86.1 4.5 %collective-permute-start.2 = (f32[512,128]{1,0:T(8,128)S(1)}, f32[512,128]{1,0:T(8,128)S(1)}, u32[]{:S(2)}, u32[]{:S(2)}) collective-permute-start(f32[512,128]{1,0:T(8,128)S(1)} %bitcast.11), channel_id=1, source_target_pairs={{0,32},{32,0},{1,33},{33,1},{2,34},{34,2},{3,35},{35,3},{4,36},{36... | collective-permute-start | bytes 786440 | tf_op jit(solution)/shard_map/ppermute | solution.py:365
  90.5 1.2 collective-permute-done.2.refs_5_
  91.7 0.0 copy-done.1
  91.7 0.0 copy-done.2
  91.7 9.9 %apply_normal.3 = (f32[512,128]{1,0:T(8,128)S(1)}, f32[512,128]{1,0:T(8,128)S(1)}) custom-call(s32[1]{0:T(128)} %get-tuple-element.11.core_ref, f32[2]{0:T(128)S(1)} %copy-done.1, f32[2]{0:T(128)S(1)} %copy-done.2, f32[512,128]{1,0:T(8,128)S(1)} %bitcast.16, f32[512,128]{1,0:T(8,128)S(1)} %collective-permute-done.refs_1_.refs_3_, f32[512,128]{1,0:T(8,128)S(1)} %bitcast.12, ...), custom_call_target="tpu_custom_call" | custom-call | flops 14495514624 | bytes 6291456 | tf_op jit(solution)/shard_map/apply_normal/pallas_call | solution.py:340
  101.7 0.5 collective-permute-start.3
  102.1 1.2 collective-permute-done.3
  103.3 0.7 add.23
  104.0 6.1 %all-to-all-start.4 = ((f32[128,4,128]{2,1,0:T(4,128)}), f32[128,4,128]{2,1,0:T(4,128)S(1)}, u32[]{:S(2)}, u32[]{:S(2)}) async-start(f32[128,4,128]{2,1,0:T(4,128)} %bitcast.8), calls=%async_computation.4 | async-start | bytes 524288 | tf_op jit(solution)/shard_map/all_to_all | solution.py:369
  110.2 13.5 %all-to-all-done.4 = f32[128,4,128]{2,1,0:T(4,128)S(1)} async-done(((f32[128,4,128]{2,1,0:T(4,128)}), f32[128,4,128]{2,1,0:T(4,128)S(1)}, u32[]{:S(2)}, u32[]{:S(2)}) %all-to-all-start.4) | async-done | bytes 262176 | tf_op jit(solution)/shard_map/all_to_all | solution.py:369
  123.7 0.0 copy-done
  123.7 1.2 last_update.1
  (4 shorter events, 0.1 us)
Async XLA Ops:
  2.0 30.6 %all-to-all-start = ((f32[128,4,128]{2,1,0:T(4,128)}), f32[128,4,128]{2,1,0:T(4,128)S(1)}, u32[]{:S(2)}, u32[]{:S(2)}) async-start(f32[128,4,128]{2,1,0:T(4,128)} %tile.2), calls=%async_computation | async-start | bytes 524288 | tf_op jit(solution)/shard_map/all_to_all | solution.py:369
  18.4 1.2 copy-start.3
  19.6 1.1 copy-start.4
  20.8 0.9 copy-start.5
  21.7 0.7 copy-start.6
  22.4 0.7 copy-start.7
  23.1 12.1 %copy-start.8 = (bf16[256,2048]{1,0:T(8,128)(2,1)S(1)}, bf16[256,2048]{1,0:T(8,128)(2,1)}, u32[]{:S(2)}) copy-start(bf16[256,2048]{1,0:T(8,128)(2,1)} %constant.35.clone.refs_3_.refs_7_) | copy-start | bytes 3145732
  30.1 2.5 %copy-start.9 = (f32[11,1024,128]{2,1,0:T(8,128)}, f32[11,1024,128]{2,1,0:T(8,128)S(1)}, u32[]{:S(2)}) copy-start(f32[11,1024,128]{2,1,0:T(8,128)S(1)} %get-tuple-element.13.refs_2_.refs_6_) | copy-start | bytes 17301508
  32.6 2.7 %collective-permute-start = (f32[512,128]{1,0:T(8,128)S(1)}, f32[512,128]{1,0:T(8,128)S(1)}, u32[]{:S(2)}, u32[]{:S(2)}) collective-permute-start(f32[512,128]{1,0:T(8,128)S(1)} %bitcast.14), channel_id=1, source_target_pairs={{0,32},{32,0},{1,33},{33,1},{2,34},{34,2},{3,35},{35,3},{4,36},{36... | collective-permute-start | bytes 786440 | tf_op jit(solution)/shard_map/ppermute | solution.py:365
  35.3 2.6 %copy-start.10 = (f32[11,1024,128]{2,1,0:T(8,128)S(1)}, f32[11,1024,128]{2,1,0:T(8,128)}, u32[]{:S(2)}) copy-start(f32[11,1024,128]{2,1,0:T(8,128)} %copy-done.9) | copy-start | bytes 17301508
  37.9 53.8 %copy-start.1 = (f32[2]{0:T(128)S(1)}, f32[2]{0:T(128)}, u32[]{:S(2)}) copy-start(f32[2]{0:T(128)} %alpha_ref.1) | copy-start | bytes 28
  37.9 53.8 %copy-start.2 = (f32[2]{0:T(128)S(1)}, f32[2]{0:T(128)}, u32[]{:S(2)}) copy-start(f32[2]{0:T(128)} %beta_ref.1) | copy-start | bytes 28
  47.3 1.6 %collective-permute-start.1 = (f32[512,128]{1,0:T(8,128)S(1)}, f32[512,128]{1,0:T(8,128)S(1)}, u32[]{:S(2)}, u32[]{:S(2)}) collective-permute-start(f32[512,128]{1,0:T(8,128)S(1)} %get-tuple-element.15), channel_id=1, source_target_pairs={{0,32},{32,0},{1,33},{33,1},{2,34},{34,2},{3,35},{35,3},{4,36},{36... | collective-permute-start | bytes 786440 | tf_op jit(solution)/shard_map/ppermute | solution.py:365
  86.1 37.6 %copy-start = (f32[4,128]{1,0:T(4,128)S(1)}, f32[4,128]{1,0:T(4,128)}, u32[]{:S(2)}) copy-start(f32[4,128]{1,0:T(4,128)} %right_ref.1) | copy-start | bytes 6148
  86.1 5.6 %collective-permute-start.2 = (f32[512,128]{1,0:T(8,128)S(1)}, f32[512,128]{1,0:T(8,128)S(1)}, u32[]{:S(2)}, u32[]{:S(2)}) collective-permute-start(f32[512,128]{1,0:T(8,128)S(1)} %bitcast.11), channel_id=1, source_target_pairs={{0,32},{32,0},{1,33},{33,1},{2,34},{34,2},{3,35},{35,3},{4,36},{36... | collective-permute-start | bytes 786440 | tf_op jit(solution)/shard_map/ppermute | solution.py:365
  101.7 1.6 %collective-permute-start.3 = (f32[512,128]{1,0:T(8,128)S(1)}, f32[512,128]{1,0:T(8,128)S(1)}, u32[]{:S(2)}, u32[]{:S(2)}) collective-permute-start(f32[512,128]{1,0:T(8,128)S(1)} %get-tuple-element.17), channel_id=1, source_target_pairs={{0,32},{32,0},{1,33},{33,1},{2,34},{34,2},{3,35},{35,3},{4,36},{36... | collective-permute-start | bytes 786440 | tf_op jit(solution)/shard_map/ppermute | solution.py:365
  104.0 19.7 %all-to-all-start.4 = ((f32[128,4,128]{2,1,0:T(4,128)}), f32[128,4,128]{2,1,0:T(4,128)S(1)}, u32[]{:S(2)}, u32[]{:S(2)}) async-start(f32[128,4,128]{2,1,0:T(4,128)} %bitcast.8), calls=%async_computation.4 | async-start | bytes 524288 | tf_op jit(solution)/shard_map/all_to_all | solution.py:369

commit v6 on v5

--- a/solution.py
+++ b/solution.py
@@ -120,13 +120,13 @@
     core_out_ref[0] = core_ref[0]
     seg_local = rows_ref.shape[0]
     maps_ref, weights_ref, twist_ref = table_parts(tables_ref)
-    lane = lax.broadcasted_iota(jnp.int32, (SPAN, LANES), 0).astype(jnp.float32)
+    lane = lax.broadcasted_iota(jnp.int32, (BLOCKS, SPAN), 1).astype(jnp.float32)
+    turn = lax.broadcasted_iota(jnp.int32, (BLOCKS, SPAN), 0).astype(jnp.float32)
+    twist_cosine, twist_sine = cosine_sine(lane * turn * (2.0 * math.pi / TILES))
     for block in range(BLOCKS):
         at = pl.ds(block * SPAN, SPAN)
-        if block > 0:
-            twist_cosine, twist_sine = cosine_sine(lane * (2.0 * math.pi * block / TILES))
-            twist_ref[0, at, :] = twist_cosine
-            twist_ref[1, at, :] = -twist_sine
+        for part, value in enumerate((twist_cosine, -twist_sine)):
+            twist_ref[part, at, :] = jnp.broadcast_to(value[block : block + 1, :], (LANES, SPAN)).T
         field = field_ref[:, at]
         field = jnp.concatenate([field, field], axis=0).T
         named = seg_map_ref[:, at]
@@ -324,7 +324,7 @@
         ),
         in_specs=specs(2, 5),
         out_specs=(specs(0, 1)[0], specs(1, 0)[0]),
-        compiler_params=limit(8),
+        compiler_params=limit(60),
         cost_estimate=pl.CostEstimate(
             flops=2 * seg_local * TILES * samples * 2 * LANES,
             transcendentals=2 * seg_local * TILES * LANES,

time: 125 us -> 121 us (0.968)
  local copies, waits for them, and re-layouts: 11.3 us -> 4.18 us
  blocking collectives: 37 us -> 33.1 us
  waiting for transfers between devices: 18.1 us -> 21.2 us
  Pallas kernels: 27.5 us -> 30.4 us
    unnamed x22 -> x10, local copies, waits for them, and re-layouts: 9.88 us -> 2.65 us
    all_to_all x3, blocking collectives: 37 us -> 33.1 us  [exchange(): return lax.all_to_all(value, axes, 0, 0, tiled=True)]
    all_to_all x2, waiting for transfers between devices: 13.5 us -> 16.5 us  [exchange(): return lax.all_to_all(value, axes, 0, 0, tiled=True)]
    pallas_call x1, Pallas kernels: 6.94 us -> 9.92 us  [prepare(): pl.pallas_call(prepare_kernel, out_shape=(jax.ShapeDtypeStruct((3 * seg_l...]
  transfers between devices with their start and end apart: 6 -> 6, of which waited for: 5 -> 6; matrix products, arithmetic and copies ran while one was open for 0% -> 0% of each run, Pallas kernels for 6% -> 8%
where the time goes in v6:
time: 121 us
  blocking collectives  33.1 us (27%)
  starting transfers between devices  30.6 us (25%)
  Pallas kernels  30.4 us (25%)
  waiting for transfers between devices  21.2 us (18%)
  local copies, waits for them, and re-layouts  4.18 us (3%)
    all_to_all x3, blocking collectives, exchange(): return lax.all_to_all(value, axes, 0, 0, tiled=True)  33.1 us
    all_to_all x2, starting transfers between devices, exchange(): return lax.all_to_all(value, axes, 0, 0, tiled=True)  22.5 us
    pallas_call x2, Pallas kernels, apply_normal(): pl.pallas_call(functools.partial(normal_kernel, len(steps) > 0), out_shap...  19.2 us
    all_to_all x2, waiting for transfers between devices, exchange(): return lax.all_to_all(value, axes, 0, 0, tiled=True)  16.5 us
    pallas_call x1, Pallas kernels, prepare(): pl.pallas_call(prepare_kernel, out_shape=(jax.ShapeDtypeStruct((3 * seg_l...  9.92 us
    ppermute x4, starting transfers between devices, swap_cores(): return lax.ppermute(value, 'core', [(0, 1), (1, 0)])  8.13 us
    ppermute x4, waiting for transfers between devices, swap_cores(): return lax.ppermute(value, 'core', [(0, 1), (1, 0)])  4.65 us
    unnamed x10, local copies, waits for them, and re-layouts  2.65 us
  transfers between devices with their start and end apart: 6, of which 6 were waited for; matrix products, arithmetic and copies ran while one was open for 0% of the time, Pallas kernels for 8%

profile of v6, /device:TPU:1, one launch (start us, length us, event | category | flops | bytes accessed | tf_op | source)
XLA Modules:
  0.0 120.9 jit_solution(5988525644404344662)
XLA Ops:
  0.6 0.0 copy-start.3
  0.6 1.5 %tile.2 = f32[128,4,128]{2,1,0:T(4,128)} broadcast(f32[4,128]{1,0:T(4,128)} %right_ref.1), dimensions={1,2} | broadcast | bytes 264192 | tf_op jit(solution)/shard_map/tile | solution.py:414
  2.2 16.3 %all-to-all-start = ((f32[128,4,128]{2,1,0:T(4,128)}), f32[128,4,128]{2,1,0:T(4,128)S(1)}, u32[]{:S(2)}, u32[]{:S(2)}) async-start(f32[128,4,128]{2,1,0:T(4,128)} %tile.2), calls=%async_computation | async-start | bytes 524288 | tf_op jit(solution)/shard_map/all_to_all | solution.py:369
  18.5 9.9 %maps_and_weights.1 = (f32[11,1024,128]{2,1,0:T(8,128)}, s32[1]{0:T(128)}) custom-call(s32[1]{0:T(128)} %bitcast.1.first_ref, s32[1]{0:T(128)} %bitcast.2.core_ref, f32[2,1024,128]{2,1,0:T(8,128)} %sens_ref.1, f32[64,1024]{1,0:T(8,128)} %bitcast.19, s32[4,1024]{1,0:T(4,128)} %bitcast.20, s32[3,1024]{1,0:T(4,128)} %rows_ref.1, f32[3,64,1024]{2,1,0:T(8,128)} %bitcast.18), custom_call_target="tpu_custom_call" | custom-call | flops 1610612736 | bytes 6553600 | tf_op jit(solution)/shard_map/maps_and_weights/pallas_call | solution.py:319
  28.4 3.0 %all-to-all-done = f32[128,4,128]{2,1,0:T(4,128)S(1)} async-done(((f32[128,4,128]{2,1,0:T(4,128)}), f32[128,4,128]{2,1,0:T(4,128)S(1)}, u32[]{:S(2)}, u32[]{:S(2)}) %all-to-all-start) | async-done | bytes 262176 | tf_op jit(solution)/shard_map/all_to_all | solution.py:369
  31.5 2.8 %collective-permute-start = (f32[512,128]{1,0:T(8,128)S(1)}, f32[512,128]{1,0:T(8,128)S(1)}, u32[]{:S(2)}, u32[]{:S(2)}) collective-permute-start(f32[512,128]{1,0:T(8,128)S(1)} %bitcast.14), channel_id=1, source_target_pairs={{0,32},{32,0},{1,33},{33,1},{2,34},{34,2},{3,35},{35,3},{4,36},{36... | collective-permute-start | bytes 786440 | tf_op jit(solution)/shard_map/ppermute | solution.py:365
  34.2 1.2 collective-permute-done.refs_1_.refs_3_
  35.4 0.0 copy-done.3
  35.4 0.0 copy-start.4
  35.4 2.6 %copy-done.4 = f32[11,1024,128]{2,1,0:T(8,128)S(1)} copy-done((f32[11,1024,128]{2,1,0:T(8,128)S(1)}, f32[11,1024,128]{2,1,0:T(8,128)}, u32[]{:S(2)}) %copy-start.4) | copy-done | bytes 5767192
  38.0 0.0 copy-start.1
  38.0 0.0 copy-start.2
  38.0 9.4 %apply_normal.2 = (f32[512,128]{1,0:T(8,128)S(1)}, f32[512,128]{1,0:T(8,128)S(1)}) custom-call(s32[1]{0:T(128)} %get-tuple-element.11.core_ref, f32[512,128]{1,0:T(8,128)S(1)} %bitcast.15, f32[512,128]{1,0:T(8,128)S(1)} %collective-permute-done.refs_1_.refs_3_, f32[11,1024,128]{2,1,0:T(8,128)S(1)} %copy-done.4, bf16[256,2048]{1,0:T(8,128)(2,1)S(1)} %copy-done.3), custom_call_target="tpu_custom_call" | custom-call | flops 14495514624 | bytes 6291456 | tf_op jit(solution)/shard_map/apply_normal/pallas_call | solution.py:340
  47.4 0.5 collective-permute-start.1
  47.8 1.2 collective-permute-done.1
  49.0 10.9 %all_to_all.41.parts_ref = f32[16,32,128]{2,1,0:T(8,128)S(1)} all-to-all(f32[16,32,128]{2,1,0:T(8,128)S(1)} %bitcast.17), channel_id=1, replica_groups=mesh['y'=4,'core'=2,'x'=4,'z_lo'=4,'z_hi'=2] {'y','x'}, dimensions={0} | all-to-all | bytes 524288 | tf_op jit(solution)/shard_map/all_to_all | solution.py:369
  60.0 12.0 %all_to_all.42.parts_ref = f32[8,32,128]{2,1,0:T(8,128)S(1)} all-to-all(f32[8,32,128]{2,1,0:T(8,128)S(1)} %sum_and_copy.2), channel_id=1, replica_groups=mesh['y'=4,'core'=2,'x'=4,'z_lo'=4,'z_hi'=2] {'z_lo','z_hi'}, dimensions={0} | all-to-all | bytes 262144 | tf_op jit(solution)/shard_map/all_to_all | solution.py:369
  72.0 10.1 %all_to_all.43 = f32[16,32,128]{2,1,0:T(8,128)S(1)} all-to-all(f32[16,32,128]{2,1,0:T(8,128)S(1)} %sum_and_copy.3), channel_id=1, replica_groups=mesh['y'=4,'core'=2,'x'=4,'z_lo'=4,'z_hi'=2] {'y','x'}, dimensions={0} | all-to-all | bytes 524288 | tf_op jit(solution)/shard_map/all_to_all | solution.py:369
  82.2 0.0 copy-start
  82.2 4.5 %collective-permute-start.2 = (f32[512,128]{1,0:T(8,128)S(1)}, f32[512,128]{1,0:T(8,128)S(1)}, u32[]{:S(2)}, u32[]{:S(2)}) collective-permute-start(f32[512,128]{1,0:T(8,128)S(1)} %bitcast.11), channel_id=1, source_target_pairs={{0,32},{32,0},{1,33},{33,1},{2,34},{34,2},{3,35},{35,3},{4,36},{36... | collective-permute-start | bytes 786440 | tf_op jit(solution)/shard_map/ppermute | solution.py:365
  86.6 1.2 collective-permute-done.2.refs_5_
  87.8 0.0 copy-done.1
  87.8 0.0 copy-done.2
  87.8 9.9 %apply_normal.3 = (f32[512,128]{1,0:T(8,128)S(1)}, f32[512,128]{1,0:T(8,128)S(1)}) custom-call(s32[1]{0:T(128)} %get-tuple-element.11.core_ref, f32[2]{0:T(128)S(1)} %copy-done.1, f32[2]{0:T(128)S(1)} %copy-done.2, f32[512,128]{1,0:T(8,128)S(1)} %bitcast.16, f32[512,128]{1,0:T(8,128)S(1)} %collective-permute-done.refs_1_.refs_3_, f32[512,128]{1,0:T(8,128)S(1)} %bitcast.12, ...), custom_call_target="tpu_custom_call" | custom-call | flops 14495514624 | bytes 6291456 | tf_op jit(solution)/shard_map/apply_normal/pallas_call | solution.py:340
  97.7 0.5 collective-permute-start.3
  98.1 1.2 collective-permute-done.3
  99.3 0.7 add.23
  100.0 6.2 %all-to-all-start.4 = ((f32[128,4,128]{2,1,0:T(4,128)}), f32[128,4,128]{2,1,0:T(4,128)S(1)}, u32[]{:S(2)}, u32[]{:S(2)}) async-start(f32[128,4,128]{2,1,0:T(4,128)} %bitcast.8), calls=%async_computation.4 | async-start | bytes 524288 | tf_op jit(solution)/shard_map/all_to_all | solution.py:369
  106.2 13.5 %all-to-all-done.4 = f32[128,4,128]{2,1,0:T(4,128)S(1)} async-done(((f32[128,4,128]{2,1,0:T(4,128)}), f32[128,4,128]{2,1,0:T(4,128)S(1)}, u32[]{:S(2)}, u32[]{:S(2)}) %all-to-all-start.4) | async-done | bytes 262176 | tf_op jit(solution)/shard_map/all_to_all | solution.py:369
  119.7 0.0 copy-done
  119.7 1.2 last_update.1
  (4 shorter events, 0.1 us)
Async XLA Ops:
  0.6 34.8 %copy-start.3 = (bf16[256,2048]{1,0:T(8,128)(2,1)S(1)}, bf16[256,2048]{1,0:T(8,128)(2,1)}, u32[]{:S(2)}) copy-start(bf16[256,2048]{1,0:T(8,128)(2,1)} %constant.35.clone.refs_3_.refs_7_) | copy-start | bytes 3145732
  2.2 29.3 %all-to-all-start = ((f32[128,4,128]{2,1,0:T(4,128)}), f32[128,4,128]{2,1,0:T(4,128)S(1)}, u32[]{:S(2)}, u32[]{:S(2)}) async-start(f32[128,4,128]{2,1,0:T(4,128)} %tile.2), calls=%async_computation | async-start | bytes 524288 | tf_op jit(solution)/shard_map/all_to_all | solution.py:369
  31.5 3.9 %collective-permute-start = (f32[512,128]{1,0:T(8,128)S(1)}, f32[512,128]{1,0:T(8,128)S(1)}, u32[]{:S(2)}, u32[]{:S(2)}) collective-permute-start(f32[512,128]{1,0:T(8,128)S(1)} %bitcast.14), channel_id=1, source_target_pairs={{0,32},{32,0},{1,33},{33,1},{2,34},{34,2},{3,35},{35,3},{4,36},{36... | collective-permute-start | bytes 786440 | tf_op jit(solution)/shard_map/ppermute | solution.py:365
  35.4 2.6 %copy-start.4 = (f32[11,1024,128]{2,1,0:T(8,128)S(1)}, f32[11,1024,128]{2,1,0:T(8,128)}, u32[]{:S(2)}) copy-start(f32[11,1024,128]{2,1,0:T(8,128)} %get-tuple-element.13.refs_2_.refs_6_) | copy-start | bytes 17301508
  38.0 49.8 %copy-start.1 = (f32[2]{0:T(128)S(1)}, f32[2]{0:T(128)}, u32[]{:S(2)}) copy-start(f32[2]{0:T(128)} %alpha_ref.1) | copy-start | bytes 28
  38.0 49.8 %copy-start.2 = (f32[2]{0:T(128)S(1)}, f32[2]{0:T(128)}, u32[]{:S(2)}) copy-start(f32[2]{0:T(128)} %beta_ref.1) | copy-start | bytes 28
  47.4 1.6 %collective-permute-start.1 = (f32[512,128]{1,0:T(8,128)S(1)}, f32[512,128]{1,0:T(8,128)S(1)}, u32[]{:S(2)}, u32[]{:S(2)}) collective-permute-start(f32[512,128]{1,0:T(8,128)S(1)} %get-tuple-element.15), channel_id=1, source_target_pairs={{0,32},{32,0},{1,33},{33,1},{2,34},{34,2},{3,35},{35,3},{4,36},{36... | collective-permute-start | bytes 786440 | tf_op jit(solution)/shard_map/ppermute | solution.py:365
  82.2 37.6 %copy-start = (f32[4,128]{1,0:T(4,128)S(1)}, f32[4,128]{1,0:T(4,128)}, u32[]{:S(2)}) copy-start(f32[4,128]{1,0:T(4,128)} %right_ref.1) | copy-start | bytes 6148
  82.2 5.6 %collective-permute-start.2 = (f32[512,128]{1,0:T(8,128)S(1)}, f32[512,128]{1,0:T(8,128)S(1)}, u32[]{:S(2)}, u32[]{:S(2)}) collective-permute-start(f32[512,128]{1,0:T(8,128)S(1)} %bitcast.11), channel_id=1, source_target_pairs={{0,32},{32,0},{1,33},{33,1},{2,34},{34,2},{3,35},{35,3},{4,36},{36... | collective-permute-start | bytes 786440 | tf_op jit(solution)/shard_map/ppermute | solution.py:365
  97.7 1.6 %collective-permute-start.3 = (f32[512,128]{1,0:T(8,128)S(1)}, f32[512,128]{1,0:T(8,128)S(1)}, u32[]{:S(2)}, u32[]{:S(2)}) collective-permute-start(f32[512,128]{1,0:T(8,128)S(1)} %get-tuple-element.17), channel_id=1, source_target_pairs={{0,32},{32,0},{1,33},{33,1},{2,34},{34,2},{3,35},{35,3},{4,36},{36... | collective-permute-start | bytes 786440 | tf_op jit(solution)/shard_map/ppermute | solution.py:365
  100.0 19.7 %all-to-all-start.4 = ((f32[128,4,128]{2,1,0:T(4,128)}), f32[128,4,128]{2,1,0:T(4,128)S(1)}, u32[]{:S(2)}, u32[]{:S(2)}) async-start(f32[128,4,128]{2,1,0:T(4,128)} %bitcast.8), calls=%async_computation.4 | async-start | bytes 524288 | tf_op jit(solution)/shard_map/all_to_all | solution.py:369

commit v7 on v6

--- a/solution.py
+++ b/solution.py
@@ -194,10 +194,22 @@
     maps_ref, weights_ref, twist_ref = table_parts(tables_ref)
     segments = weights_ref.shape[0]
 
-    def transform(which, axis):
-        high = transforms_ref[:, pl.ds(4 * SPAN * which, 2 * SPAN)]
-        low = transforms_ref[:, pl.ds(4 * SPAN * which + 2 * SPAN, 2 * SPAN)]
-        return jnp.concatenate([high, low, high] if axis == 1 else [high, high, low], axis=axis)
+    def three_passes(which, data, data_left):
+        matrix_high = transforms_ref[:, pl.ds(4 * SPAN * which, 2 * SPAN)]
+        matrix_low = transforms_ref[:, pl.ds(4 * SPAN * which + 2 * SPAN, 2 * SPAN)]
+
+        def product(matrix, value):
+            pair = (value, matrix) if data_left else (matrix, value)
+            return jnp.dot(*pair, preferred_element_type=jnp.float32)
+
+        high, low = data
+        return product(matrix_high, high) + product(matrix_low, high) + product(matrix_high, low)
+
+    def halves(ref, index, axis):
+        half = ref.shape[axis] // 2
+        if axis == 0:
+            return ref[pl.ds(0, half), index], ref[pl.ds(half, half), index]
+        return ref[index, pl.ds(0, half)], ref[index, pl.ds(half, half)]
 
     core = core_ref[0]
     first_half = lax.broadcasted_iota(jnp.int32, (SPAN, LANES), 1) < TV
@@ -233,41 +245,35 @@
                     high, low = split(value)
                     start = part * SPAN + chunk * CHUNK
                     turned[pl.ds(start, CHUNK), lanes] = high
-                    turned[pl.ds(2 * SPAN + start, CHUNK), lanes] = high
-                    turned[pl.ds(4 * SPAN + start, CHUNK), lanes] = low
+                    turned[pl.ds(2 * SPAN + start, CHUNK), lanes] = low
         for pair in range(BLOCKS // 2):
-            grid = jnp.dot(
-                transform(0, 1), turned[:, pl.ds(pair * 2 * LANES, 2 * LANES)], preferred_element_type=jnp.float32
-            )
+            grid = three_passes(0, halves(turned, pl.ds(pair * 2 * LANES, 2 * LANES), 0), False)
             for side in range(2):
                 rows = pl.ds((2 * pair + side) * SPAN, SPAN)
                 for part in range(2):
                     high, low = split(grid[part * SPAN : (part + 1) * SPAN, side * LANES : (side + 1) * LANES])
                     left[rows, pl.ds(part * LANES, LANES)] = high
                     left[rows, pl.ds((2 + part) * LANES, LANES)] = low
-                    left[rows, pl.ds((4 + part) * LANES, LANES)] = high
         for pair in range(BLOCKS // 2):
             rows = pl.ds(pair * 2 * SPAN, 2 * SPAN)
-            kspace = jnp.dot(left[rows, :], transform(2, 0), preferred_element_type=jnp.float32)
+            kspace = three_passes(2, halves(left, rows, 1), True)
             weights = weights_ref[segment, rows, :]
             high, low = split(kspace * jnp.concatenate([weights, weights], axis=1))
             left_back[rows, pl.ds(0, 2 * LANES)] = high
             left_back[rows, pl.ds(2 * LANES, 2 * LANES)] = low
-            left_back[rows, pl.ds(4 * LANES, 2 * LANES)] = high
         for pair in range(BLOCKS // 2):
             rows = pl.ds(pair * 2 * SPAN, 2 * SPAN)
-            grid = jnp.dot(left_back[rows, :], transform(3, 0), preferred_element_type=jnp.float32)
+            grid = three_passes(3, halves(left_back, rows, 1), True)
             high, low = split(grid)
             for side in range(2):
                 lanes = pl.ds((2 * pair + side) * LANES, LANES)
                 for part in range(2):
                     piece = (slice(side * SPAN, (side + 1) * SPAN), slice(part * LANES, (part + 1) * LANES))
                     right[pl.ds(part * SPAN, SPAN), lanes] = high[piece]
-                    right[pl.ds((2 + part) * SPAN, SPAN), lanes] = high[piece]
-                    right[pl.ds((4 + part) * SPAN, SPAN), lanes] = low[piece]
+                    right[pl.ds((2 + part) * SPAN, SPAN), lanes] = low[piece]
         for pair in range(BLOCKS // 2):
             lanes = pl.ds(pair * 2 * LANES, 2 * LANES)
-            back[:, lanes] = jnp.dot(transform(1, 1), right[:, lanes], preferred_element_type=jnp.float32)
+            back[:, lanes] = three_passes(1, halves(right, lanes, 0), False)
         for chunk in range(SPAN // CHUNK):
             real, imag = [], []
             for block in range(BLOCKS):
@@ -344,10 +350,10 @@
         out_specs=tuple(specs(0, 2)),
         scratch_shapes=[
             pltpu.VMEM((2, TILES, LANES), jnp.float32),
-            pltpu.VMEM((6 * SPAN, BLOCKS * LANES), jnp.bfloat16),
-            pltpu.VMEM((TILES, 6 * LANES), jnp.bfloat16),
-            pltpu.VMEM((TILES, 6 * LANES), jnp.bfloat16),
-            pltpu.VMEM((6 * SPAN, BLOCKS * LANES), jnp.bfloat16),
+            pltpu.VMEM((4 * SPAN, BLOCKS * LANES), jnp.bfloat16),
+            pltpu.VMEM((TILES, 4 * LANES), jnp.bfloat16),
+            pltpu.VMEM((TILES, 4 * LANES), jnp.bfloat16),
+            pltpu.VMEM((4 * SPAN, BLOCKS * LANES), jnp.bfloat16),
             pltpu.VMEM((2 * SPAN, BLOCKS * LANES), jnp.float32),
             pltpu.VMEM((2, TILES, LANES), jnp.float32),
         ],

time: 121 us -> 121 us (level)
  no operation moved by 1% of the time
where the time goes in v7:
time: 121 us; the launch traced here: 120 us
  blocking collectives  33.1 us (27%)
  starting transfers between devices  30.8 us (25%)
  Pallas kernels  29.4 us (24%)
  waiting for transfers between devices  21.5 us (18%)
  local copies, waits for them, and re-layouts  4.18 us (3%)
    all_to_all x3, blocking collectives, exchange(): return lax.all_to_all(value, axes, 0, 0, tiled=True)  33.1 us
    all_to_all x2, starting transfers between devices, exchange(): return lax.all_to_all(value, axes, 0, 0, tiled=True)  22.5 us
    pallas_call x2, Pallas kernels, apply_normal(): pl.pallas_call(functools.partial(normal_kernel, len(steps) > 0), out_shap...  18.2 us
    all_to_all x2, waiting for transfers between devices, exchange(): return lax.all_to_all(value, axes, 0, 0, tiled=True)  16.8 us
    pallas_call x1, Pallas kernels, prepare(): pl.pallas_call(prepare_kernel, out_shape=(jax.ShapeDtypeStruct((3 * seg_l...  9.92 us
    ppermute x4, starting transfers between devices, swap_cores(): return lax.ppermute(value, 'core', [(0, 1), (1, 0)])  8.26 us
    ppermute x4, waiting for transfers between devices, swap_cores(): return lax.ppermute(value, 'core', [(0, 1), (1, 0)])  4.65 us
    unnamed x10, local copies, waits for them, and re-layouts  2.65 us
  transfers between devices with their start and end apart: 6, of which 6 were waited for; matrix products, arithmetic and copies ran while one was open for 0% of the time, Pallas kernels for 8%

profile of v7, /device:TPU:1, one launch (start us, length us, event | category | flops | bytes accessed | tf_op | source)
XLA Modules:
  0.0 120.4 jit_solution(6033551942046752323)
XLA Ops:
  0.6 0.0 copy-start.3
  0.6 1.5 %tile.2 = f32[128,4,128]{2,1,0:T(4,128)} broadcast(f32[4,128]{1,0:T(4,128)} %right_ref.1), dimensions={1,2} | broadcast | bytes 264192 | tf_op jit(solution)/shard_map/tile | solution.py:420
  2.2 16.3 %all-to-all-start = ((f32[128,4,128]{2,1,0:T(4,128)}), f32[128,4,128]{2,1,0:T(4,128)S(1)}, u32[]{:S(2)}, u32[]{:S(2)}) async-start(f32[128,4,128]{2,1,0:T(4,128)} %tile.2), calls=%async_computation | async-start | bytes 524288 | tf_op jit(solution)/shard_map/all_to_all | solution.py:375
  18.5 9.9 %maps_and_weights.1 = (f32[11,1024,128]{2,1,0:T(8,128)}, s32[1]{0:T(128)}) custom-call(s32[1]{0:T(128)} %bitcast.1.first_ref, s32[1]{0:T(128)} %bitcast.2.core_ref, f32[2,1024,128]{2,1,0:T(8,128)} %sens_ref.1, f32[64,1024]{1,0:T(8,128)} %bitcast.19, s32[4,1024]{1,0:T(4,128)} %bitcast.20, s32[3,1024]{1,0:T(4,128)} %rows_ref.1, f32[3,64,1024]{2,1,0:T(8,128)} %bitcast.18), custom_call_target="tpu_custom_call" | custom-call | flops 1610612736 | bytes 6553600 | tf_op jit(solution)/shard_map/maps_and_weights/pallas_call | solution.py:325
  28.4 3.0 %all-to-all-done = f32[128,4,128]{2,1,0:T(4,128)S(1)} async-done(((f32[128,4,128]{2,1,0:T(4,128)}), f32[128,4,128]{2,1,0:T(4,128)S(1)}, u32[]{:S(2)}, u32[]{:S(2)}) %all-to-all-start) | async-done | bytes 262176 | tf_op jit(solution)/shard_map/all_to_all | solution.py:375
  31.5 2.8 %collective-permute-start = (f32[512,128]{1,0:T(8,128)S(1)}, f32[512,128]{1,0:T(8,128)S(1)}, u32[]{:S(2)}, u32[]{:S(2)}) collective-permute-start(f32[512,128]{1,0:T(8,128)S(1)} %bitcast.14), channel_id=1, source_target_pairs={{0,32},{32,0},{1,33},{33,1},{2,34},{34,2},{3,35},{35,3},{4,36},{36... | collective-permute-start | bytes 786440 | tf_op jit(solution)/shard_map/ppermute | solution.py:371
  34.2 1.2 collective-permute-done.refs_1_.refs_3_
  35.4 0.0 copy-done.3
  35.4 0.0 copy-start.4
  35.4 2.6 %copy-done.4 = f32[11,1024,128]{2,1,0:T(8,128)S(1)} copy-done((f32[11,1024,128]{2,1,0:T(8,128)S(1)}, f32[11,1024,128]{2,1,0:T(8,128)}, u32[]{:S(2)}) %copy-start.4) | copy-done | bytes 5767192
  38.0 0.0 copy-start.1
  38.0 0.0 copy-start.2
  38.0 8.8 %apply_normal.2 = (f32[512,128]{1,0:T(8,128)S(1)}, f32[512,128]{1,0:T(8,128)S(1)}) custom-call(s32[1]{0:T(128)} %get-tuple-element.11.core_ref, f32[512,128]{1,0:T(8,128)S(1)} %bitcast.15, f32[512,128]{1,0:T(8,128)S(1)} %collective-permute-done.refs_1_.refs_3_, f32[11,1024,128]{2,1,0:T(8,128)S(1)} %copy-done.4, bf16[256,2048]{1,0:T(8,128)(2,1)S(1)} %copy-done.3), custom_call_target="tpu_custom_call" | custom-call | flops 14495514624 | bytes 6291456 | tf_op jit(solution)/shard_map/apply_normal/pallas_call | solution.py:346
  46.9 0.5 collective-permute-start.1
  47.4 1.2 collective-permute-done.1
  48.5 10.9 %all_to_all.41.parts_ref = f32[16,32,128]{2,1,0:T(8,128)S(1)} all-to-all(f32[16,32,128]{2,1,0:T(8,128)S(1)} %bitcast.17), channel_id=1, replica_groups=mesh['y'=4,'core'=2,'x'=4,'z_lo'=4,'z_hi'=2] {'y','x'}, dimensions={0} | all-to-all | bytes 524288 | tf_op jit(solution)/shard_map/all_to_all | solution.py:375
  59.5 12.0 %all_to_all.42.parts_ref = f32[8,32,128]{2,1,0:T(8,128)S(1)} all-to-all(f32[8,32,128]{2,1,0:T(8,128)S(1)} %sum_and_copy.2), channel_id=1, replica_groups=mesh['y'=4,'core'=2,'x'=4,'z_lo'=4,'z_hi'=2] {'z_lo','z_hi'}, dimensions={0} | all-to-all | bytes 262144 | tf_op jit(solution)/shard_map/all_to_all | solution.py:375
  71.5 10.2 %all_to_all.43 = f32[16,32,128]{2,1,0:T(8,128)S(1)} all-to-all(f32[16,32,128]{2,1,0:T(8,128)S(1)} %sum_and_copy.3), channel_id=1, replica_groups=mesh['y'=4,'core'=2,'x'=4,'z_lo'=4,'z_hi'=2] {'y','x'}, dimensions={0} | all-to-all | bytes 524288 | tf_op jit(solution)/shard_map/all_to_all | solution.py:375
  81.7 0.0 copy-start
  81.7 4.6 %collective-permute-start.2 = (f32[512,128]{1,0:T(8,128)S(1)}, f32[512,128]{1,0:T(8,128)S(1)}, u32[]{:S(2)}, u32[]{:S(2)}) collective-permute-start(f32[512,128]{1,0:T(8,128)S(1)} %bitcast.11), channel_id=1, source_target_pairs={{0,32},{32,0},{1,33},{33,1},{2,34},{34,2},{3,35},{35,3},{4,36},{36... | collective-permute-start | bytes 786440 | tf_op jit(solution)/shard_map/ppermute | solution.py:371
  86.3 1.2 collective-permute-done.2.refs_5_
  87.5 0.0 copy-done.1
  87.5 0.0 copy-done.2
  87.5 9.4 %apply_normal.3 = (f32[512,128]{1,0:T(8,128)S(1)}, f32[512,128]{1,0:T(8,128)S(1)}) custom-call(s32[1]{0:T(128)} %get-tuple-element.11.core_ref, f32[2]{0:T(128)S(1)} %copy-done.1, f32[2]{0:T(128)S(1)} %copy-done.2, f32[512,128]{1,0:T(8,128)S(1)} %bitcast.16, f32[512,128]{1,0:T(8,128)S(1)} %collective-permute-done.refs_1_.refs_3_, f32[512,128]{1,0:T(8,128)S(1)} %bitcast.12, ...), custom_call_target="tpu_custom_call" | custom-call | flops 14495514624 | bytes 6291456 | tf_op jit(solution)/shard_map/apply_normal/pallas_call | solution.py:346
  96.8 0.5 collective-permute-start.3
  97.3 1.2 collective-permute-done.3
  98.5 0.7 add.23
  99.2 6.2 %all-to-all-start.4 = ((f32[128,4,128]{2,1,0:T(4,128)}), f32[128,4,128]{2,1,0:T(4,128)S(1)}, u32[]{:S(2)}, u32[]{:S(2)}) async-start(f32[128,4,128]{2,1,0:T(4,128)} %bitcast.8), calls=%async_computation.4 | async-start | bytes 524288 | tf_op jit(solution)/shard_map/all_to_all | solution.py:375
  105.4 13.8 %all-to-all-done.4 = f32[128,4,128]{2,1,0:T(4,128)S(1)} async-done(((f32[128,4,128]{2,1,0:T(4,128)}), f32[128,4,128]{2,1,0:T(4,128)S(1)}, u32[]{:S(2)}, u32[]{:S(2)}) %all-to-all-start.4) | async-done | bytes 262176 | tf_op jit(solution)/shard_map/all_to_all | solution.py:375
  119.2 0.0 copy-done
  119.2 1.2 last_update.1
  (4 shorter events, 0.1 us)
Async XLA Ops:
  0.6 34.8 %copy-start.3 = (bf16[256,2048]{1,0:T(8,128)(2,1)S(1)}, bf16[256,2048]{1,0:T(8,128)(2,1)}, u32[]{:S(2)}) copy-start(bf16[256,2048]{1,0:T(8,128)(2,1)} %constant.35.clone.refs_3_.refs_7_) | copy-start | bytes 3145732
  2.2 29.3 %all-to-all-start = ((f32[128,4,128]{2,1,0:T(4,128)}), f32[128,4,128]{2,1,0:T(4,128)S(1)}, u32[]{:S(2)}, u32[]{:S(2)}) async-start(f32[128,4,128]{2,1,0:T(4,128)} %tile.2), calls=%async_computation | async-start | bytes 524288 | tf_op jit(solution)/shard_map/all_to_all | solution.py:375
  31.5 3.9 %collective-permute-start = (f32[512,128]{1,0:T(8,128)S(1)}, f32[512,128]{1,0:T(8,128)S(1)}, u32[]{:S(2)}, u32[]{:S(2)}) collective-permute-start(f32[512,128]{1,0:T(8,128)S(1)} %bitcast.14), channel_id=1, source_target_pairs={{0,32},{32,0},{1,33},{33,1},{2,34},{34,2},{3,35},{35,3},{4,36},{36... | collective-permute-start | bytes 786440 | tf_op jit(solution)/shard_map/ppermute | solution.py:371
  35.4 2.6 %copy-start.4 = (f32[11,1024,128]{2,1,0:T(8,128)S(1)}, f32[11,1024,128]{2,1,0:T(8,128)}, u32[]{:S(2)}) copy-start(f32[11,1024,128]{2,1,0:T(8,128)} %get-tuple-element.13.refs_2_.refs_6_) | copy-start | bytes 17301508
  38.0 49.5 %copy-start.1 = (f32[2]{0:T(128)S(1)}, f32[2]{0:T(128)}, u32[]{:S(2)}) copy-start(f32[2]{0:T(128)} %alpha_ref.1) | copy-start | bytes 28
  38.0 49.5 %copy-start.2 = (f32[2]{0:T(128)S(1)}, f32[2]{0:T(128)}, u32[]{:S(2)}) copy-start(f32[2]{0:T(128)} %beta_ref.1) | copy-start | bytes 28
  46.9 1.6 %collective-permute-start.1 = (f32[512,128]{1,0:T(8,128)S(1)}, f32[512,128]{1,0:T(8,128)S(1)}, u32[]{:S(2)}, u32[]{:S(2)}) collective-permute-start(f32[512,128]{1,0:T(8,128)S(1)} %get-tuple-element.15), channel_id=1, source_target_pairs={{0,32},{32,0},{1,33},{33,1},{2,34},{34,2},{3,35},{35,3},{4,36},{36... | collective-permute-start | bytes 786440 | tf_op jit(solution)/shard_map/ppermute | solution.py:371
  81.7 37.5 %copy-start = (f32[4,128]{1,0:T(4,128)S(1)}, f32[4,128]{1,0:T(4,128)}, u32[]{:S(2)}) copy-start(f32[4,128]{1,0:T(4,128)} %right_ref.1) | copy-start | bytes 6148
  81.7 5.7 %collective-permute-start.2 = (f32[512,128]{1,0:T(8,128)S(1)}, f32[512,128]{1,0:T(8,128)S(1)}, u32[]{:S(2)}, u32[]{:S(2)}) collective-permute-start(f32[512,128]{1,0:T(8,128)S(1)} %bitcast.11), channel_id=1, source_target_pairs={{0,32},{32,0},{1,33},{33,1},{2,34},{34,2},{3,35},{35,3},{4,36},{36... | collective-permute-start | bytes 786440 | tf_op jit(solution)/shard_map/ppermute | solution.py:371
  96.8 1.6 %collective-permute-start.3 = (f32[512,128]{1,0:T(8,128)S(1)}, f32[512,128]{1,0:T(8,128)S(1)}, u32[]{:S(2)}, u32[]{:S(2)}) collective-permute-start(f32[512,128]{1,0:T(8,128)S(1)} %get-tuple-element.17), channel_id=1, source_target_pairs={{0,32},{32,0},{1,33},{33,1},{2,34},{34,2},{3,35},{35,3},{4,36},{36... | collective-permute-start | bytes 786440 | tf_op jit(solution)/shard_map/ppermute | solution.py:371
  99.2 20.0 %all-to-all-start.4 = ((f32[128,4,128]{2,1,0:T(4,128)}), f32[128,4,128]{2,1,0:T(4,128)S(1)}, u32[]{:S(2)}, u32[]{:S(2)}) async-start(f32[128,4,128]{2,1,0:T(4,128)} %bitcast.8), calls=%async_computation.4 | async-start | bytes 524288 | tf_op jit(solution)/shard_map/all_to_all | solution.py:375
